TPU v7x, 32 devices: a whole 2x2x4 slice. The times are simulated.
32 devices in a mesh: grp: 4 (over y, x), dev: 8 (over z, core).
Axes of the slice: x: 2, y: 2, z: 4, core: 2. Of those that a mesh axis runs over, the one named last changes fastest.
Arguments:
- node_latent: bfloat16 [4, 2048, 512], P('grp', 'dev'), may hold values from -6 to 6
- edge_latent: bfloat16 [4, 8, 8, 256, 512], P('grp', 'dev'), may hold values from -6 to 6
- node_cotangent: bfloat16 [4, 2048, 512], P('grp', 'dev'), may hold values from -6 to 6
- edge_cotangent: bfloat16 [4, 8, 8, 256, 512], P('grp', 'dev'), may hold values from -6 to 6
- edge_sender: int32 [8, 8, 256], P(None, 'dev'), may hold values from 0 to 255
- edge_receiver: int32 [8, 8, 256], P('dev'), may hold values from 0 to 255
- live_counts: int32 [8, 8], P('dev'), may hold values from 1 to 256, as said below
- edge_lift: bfloat16 [1536, 512], replicated, may hold values from -0.15625 to 0.15625
- edge_bias: float32 [512], replicated, may hold values from -3 to 3
- edge_mix: bfloat16 [512, 512], replicated, may hold values from -0.25 to 0.25
- edge_gain: float32 [512], replicated, may hold values from 0.5 to 2
- node_lift: bfloat16 [1024, 512], replicated, may hold values from -0.1875 to 0.1875
- node_bias: float32 [512], replicated, may hold values from -3 to 3
- node_mix: bfloat16 [512, 512], replicated, may hold values from -0.25 to 0.25
- node_gain: float32 [512], replicated, may hold values from 0.5 to 2
Outputs:
- grad_nodes: float32 [4, 2048, 512], P('grp', 'dev')
- grad_edges: bfloat16 [4, 8, 8, 256, 512], P('grp', 'dev')
- edge_lift_grad: float32 [1536, 512], replicated
- edge_bias_grad: float32 [512], replicated
- edge_mix_grad: float32 [512, 512], replicated
- edge_gain_grad: float32 [512], replicated
- node_lift_grad: float32 [1024, 512], replicated
- node_bias_grad: float32 [512], replicated
- node_mix_grad: float32 [512, 512], replicated
- node_gain_grad: float32 [512], replicated
Inputs may be any that keep to these rules, and one draw needn't show every extreme that they name: Slots k >= live_counts[r, s] of block (r, s) are padding. Owners are numbered along a closed curve over the sphere's partition: blocks with r == s or with r and s at most 2 apart around that loop of 8 owners hold most of a receiver's live edges, the other blocks only a few long-range edges; some block of every draw has all 256 slots live.
All inputs are finite; a program needn't handle non-finite values.
Results may differ from a plain program's by a relative error of at most 0.0075.
Values may be sent and summed in bfloat16 or wider, within the bound.
No kernel may reach another device: no remote copies, remote signals or barrier semaphores. Data moves between devices by JAX's collectives and lax.ppermute only.
A program may use at most 128 MiB of HBM per device.

v0:
```python
import jax
import jax.numpy as jnp
from jax import lax
from jax.sharding import PartitionSpec as P

EPSILON = 1e-05


def silu_grad(values):
    sigmoid = jax.nn.sigmoid(values)
    return sigmoid * (1.0 + values * (1.0 - sigmoid))


def norm_forward(values):
    centred = values - jnp.mean(values, axis=-1, keepdims=True)
    inverse = lax.rsqrt(jnp.mean(centred * centred, axis=-1, keepdims=True) + EPSILON)
    return (centred * inverse, inverse)


def norm_backward(grad_hat, normed, inverse):
    spread = jnp.mean(grad_hat * normed, axis=-1, keepdims=True)
    return inverse * (grad_hat - jnp.mean(grad_hat, axis=-1, keepdims=True) - normed * spread)


def matmul(left, right):
    return jnp.dot(left, right, preferred_element_type=jnp.float32)


def contract_rows(left, right):
    return lax.dot_general(
        left, right, (((0,), (0,)), ((), ())), preferred_element_type=jnp.float32
    )


def contract_features(left, right):
    return lax.dot_general(
        left, right, (((1,), (1,)), ((), ())), preferred_element_type=jnp.float32
    )


def per_device(
    node_latent,
    edge_latent,
    node_cotangent,
    edge_cotangent,
    edge_sender,
    edge_receiver,
    live_counts,
    edge_lift,
    edge_bias,
    edge_mix,
    edge_gain,
    node_lift,
    node_bias,
    node_mix,
    node_gain,
):
    width = node_latent.shape[2]
    nodes = node_latent[0]
    local_nodes = nodes.shape[0]
    peers = edge_receiver.shape[1]
    slots = edge_receiver.shape[2]
    total_rows = peers * slots
    edges = edge_latent.reshape(total_rows, width)
    edge_seed = edge_cotangent.reshape(total_rows, width).astype(jnp.float32)
    receiver_index = edge_receiver.reshape(total_rows)
    sender_index = edge_sender.reshape(total_rows)
    live = (
        lax.broadcasted_iota(jnp.int32, (peers, slots), 1) < live_counts.reshape(peers, 1)
    ).reshape(total_rows, 1)
    receiver_table = (
        lax.broadcasted_iota(jnp.int32, (local_nodes, total_rows), 0) == receiver_index[None, :]
    ).astype(jnp.bfloat16)
    sender_table = (
        lax.broadcasted_iota(jnp.int32, (local_nodes, total_rows), 0) == sender_index[None, :]
    ).astype(jnp.bfloat16)
    lift_edge_part = edge_lift[:width]
    lift_sender_part = edge_lift[width : 2 * width]
    lift_receiver_part = edge_lift[2 * width :]
    outgoing = jnp.take(nodes, sender_index, axis=0).reshape(peers, slots, width)
    block = lax.all_to_all(outgoing, "dev", split_axis=0, concat_axis=0, tiled=True)
    fetched = block
    sender_term = jnp.einsum(
        "pkc,cd->pkd", block, lift_sender_part, preferred_element_type=jnp.float32
    )
    fetched = fetched.reshape(total_rows, width)
    receiver_rows = jnp.take(nodes, receiver_index, axis=0)
    pre_edge = (
        matmul(edges, lift_edge_part)
        + sender_term.reshape(total_rows, width)
        + matmul(receiver_rows, lift_receiver_part)
        + edge_bias
    )
    hidden_edge = jax.nn.silu(pre_edge).astype(jnp.bfloat16)
    normed_edge, inverse_edge = norm_forward(matmul(hidden_edge, edge_mix))
    message = jnp.where(live, normed_edge * edge_gain, 0.0).astype(jnp.bfloat16)
    summed = matmul(receiver_table, message).astype(jnp.bfloat16)
    joined = jnp.concatenate([nodes, summed], axis=1)
    pre_node = matmul(joined, node_lift) + node_bias
    hidden_node = jax.nn.silu(pre_node).astype(jnp.bfloat16)
    normed_node, inverse_node = norm_forward(matmul(hidden_node, node_mix))
    grad_update = node_cotangent[0].astype(jnp.float32)
    node_gain_grad = jnp.sum(grad_update * normed_node, axis=0)
    grad_out_node = norm_backward(grad_update * node_gain, normed_node, inverse_node).astype(
        jnp.bfloat16
    )
    node_mix_grad = contract_rows(hidden_node, grad_out_node)
    grad_pre_node = (contract_features(grad_out_node, node_mix) * silu_grad(pre_node)).astype(
        jnp.bfloat16
    )
    node_bias_grad = jnp.sum(grad_pre_node.astype(jnp.float32), axis=0)
    node_lift_grad = contract_rows(joined, grad_pre_node)
    grad_joined = contract_features(grad_pre_node, node_lift)
    grad_message = jnp.where(
        live, edge_seed + jnp.take(grad_joined[:, width:], receiver_index, axis=0), 0.0
    )
    edge_gain_grad = jnp.sum(grad_message * normed_edge, axis=0)
    grad_out_edge = norm_backward(grad_message * edge_gain, normed_edge, inverse_edge).astype(
        jnp.bfloat16
    )
    edge_mix_grad = contract_rows(hidden_edge, grad_out_edge)
    grad_pre_edge = (contract_features(grad_out_edge, edge_mix) * silu_grad(pre_edge)).astype(
        jnp.bfloat16
    )
    edge_bias_grad = jnp.sum(grad_pre_edge.astype(jnp.float32), axis=0)
    edge_lift_grad = jnp.concatenate(
        [
            contract_rows(edges, grad_pre_edge),
            contract_rows(fetched, grad_pre_edge),
            contract_rows(receiver_rows, grad_pre_edge),
        ],
        axis=0,
    )
    grad_stacked = contract_features(grad_pre_edge, edge_lift).astype(jnp.bfloat16)
    grad_edge_part = grad_stacked[:, :width]
    grad_receiver_part = grad_stacked[:, 2 * width :]
    arriving = lax.all_to_all(
        grad_stacked[:, width : 2 * width].reshape(peers, slots, width),
        "dev",
        split_axis=0,
        concat_axis=0,
        tiled=True,
    )
    grad_edges = jnp.where(live, edge_seed + grad_edge_part.astype(jnp.float32), 0.0).astype(
        jnp.bfloat16
    )
    grad_nodes = (
        grad_update
        + grad_joined[:, :width]
        + matmul(receiver_table, grad_receiver_part)
        + matmul(sender_table, arriving.reshape(total_rows, width))
    )
    summed_grads = lax.psum(
        (
            edge_lift_grad,
            edge_bias_grad,
            edge_mix_grad,
            edge_gain_grad,
            node_lift_grad,
            node_bias_grad,
            node_mix_grad,
            node_gain_grad,
        ),
        ("grp", "dev"),
    )
    groups = lax.axis_size("grp") * lax.axis_size("dev")
    edge_scale = float(total_rows * groups) ** (-0.5)
    node_scale = float(local_nodes * groups) ** (-0.5)
    return (
        grad_nodes[None],
        grad_edges.reshape(1, 1, peers, slots, width),
        summed_grads[0] * edge_scale,
        summed_grads[1] * edge_scale,
        summed_grads[2] * edge_scale,
        summed_grads[3] * edge_scale,
        summed_grads[4] * node_scale,
        summed_grads[5] * node_scale,
        summed_grads[6] * node_scale,
        summed_grads[7] * node_scale,
    )


def solution(mesh):
    return jax.shard_map(
        per_device,
        mesh=mesh,
        in_specs=(
            P("grp", "dev", None),
            P("grp", "dev", None, None, None),
            P("grp", "dev", None),
            P("grp", "dev", None, None, None),
            P(None, "dev", None),
            P("dev", None, None),
            P("dev", None),
            P(),
            P(),
            P(),
            P(),
            P(),
            P(),
            P(),
            P(),
        ),
        out_specs=(
            P("grp", "dev", None),
            P("grp", "dev", None, None, None),
            P(),
            P(),
            P(),
            P(),
            P(),
            P(),
            P(),
            P(),
        ),
        check_vma=False,
    )
```

profile of v0, /device:TPU:0, one launch (start us, length us, event | category | flops | bytes accessed | tf_op | source)
XLA Modules:
  0.0 370.4 jit_solution(497550154513148223)
XLA Ops:
  8.7 10.2 %gather_fusion.1 = bf16[2048,512]{1,0:T(8,128)(2,1)} fusion(bf16[256,512]{1,0:T(8,128)(2,1)} %bitcast.76, s32[2048]{0:T(1024)S(1)} %fusion.33), kind=kCustom, calls=%fused_computation.clone | custom fusion | bytes 4202496 | tf_op jit(solution)/shard_map/jit(_take)/gather | solution.py:80
  19.0 2.7 broadcast_select_fusion.1
  21.7 6.5 %all-to-all-start = ((bf16[8,256,512]{2,1,0:T(8,128)(2,1)}), bf16[8,256,512]{2,1,0:T(8,128)(2,1)}, u32[]{:S(2)}, u32[]{:S(2)}) async-start(bf16[8,256,512]{2,1,0:T(8,128)(2,1)} %bitcast.83), calls=%async_computation | async-start | bytes 4194304 | tf_op jit(solution)/shard_map/all_to_all | solution.py:81
  28.3 9.2 %gather_fusion.2 = bf16[2048,512]{1,0:T(8,128)(2,1)} fusion(bf16[256,512]{1,0:T(8,128)(2,1)S(1)} %bitcast.77, s32[2048]{0:T(1024)S(1)} %fusion.34), kind=kCustom, calls=%fused_computation.1.clone | custom fusion | bytes 4202496 | tf_op jit(solution)/shard_map/jit(_take)/gather | solution.py:87
  37.5 4.2 %copy.41 = f32[2048,512]{0,1:T(8,128)} copy(bf16[2048,512]{1,0:T(8,128)(2,1)} %bitcast.81) | data formatting | bytes 6291456 | tf_op jit(solution)/shard_map/convert_element_type | solution.py:65
  41.9 4.2 %fusion.30 = f32[2048,512]{1,0:T(8,128)} fusion(bf16[2048,512]{1,0:T(8,128)(2,1)S(1)} %bitcast.74, bf16[1536,512]{1,0:T(8,128)(2,1)} %param.24), kind=kOutput, calls=%fused_computation.67 | convolution fusion | flops 1073741824 | bytes 6815744 | tf_op jit(solution)/shard_map/dot_general | solution.py:26
  46.1 31.2 %all-to-all-done = bf16[8,256,512]{2,1,0:T(8,128)(2,1)} async-done(((bf16[8,256,512]{2,1,0:T(8,128)(2,1)}), bf16[8,256,512]{2,1,0:T(8,128)(2,1)}, u32[]{:S(2)}, u32[]{:S(2)}) %all-to-all-start) | async-done | bytes 2097184 | tf_op jit(solution)/shard_map/all_to_all | solution.py:81
  77.4 3.1 fusion.26
  81.0 5.3 %multiply_convert_fusion.2 = (bf16[2048,512]{1,0:T(8,128)(2,1)S(1)}, f32[2048,512]{1,0:T(8,128)}) fusion(f32[512]{0:T(512)S(1)} %copy-done.32, bf16[1536,512]{1,0:T(8,128)(2,1)} %param.24, bf16[2048,512]{1,0:T(8,128)(2,1)S(1)} %copy-done.13, pred[2048]{0:T(1024)(128)(4,1)S(1)} %compare_and_fusion, f32[2048,512]{1,0:T(8,128)S(1)} %copy-done.6, ...), kind=kOutput, calls=%fused_computation.17 | convolution fusion | flops 1083179008 | bytes 17305600 | tf_op jit(solution)/shard_map/dot_general | solution.py:26
  94.6 8.9 %gather_fusion = f32[2048,512]{1,0:T(8,128)} fusion(f32[256,512]{1,0:T(8,128)S(1)} %slice.39, s32[2048]{0:T(1024)S(1)} %broadcast_clamp_fusion), kind=kCustom, calls=%fused_computation.2 | custom fusion | bytes 8396800 | tf_op jit(solution)/shard_map/jit(_take)/gather | solution.py:115
  103.5 5.4 %copy.35 = f32[2048,512]{0,1:T(8,128)} copy(f32[2048,512]{1,0:T(8,128)} %gather_fusion) | data formatting | bytes 8388608 | tf_op jit(solution)/shard_map/jit(_take)/gather | solution.py:115
  108.9 5.9 %multiply_reduce_fusion = (f32[512]{0:T(512)S(1)}, f32[2048]{0:T(1024)S(1)}, f32[2048,512]{0,1:T(8,128)S(1)}) fusion(f32[2048,512]{0,1:T(8,128)} %copy-done.2, f32[2048]{0:T(1024)S(1)} %add_rsqrt_fusion, f32[2048]{0:T(1024)S(1)} %broadcast_multiply_fusion.5, f32[512]{0:T(512)S(1)} %copy-done.28, f32[2048,512]{0,1:T(8,128)} %copy.41, f32[2048,512]{0,1:T(8,128)} %copy.35, ...), kind=kLoop, calls=%fused_computation.7 | loop fusion | flops 10483200 | bytes 16809984 | tf_op jit(solution)/shard_map/reduce_sum | solution.py:117
  120.0 2.8 convert_reduce_fusion
  131.5 2.9 fusion.47
  136.3 5.5 %convolution_convert_fusion = bf16[2048,1536]{0,1:T(8,128)(2,1)S(1)} fusion(bf16[2048,512]{1,0:T(8,128)(2,1)} %copy-done.36, bf16[1536,512]{1,0:T(8,128)(2,1)} %param.24), kind=kOutput, calls=%fused_computation.3 | convolution fusion | flops 3224371200 | bytes 9961472 | tf_op jit(solution)/shard_map/dot_general | solution.py:36
  145.2 4.4 %all-to-all-start.1 = ((bf16[8,256,512]{1,2,0:T(8,128)(2,1)}), bf16[8,256,512]{1,2,0:T(8,128)(2,1)}, u32[]{:S(2)}, u32[]{:S(2)}) async-start(bf16[8,256,512]{1,2,0:T(8,128)(2,1)} %bitcast.82), calls=%async_computation.1 | async-start | bytes 4194304 | tf_op jit(solution)/shard_map/all_to_all | solution.py:137
  149.6 5.0 %select_convert_fusion = bf16[2048,512]{0,1:T(8,128)(2,1)} fusion(f32[2048,512]{0,1:T(8,128)} %copy.41, bf16[2048,1536]{0,1:T(8,128)(2,1)} %copy-done.10, pred[2048]{0:T(1024)(128)(4,1)S(1)} %lt.53), kind=kLoop, calls=%fused_computation.9 | loop fusion | flops 4194304 | bytes 8390656 | tf_op jit(solution)/shard_map/convert_element_type | solution.py:144
  154.6 4.0 %copy.42 = bf16[2048,512]{1,0:T(8,128)(2,1)} copy(bf16[2048,512]{0,1:T(8,128)(2,1)} %select_convert_fusion) | data formatting | bytes 4194304
  158.6 84.2 %all-reduce = (f32[512]{0:T(512)S(1)}, f32[512]{0:T(512)S(1)}, f32[512]{0:T(512)S(1)}, f32[512]{0:T(512)S(1)}) all-reduce(f32[512]{0:T(512)S(1)} %get-tuple-element.61, f32[512]{0:T(512)S(1)} %get-tuple-element.41, f32[512]{0:T(512)S(1)} %get-tuple-element.63, ...), channel_id=1, replica_groups=mesh['grp'=4,'dev'=8] {'grp','dev'}, use_global_device_ids=true, to_apply=%region_10.12 | all-reduce | flops 2048 | bytes 16384 | tf_op jit(solution)/shard_map/psum | solution.py:153
  245.2 3.1 fusion.9
  248.3 99.6 %all-reduce.4.cloned.1.call-done = (f32[1536,512]{1,0:T(8,128)}, f32[512,512]{1,0:T(8,128)}, f32[1024,512]{1,0:T(8,128)}, f32[512,512]{1,0:T(8,128)}) async-done(((f32[1536,512]{1,0:T(8,128)}, f32[512,512]{1,0:T(8,128)}, f32[1024,512]{1,0:T(8,128)}, f32[512,512]{1,0:T(8,128)}), (f32[1536,512]{1,0:T(8,128)}, f32[512,512]{1,0:T(8,128)}, f32[1024,512]{1,0:T(8,128)}, ...) | async-done | bytes 7340048 | tf_op jit(solution)/shard_map/psum | solution.py:153
  350.4 2.5 broadcast_multiply_fusion.2
  356.5 4.0 %copy.38 = bf16[8,256,512]{2,1,0:T(8,128)(2,1)} copy(bf16[8,256,512]{1,2,0:T(8,128)(2,1)} %all-to-all-done.1) | data formatting | bytes 4194304 | tf_op jit(solution)/shard_map/all_to_all | solution.py:137
  360.5 3.1 fusion.8
  (127 shorter events, 37.8 us)
Async XLA Ops:
  7.2 34.7 %copy-start = (bf16[1,1,8,256,512]{4,3,2,1,0:T(8,128)(2,1)S(1)}, bf16[1,1,8,256,512]{4,3,2,1,0:T(8,128)(2,1)}, u32[]{:S(2)}) copy-start(bf16[1,1,8,256,512]{4,3,2,1,0:T(8,128)(2,1)} %param.18) | copy-start | bytes 6291460
  21.7 6.5 %copy-start.26 = (s32[1,8,256]{2,1,0:T(8,128)S(1)}, s32[1,8,256]{2,1,0:T(8,128)}, u32[]{:S(2)}) copy-start(s32[1,8,256]{2,1,0:T(8,128)} %param.22) | copy-start | bytes 24580
  21.7 6.5 %copy-start.1 = (bf16[1,256,512]{2,1,0:T(8,128)(2,1)S(1)}, bf16[1,256,512]{2,1,0:T(8,128)(2,1)}, u32[]{:S(2)}) copy-start(bf16[1,256,512]{2,1,0:T(8,128)(2,1)} %param.17) | copy-start | bytes 786436
  21.7 55.6 %all-to-all-start = ((bf16[8,256,512]{2,1,0:T(8,128)(2,1)}), bf16[8,256,512]{2,1,0:T(8,128)(2,1)}, u32[]{:S(2)}, u32[]{:S(2)}) async-start(bf16[8,256,512]{2,1,0:T(8,128)(2,1)} %bitcast.83), calls=%async_computation | async-start | bytes 4194304 | tf_op jit(solution)/shard_map/all_to_all | solution.py:81
  28.2 319.7 %all-reduce.4.cloned.1.call-start = ((), (), s32[]{:S(2)}) async-start(), calls=%async_computation.2 | async-start | bytes 14680064 | tf_op jit(solution)/shard_map/psum | solution.py:153
  37.5 4.2 %copy-start.30 = (s32[1,8]{1,0:T(1,128)S(1)}, s32[1,8]{1,0:T(1,128)}, u32[]{:S(2)}) copy-start(s32[1,8]{1,0:T(1,128)} %param.23) | copy-start | bytes 100
  46.1 34.3 %copy-start.32 = (f32[512]{0:T(512)S(1)}, f32[512]{0:T(512)}, u32[]{:S(2)}) copy-start(f32[512]{0:T(512)} %param.25) | copy-start | bytes 6148
  77.4 3.1 copy-start.6
  77.4 3.7 copy-start.13
  81.0 5.3 %copy-start.19 = (bf16[512,512]{1,0:T(8,128)(2,1)S(1)}, bf16[512,512]{1,0:T(8,128)(2,1)}, u32[]{:S(2)}) copy-start(bf16[512,512]{1,0:T(8,128)(2,1)} %param.26) | copy-start | bytes 1572868
  108.9 5.9 %copy-start.4 = (f32[2048,512]{1,0:T(8,128)S(1)}, f32[2048,512]{1,0:T(8,128)}, u32[]{:S(2)}) copy-start(f32[2048,512]{1,0:T(8,128)} %gather_fusion) | copy-start | bytes 12582916
  108.9 6.5 %copy-start.5 = (bf16[1,1,8,256,512]{4,3,2,1,0:T(8,128)(2,1)S(1)}, bf16[1,1,8,256,512]{4,3,2,1,0:T(8,128)(2,1)}, u32[]{:S(2)}) copy-start(bf16[1,1,8,256,512]{4,3,2,1,0:T(8,128)(2,1)} %param.20) | copy-start | bytes 6291460
  120.0 2.8 copy-start.14
  122.8 8.7 %copy-start.36 = (bf16[2048,512]{1,0:T(8,128)(2,1)}, bf16[2048,512]{1,0:T(8,128)(2,1)S(1)}, u32[]{:S(2)}) copy-start(bf16[2048,512]{1,0:T(8,128)(2,1)S(1)} %get-tuple-element.62) | copy-start | bytes 6291460
  125.8 4.1 %copy-start.22 = (bf16[1,256,512]{2,1,0:T(8,128)(2,1)S(1)}, bf16[1,256,512]{2,1,0:T(8,128)(2,1)}, u32[]{:S(2)}) copy-start(bf16[1,256,512]{2,1,0:T(8,128)(2,1)} %param.19) | copy-start | bytes 786436
  125.8 4.1 %copy-start.35 = (f32[256,512]{1,0:T(8,128)S(1)}, f32[256,512]{1,0:T(8,128)}, u32[]{:S(2)}) copy-start(f32[256,512]{1,0:T(8,128)} %copy-done.34) | copy-start | bytes 1572868
  141.8 3.4 copy-start.10
  145.2 211.2 %all-to-all-start.1 = ((bf16[8,256,512]{1,2,0:T(8,128)(2,1)}), bf16[8,256,512]{1,2,0:T(8,128)(2,1)}, u32[]{:S(2)}, u32[]{:S(2)}) async-start(bf16[8,256,512]{1,2,0:T(8,128)(2,1)} %bitcast.82), calls=%async_computation.1 | async-start | bytes 4194304 | tf_op jit(solution)/shard_map/all_to_all | solution.py:137
  154.6 90.6 %copy-start.12 = (f32[256,1024]{1,0:T(8,128)S(1)}, f32[256,1024]{1,0:T(8,128)}, u32[]{:S(2)}) copy-start(f32[256,1024]{1,0:T(8,128)} %copy-done.11) | copy-start | bytes 3145732
  154.6 90.6 %copy-start.23 = (bf16[1,256,512]{2,1,0:T(8,128)(2,1)S(1)}, bf16[1,256,512]{2,1,0:T(8,128)(2,1)}, u32[]{:S(2)}) copy-start(bf16[1,256,512]{2,1,0:T(8,128)(2,1)} %param.19) | copy-start | bytes 786436
  347.9 4.9 %copy-start.15 = (f32[1024,512]{1,0:T(8,128)S(1)}, f32[1024,512]{1,0:T(8,128)}, u32[]{:S(2)}) copy-start(f32[1024,512]{1,0:T(8,128)} %get-tuple-element.52) | copy-start | bytes 6291460
  350.4 4.0 %copy-start.9 = (f32[1536,512]{1,0:T(8,128)S(1)}, f32[1536,512]{1,0:T(8,128)}, u32[]{:S(2)}) copy-start(f32[1536,512]{1,0:T(8,128)} %get-tuple-element.50) | copy-start | bytes 9437188
  356.5 4.0 %copy-start.27 = (s32[8,1,256]{2,1,0:T(1,128)S(1)}, s32[8,1,256]{2,1,0:T(1,128)}, u32[]{:S(2)}) copy-start(s32[8,1,256]{2,1,0:T(1,128)} %param.21) | copy-start | bytes 24580
  356.5 4.0 %copy-start.37 = (f32[256,512]{1,0:T(8,128)S(1)}, f32[256,512]{1,0:T(8,128)}, u32[]{:S(2)}) copy-start(f32[256,512]{1,0:T(8,128)} %fusion.9) | copy-start | bytes 1572868
  (18 other events, 29.5 us)
Sparse Core Ops, SparseCore 0:
  136.4 211.4 all-reduce.3
where the time goes:
time: 371 us; the launch traced here: 370 us
  waiting for transfers between devices  131 us (35%)
  blocking collectives  84.2 us (23%)
  local copies, waits for them, and re-layouts  55.5 us (15%)
  matrix products  42.5 us (11%)
  other arithmetic  31.9 us (9%)
  between operations  14.5 us (4%)
  starting transfers between devices  10.9 us (3%)
    psum x1, waiting for transfers between devices, per_device(): lax.psum((edge_lift_grad, edge_bias_grad, edge_mix_grad, edge_gain_grad,...  99.6 us
    psum x1, blocking collectives, per_device(): lax.psum((edge_lift_grad, edge_bias_grad, edge_mix_grad, edge_gain_grad,...  84.2 us
    all_to_all x1, waiting for transfers between devices, per_device(): lax.all_to_all(outgoing, 'dev', split_axis=0, concat_axis=0, tiled=True)  31.2 us
    dot_general x8, matrix products, matmul(): return jnp.dot(left, right, preferred_element_type=jnp.float32)  19 us
    gather x2, local copies, waits for them, and re-layouts, per_device(): jnp.take(grad_joined[:, width:], receiver_index, axis=0)  14.4 us
    unnamed x82, local copies, waits for them, and re-layouts  11.6 us
    dot_general x6, matrix products, contract_rows(): lax.dot_general(left, right, (((0,), (0,)), ((), ())), preferred_element_...  11.2 us
    gather x1, local copies, waits for them, and re-layouts, per_device(): jnp.take(nodes, sender_index, axis=0).reshape(peers, slots, width)  10.2 us
  transfers between devices with their start and end apart: 3, of which 2 were waited for; matrix products, arithmetic and copies ran while one was open for 13% of the time, Pallas kernels for 0%

commit v1 on v0

v1 whole, which is shorter than its diff:
```python
import jax
import jax.numpy as jnp
from jax import lax
from jax.experimental import pallas as pl
from jax.experimental.pallas import tpu as pltpu
from jax.sharding import PartitionSpec as P

EPSILON = 1e-05
CHUNKS = 32
BF16 = jnp.bfloat16
F32 = jnp.float32


def matmul(left, right):
    return jnp.dot(left, right, preferred_element_type=F32)


def contract_rows(left, right):
    return lax.dot_general(left, right, (((0,), (0,)), ((), ())), preferred_element_type=F32)


def contract_features(left, right):
    return lax.dot_general(left, right, (((1,), (1,)), ((), ())), preferred_element_type=F32)


def one_hot(index_row, nodes):
    rows = lax.broadcasted_iota(jnp.int32, (nodes, index_row.shape[1]), 0)
    return jnp.where(rows == index_row, 1.0, 0.0).astype(BF16)


def silu_pair(values):
    gate = 0.5 * jnp.tanh(0.5 * values) + 0.5
    hidden = values * gate
    return hidden, gate + hidden * (1.0 - gate)


def norm_forward(values):
    centred = values - jnp.mean(values, axis=-1, keepdims=True)
    inverse = lax.rsqrt(jnp.mean(centred * centred, axis=-1, keepdims=True) + EPSILON)
    return centred * inverse, inverse


def norm_backward(grad_hat, normed, inverse):
    spread = jnp.mean(grad_hat * normed, axis=-1, keepdims=True)
    return inverse * (grad_hat - jnp.mean(grad_hat, axis=-1, keepdims=True) - normed * spread)


def live_rows(count, shape):
    return lax.broadcasted_iota(jnp.int32, shape, 0) < count


def store_chunks(order_ref, source_ref, target_ref):
    rows = source_ref.shape[0] // CHUNKS

    def step(place, carry):
        start = pl.multiple_of(order_ref[place] * rows, rows)
        target = pl.multiple_of(place * rows, rows)
        target_ref[pl.ds(target, rows), :] = source_ref[pl.ds(start, rows), :].astype(BF16)
        return carry

    lax.fori_loop(0, CHUNKS, step, 0)


def lift_kernel(edges_ref, receiver_ref, nodes_ref, lift_ref, bias_ref, pre_ref):
    width = nodes_ref.shape[1]
    table = one_hot(receiver_ref[0], nodes_ref.shape[0])
    receivers = contract_rows(table, nodes_ref[...]).astype(BF16)
    pre_ref[0] = (
        matmul(edges_ref[0], lift_ref[:width])
        + matmul(receivers, lift_ref[2 * width :])
        + bias_ref[...]
    )


def forward_kernel(
    owner_ref,
    live_ref,
    order_ref,
    pre_ref,
    gathered_ref,
    sender_ref,
    receiver_ref,
    nodes_ref,
    seed_ref,
    lift_ref,
    mix_ref,
    gain_ref,
    node_lift_ref,
    node_bias_ref,
    node_mix_ref,
    node_gain_ref,
    hidden_ref,
    normed_ref,
    slope_ref,
    inverse_ref,
    base_ref,
    summed_grad_ref,
    packed_ref,
    small_ref,
    summed_ref,
    total_ref,
):
    step = pl.program_id(0)
    nodes_count, width = nodes_ref.shape
    owner = owner_ref[step]
    senders = contract_rows(
        one_hot(sender_ref[0], nodes_count), gathered_ref[0, :nodes_count]
    ).astype(BF16)
    pre = pre_ref[0] + matmul(senders, lift_ref[...])
    hidden, slope = silu_pair(pre)
    hidden = hidden.astype(BF16)
    normed, inverse = norm_forward(matmul(hidden, mix_ref[...]))
    hidden_ref[0] = hidden
    slope_ref[0] = slope.astype(BF16)
    normed_ref[0] = normed.astype(BF16)
    inverse_ref[0] = inverse
    live = live_rows(live_ref[owner], normed.shape)
    message = jnp.where(live, normed * gain_ref[...], 0.0).astype(BF16)

    @pl.when(step == 0)
    def _():
        summed_ref[...] = jnp.zeros_like(summed_ref)

    summed_ref[...] += matmul(one_hot(receiver_ref[0], nodes_count), message)

    @pl.when(step == pl.num_programs(0) - 1)
    def _():
        nodes = nodes_ref[...]
        summed = summed_ref[...].astype(BF16)
        pre_node = (
            matmul(nodes, node_lift_ref[:width])
            + matmul(summed, node_lift_ref[width:])
            + node_bias_ref[...]
        )
        hidden_node, slope_node = silu_pair(pre_node)
        hidden_node = hidden_node.astype(BF16)
        normed_node, inverse_node = norm_forward(matmul(hidden_node, node_mix_ref[...]))
        seed = seed_ref[...].astype(F32)
        small_ref[1:2, :] = jnp.sum(seed * normed_node, axis=0, keepdims=True)
        grad_out = norm_backward(seed * node_gain_ref[...], normed_node, inverse_node).astype(BF16)
        total_ref[2 * width :, :] = contract_rows(hidden_node, grad_out)
        grad_pre = (contract_features(grad_out, node_mix_ref[...]) * slope_node).astype(BF16)
        small_ref[0:1, :] = jnp.sum(grad_pre.astype(F32), axis=0, keepdims=True)
        total_ref[:width, :] = contract_rows(nodes, grad_pre)
        total_ref[width : 2 * width, :] = contract_rows(summed, grad_pre)
        base_ref[...] = seed + contract_features(grad_pre, node_lift_ref[:width])
        summed_grad_ref[...] = contract_features(grad_pre, node_lift_ref[width:]).astype(BF16)
        store_chunks(order_ref, total_ref, packed_ref)


def backward_kernel(
    owner_ref,
    live_ref,
    order_ref,
    edges_ref,
    seed_ref,
    gathered_ref,
    sender_ref,
    receiver_ref,
    hidden_ref,
    normed_ref,
    slope_ref,
    inverse_ref,
    nodes_ref,
    base_ref,
    summed_grad_ref,
    lift_ref,
    mix_ref,
    gain_ref,
    grad_edges_ref,
    partial_ref,
    grad_nodes_ref,
    packed_ref,
    small_ref,
    received_ref,
    total_ref,
):
    step = pl.program_id(0)
    nodes_count, width = nodes_ref.shape
    live_count = live_ref[owner_ref[step]]

    @pl.when(step == 0)
    def _():
        received_ref[...] = jnp.zeros_like(received_ref)
        total_ref[...] = jnp.zeros_like(total_ref)
        small_ref[...] = jnp.zeros_like(small_ref)

    seed = seed_ref[0].astype(F32)
    live = live_rows(live_count, seed.shape)
    receiver_table = one_hot(receiver_ref[0], nodes_count)
    grad_message = jnp.where(
        live, seed + contract_rows(receiver_table, summed_grad_ref[...]), 0.0
    )
    normed = normed_ref[0].astype(F32)
    small_ref[1:2, :] += jnp.sum(grad_message * normed, axis=0, keepdims=True)
    grad_out = norm_backward(grad_message * gain_ref[...], normed, inverse_ref[0]).astype(BF16)
    total_ref[3 * width :, :] += contract_rows(hidden_ref[0], grad_out)
    grad_pre = (contract_features(grad_out, mix_ref[...]) * slope_ref[0].astype(F32)).astype(BF16)
    small_ref[0:1, :] += jnp.sum(grad_pre.astype(F32), axis=0, keepdims=True)
    total_ref[:width, :] += contract_rows(edges_ref[0], grad_pre)
    sent = matmul(one_hot(sender_ref[0], nodes_count), grad_pre).astype(BF16)
    partial_ref[0, 0] = sent
    total_ref[width : 2 * width, :] += contract_rows(gathered_ref[0, :nodes_count], sent)
    received_ref[...] += matmul(receiver_table, grad_pre)
    grad_edges_ref[0] = jnp.where(
        live, seed + contract_features(grad_pre, lift_ref[:width]), 0.0
    ).astype(BF16)

    @pl.when(step == pl.num_programs(0) - 1)
    def _():
        received = received_ref[...].astype(BF16)
        total_ref[2 * width : 3 * width, :] = contract_rows(nodes_ref[...], received)
        grad_nodes_ref[...] = base_ref[...] + contract_features(received, lift_ref[2 * width :])
        store_chunks(order_ref, total_ref, packed_ref)


def unpack_kernel(
    scale, order_ref, node_ref, edge_ref, edge_lift_ref, edge_mix_ref, node_lift_ref, node_mix_ref,
    edge_total, node_total,
):
    edge_scale, node_scale = scale
    for source, total, factor in (
        (edge_ref, edge_total, edge_scale),
        (node_ref, node_total, node_scale),
    ):
        rows = source.shape[0] // CHUNKS

        def step(place, carry, source=source, total=total, factor=factor, rows=rows):
            target = pl.multiple_of(order_ref[place] * rows, rows)
            start = pl.multiple_of(place * rows, rows)
            total[pl.ds(target, rows), :] = source[pl.ds(start, rows), :].astype(F32) * factor
            return carry

        lax.fori_loop(0, CHUNKS, step, 0)
    width = edge_lift_ref.shape[1]
    edge_lift_ref[...] = edge_total[: 3 * width]
    edge_mix_ref[...] = edge_total[3 * width :]
    node_lift_ref[...] = node_total[: 2 * width]
    node_mix_ref[...] = node_total[2 * width :]


def swap(values, axis, bit):
    size = lax.axis_size(axis)
    return lax.ppermute(values, axis, [(i, i ^ bit) for i in range(size)])


def add_rounded(left, right):
    return (left.astype(F32) + right.astype(F32)).astype(BF16)


def gather_nodes(nodes):
    pieces = []
    for piece in [nodes] + [swap(nodes, "dev", 2 * k) for k in range(1, 4)]:
        pieces += [piece, swap(piece, "dev", 1)]
    return jnp.stack(pieces)


def reduce_senders(partial):
    kept = add_rounded(partial[0], swap(partial[1], "dev", 1))
    kept = add_rounded(kept[::2], swap(kept[1::2], "dev", 2))
    return kept[0].astype(F32) + swap(kept[1], "dev", 4).astype(F32)


def reduce_plane(packed):
    half = packed.shape[0] // 2
    kept = add_rounded(packed[:half], swap(packed[half:], "dev", 1))
    parts = []
    for side, bits in enumerate(((1, 2), (2, 1))):
        part = kept[side * half // 2 : (side + 1) * half // 2]
        for bit in bits:
            rows = part.shape[0] // 2
            part = add_rounded(part[:rows], swap(part[rows:], "grp", bit))
        parts.append(part)
    return parts


def reduce_line(parts):
    kept_rows = jnp.concatenate([part[: part.shape[0] // 2] for part in parts])
    sent_rows = jnp.concatenate([part[part.shape[0] // 2 :] for part in parts])
    kept = add_rounded(kept_rows, swap(sent_rows, "dev", 2))
    kept = add_rounded(kept, swap(kept, "dev", 4))
    other = swap(kept, "dev", 2)
    results, start = [], 0
    for part in parts:
        rows = part.shape[0] // 2
        results.append(jnp.concatenate([kept[start : start + rows], other[start : start + rows]]))
        start += rows
    return results


def spread_plane(sides):
    for bits in ((2, 1), (1, 2)):
        sides = [
            jnp.concatenate([part, swap(part, "grp", bit)]) for part, bit in zip(sides, bits)
        ]
    return sides


def split_rows(part, sizes):
    pieces, start = [], 0
    for size in sizes:
        pieces.append(part[start : start + size])
        start += size
    return pieces


def chunk_order():
    group = lax.axis_index("grp")
    device = lax.axis_index("dev")
    x, y = group & 1, group >> 1
    core, z = device & 1, (device >> 1) & 1
    place = jnp.arange(CHUNKS, dtype=jnp.int32)
    first = core * 16 + x * 4 + y * 2 + z
    second = core * 16 + y * 4 + x * 2 + z
    return place ^ jnp.where((place & 8) == 0, first, second)


def small_sum(values):
    for axis, bit in (("dev", 1), ("grp", 1), ("grp", 2), ("dev", 2), ("dev", 4)):
        values = values + swap(values, axis, bit)
    return values


def shape(*dims, kind=F32):
    return jax.ShapeDtypeStruct(dims, kind)


def params(mebibytes):
    return pltpu.CompilerParams(vmem_limit_bytes=mebibytes << 20)


def whole(*dims):
    return pl.BlockSpec(dims, lambda *_: (0,) * len(dims))


def per_device(
    node_latent,
    edge_latent,
    node_cotangent,
    edge_cotangent,
    edge_sender,
    edge_receiver,
    live_counts,
    edge_lift,
    edge_bias,
    edge_mix,
    edge_gain,
    node_lift,
    node_bias,
    node_mix,
    node_gain,
):
    width = node_latent.shape[2]
    nodes = node_latent[0]
    count = nodes.shape[0]
    peers = edge_receiver.shape[1]
    slots = edge_receiver.shape[2]
    total_rows = peers * slots
    unit = total_rows * width * width
    edges = edge_latent.reshape(peers, slots, width)
    edge_seed = edge_cotangent.reshape(peers, slots, width)
    receivers = edge_receiver.reshape(peers, 1, slots)
    live = live_counts.reshape(peers)
    mine = lax.axis_index("dev")
    paired = lax.axis_size("dev") == 8 and lax.axis_size("grp") == 4
    if paired:
        owners = jnp.arange(peers, dtype=jnp.int32) ^ mine
        order = chunk_order()
        index_rows = edge_sender.reshape(total_rows // width, width).astype(BF16)
        packed_nodes = jnp.concatenate(
            [nodes, jnp.pad(index_rows, ((0, 16 - index_rows.shape[0]), (0, 0)))]
        )
        gathered = gather_nodes(packed_nodes)
        tail = gathered[:, count : count + index_rows.shape[0]].reshape(peers, peers, slots)
        senders = lax.dynamic_index_in_dim(tail, mine, 1, keepdims=True).astype(jnp.int32)
    else:
        owners = jnp.arange(peers, dtype=jnp.int32)
        order = jnp.arange(CHUNKS, dtype=jnp.int32)
        gathered = lax.all_gather(nodes, "dev")
        senders = lax.all_to_all(
            edge_sender, "dev", split_axis=0, concat_axis=1, tiled=True
        ).reshape(peers, 1, slots)
    gathered_rows = gathered.shape[1]

    bias_row = edge_bias.reshape(1, width)
    gain_row = edge_gain.reshape(1, width)

    owned = pl.BlockSpec((1, slots, width), lambda i: (i, 0, 0))
    pre = pl.pallas_call(
        lift_kernel,
        grid=(peers,),
        in_specs=[
            owned,
            pl.BlockSpec((1, 1, slots), lambda i: (i, 0, 0)),
            whole(count, width),
            whole(3 * width, width),
            whole(1, width),
        ],
        out_specs=owned,
        out_shape=shape(peers, slots, width),
        compiler_params=params(24),
        cost_estimate=pl.CostEstimate(
            flops=5 * unit, bytes_accessed=6 * total_rows * width, transcendentals=0
        ),
        name="lift",
    )(edges, receivers, nodes, edge_lift, bias_row)

    def by_owner(*dims):
        return pl.BlockSpec(
            (1,) + dims, lambda i, owner, live, order: (owner[i],) + (0,) * len(dims)
        )

    def by_step(*dims):
        return pl.BlockSpec((1,) + dims, lambda i, *_: (i,) + (0,) * len(dims))

    hidden, normed, slope, inverse, base, summed_grad, node_packed, node_small = pl.pallas_call(
        forward_kernel,
        grid_spec=pltpu.PrefetchScalarGridSpec(
            num_scalar_prefetch=3,
            grid=(peers,),
            in_specs=[
                by_owner(slots, width),
                by_step(gathered_rows, width),
                by_step(1, slots),
                by_owner(1, slots),
                whole(count, width),
                whole(count, width),
                pl.BlockSpec((width, width), lambda *_: (1, 0)),
                whole(width, width),
                whole(1, width),
                whole(2 * width, width),
                whole(1, width),
                whole(width, width),
                whole(1, width),
            ],
            out_specs=[
                by_step(slots, width),
                by_step(slots, width),
                by_step(slots, width),
                by_step(slots, 1),
                whole(count, width),
                whole(count, width),
                whole(3 * width, width),
                whole(2, width),
            ],
            scratch_shapes=[pltpu.VMEM((count, width), F32), pltpu.VMEM((3 * width, width), F32)],
        ),
        out_shape=[
            shape(peers, slots, width, kind=BF16),
            shape(peers, slots, width, kind=BF16),
            shape(peers, slots, width, kind=BF16),
            shape(peers, slots, 1),
            shape(count, width),
            shape(count, width, kind=BF16),
            shape(3 * width, width, kind=BF16),
            shape(2, width),
        ],
        compiler_params=params(32),
        cost_estimate=pl.CostEstimate(
            flops=8 * unit, bytes_accessed=16 * total_rows * width, transcendentals=total_rows * width
        ),
        name="forward",
    )(
        owners,
        live,
        order,
        pre,
        gathered,
        senders,
        receivers,
        nodes,
        node_cotangent[0],
        edge_lift,
        edge_mix,
        gain_row,
        node_lift,
        node_bias.reshape(1, width),
        node_mix,
        node_gain.reshape(1, width),
    )

    grad_edges, partial, grad_nodes, edge_packed, edge_small = pl.pallas_call(
        backward_kernel,
        grid_spec=pltpu.PrefetchScalarGridSpec(
            num_scalar_prefetch=3,
            grid=(peers,),
            in_specs=[
                by_owner(slots, width),
                by_owner(slots, width),
                by_step(gathered_rows, width),
                by_step(1, slots),
                by_owner(1, slots),
                by_step(slots, width),
                by_step(slots, width),
                by_step(slots, width),
                by_step(slots, 1),
                whole(count, width),
                whole(count, width),
                whole(count, width),
                whole(3 * width, width),
                whole(width, width),
                whole(1, width),
            ],
            out_specs=[
                by_owner(slots, width),
                pl.BlockSpec((1, 1, count, width), lambda i, *_: (i % 2, i // 2, 0, 0)),
                whole(count, width),
                whole(4 * width, width),
                whole(2, width),
            ],
            scratch_shapes=[pltpu.VMEM((count, width), F32), pltpu.VMEM((4 * width, width), F32)],
        ),
        out_shape=[
            shape(peers, slots, width, kind=BF16),
            shape(2, peers // 2, count, width, kind=BF16),
            shape(count, width),
            shape(4 * width, width, kind=BF16),
            shape(2, width),
        ],
        compiler_params=params(40),
        cost_estimate=pl.CostEstimate(
            flops=14 * unit, bytes_accessed=20 * total_rows * width, transcendentals=0
        ),
        name="backward",
    )(
        owners,
        live,
        order,
        edges,
        edge_seed,
        gathered,
        senders,
        receivers,
        hidden,
        normed,
        slope,
        inverse,
        nodes,
        base,
        summed_grad,
        edge_lift,
        edge_mix,
        gain_row,
    )

    small = jnp.concatenate([edge_small, node_small])
    if paired:
        node_parts = reduce_plane(node_packed)
        edge_parts = reduce_plane(edge_packed)
        sizes = [part.shape[0] for part in node_parts[:1] + edge_parts[:1]]
        lined = reduce_line(node_parts + edge_parts)
        sides = spread_plane([jnp.concatenate([lined[0], lined[2]]), jnp.concatenate([lined[1], lined[3]])])
        node_side, edge_side = [], []
        for side in sides:
            pieces = split_rows(side, sizes * 4)
            node_side += pieces[0::2]
            edge_side += pieces[1::2]
        own = jnp.concatenate(node_side + edge_side)
        other = swap(own, "dev", 1)
        node_half = node_packed.shape[0] // 2
        node_sum = jnp.concatenate([own[:node_half], other[:node_half]])
        edge_sum = jnp.concatenate([own[node_half:], other[node_half:]])
        small = small_sum(small)
        from_senders = reduce_senders(partial)
    else:
        node_sum, edge_sum, small = lax.psum((node_packed.astype(F32), edge_packed.astype(F32), small), ("grp", "dev"))
        ordered = jnp.swapaxes(partial, 0, 1).reshape(peers, count, width)
        from_senders = lax.psum_scatter(ordered.astype(F32), "dev", scatter_dimension=0)
    grad_nodes = grad_nodes + contract_features(
        from_senders.astype(BF16), edge_lift[width : 2 * width]
    )
    groups = lax.axis_size("grp") * lax.axis_size("dev")
    edge_scale = float(total_rows * groups) ** (-0.5)
    node_scale = float(count * groups) ** (-0.5)
    edge_lift_grad, edge_mix_grad, node_lift_grad, node_mix_grad = pl.pallas_call(
        lambda *refs: unpack_kernel((edge_scale, node_scale), *refs),
        grid_spec=pltpu.PrefetchScalarGridSpec(
            num_scalar_prefetch=1,
            grid=(1,),
            in_specs=[whole(3 * width, width), whole(4 * width, width)],
            out_specs=[
                whole(3 * width, width),
                whole(width, width),
                whole(2 * width, width),
                whole(width, width),
            ],
            scratch_shapes=[
                pltpu.VMEM((4 * width, width), F32),
                pltpu.VMEM((3 * width, width), F32),
            ],
        ),
        out_shape=[
            shape(3 * width, width),
            shape(width, width),
            shape(2 * width, width),
            shape(width, width),
        ],
        compiler_params=params(48),
        name="unpack",
    )(order, node_sum, edge_sum)
    return (
        grad_nodes[None],
        grad_edges.reshape(1, 1, peers, slots, width),
        edge_lift_grad,
        small[0] * edge_scale,
        edge_mix_grad,
        small[1] * edge_scale,
        node_lift_grad,
        small[2] * node_scale,
        node_mix_grad,
        small[3] * node_scale,
    )


def solution(mesh):
    return jax.shard_map(
        per_device,
        mesh=mesh,
        in_specs=(
            P("grp", "dev", None),
            P("grp", "dev", None, None, None),
            P("grp", "dev", None),
            P("grp", "dev", None, None, None),
            P(None, "dev", None),
            P("dev", None, None),
            P("dev", None),
            P(),
            P(),
            P(),
            P(),
            P(),
            P(),
            P(),
            P(),
        ),
        out_specs=(
            P("grp", "dev", None),
            P("grp", "dev", None, None, None),
            P(),
            P(),
            P(),
            P(),
            P(),
            P(),
            P(),
            P(),
        ),
        check_vma=False,
    )
```

time: 371 us -> 191 us (0.51)
  blocking collectives: 84.2 us -> 0 us
  waiting for transfers between devices: 131 us -> 73.1 us
  matrix products: 42.5 us -> 0.34 us
  Pallas kernels: 0 us -> 41.9 us
  starting transfers between devices: 10.9 us -> 42 us
  local copies, waits for them, and re-layouts: 55.5 us -> 25.4 us
  other arithmetic: 31.9 us -> 6.37 us
  between operations: 14.5 us -> 1.28 us
    psum x1 -> x0, waiting for transfers between devices: 99.6 us -> none  [per_device(): lax.psum((edge_lift_grad, edge_bias_grad, edge_mix_grad, edge_gain_grad,...]
    psum x1 -> x0, blocking collectives: 84.2 us -> none  [per_device(): lax.psum((edge_lift_grad, edge_bias_grad, edge_mix_grad, edge_gain_grad,...]
    ppermute x0 -> x33, waiting for transfers between devices: none -> 73.1 us  [swap(): return lax.ppermute(values, axis, [(i, i ^ bit) for i in range(size)])]
    ppermute x0 -> x33, starting transfers between devices: none -> 42 us  [swap(): return lax.ppermute(values, axis, [(i, i ^ bit) for i in range(size)])]
    pallas_call x0 -> x4, Pallas kernels: none -> 41.9 us  [the longest x1 18.3 us: per_device(): pl.pallas_call(backward_kernel, grid_spec=pltpu.PrefetchScalarGridSpec(nu...]
    gather x4 -> x0, local copies, waits for them, and re-layouts: 33.8 us -> none  [the longest x2 14.4 us: per_device(): jnp.take(grad_joined[:, width:], receiver_index, axis=0)]
    dot_general x15 -> x0, matrix products: 33.3 us -> none  [the longest x8 19 us: matmul(): return jnp.dot(left, right, preferred_element_type=jnp.float32)]
    all_to_all x2 -> x0, waiting for transfers between devices: 31.2 us -> none  [the longest x1 31.2 us: per_device(): lax.all_to_all(outgoing, 'dev', split_axis=0, concat_axis=0, tiled=True)]
  transfers between devices with their start and end apart: 3 -> 33, of which waited for: 2 -> 20; matrix products, arithmetic and copies ran while one was open for 13% -> 7% of each run, Pallas kernels for 0% -> 12%
where the time goes in v1:
time: 191 us; the launch traced here: 190 us
  waiting for transfers between devices  73.1 us (38%)
  starting transfers between devices  42 us (22%)
  Pallas kernels  41.9 us (22%)
  local copies, waits for them, and re-layouts  25.4 us (13%)
  other arithmetic  6.37 us (3%)
    ppermute x33, waiting for transfers between devices, swap(): return lax.ppermute(values, axis, [(i, i ^ bit) for i in range(size)])  73.1 us
    ppermute x33, starting transfers between devices, swap(): return lax.ppermute(values, axis, [(i, i ^ bit) for i in range(size)])  42 us
    unnamed x72, local copies, waits for them, and re-layouts  22.5 us
    pallas_call x1, Pallas kernels, per_device(): pl.pallas_call(backward_kernel, grid_spec=pltpu.PrefetchScalarGridSpec(nu...  18.3 us
    pallas_call x1, Pallas kernels, per_device(): pl.pallas_call(forward_kernel, grid_spec=pltpu.PrefetchScalarGridSpec(num...  14.1 us
    pallas_call x1, Pallas kernels, per_device(): pl.pallas_call(lift_kernel, grid=(peers,), in_specs=[owned, pl.BlockSpec(...  4.85 us
    pallas_call x1, Pallas kernels, per_device(): pl.pallas_call(lambda *refs: unpack_kernel((edge_scale, node_scale), *ref...  4.55 us
  transfers between devices with their start and end apart: 33, of which 20 were waited for; matrix products, arithmetic and copies ran while one was open for 7% of the time, Pallas kernels for 12%

profile of v1, /device:TPU:0, one launch (start us, length us, event | category | flops | bytes accessed | tf_op | source)
XLA Modules:
  0.0 190.3 jit_solution(3834644474799032460)
XLA Ops:
  2.4 4.1 %collective-permute-start.3 = (bf16[272,512]{1,0:T(8,128)(2,1)S(1)}, bf16[272,512]{1,0:T(8,128)(2,1)}, u32[]{:S(2)}, u32[]{:S(2)}) collective-permute-start(bf16[272,512]{1,0:T(8,128)(2,1)S(1)} %fusion.5), channel_id=1, source_target_pairs={{0,4},{1,5},{2,6},{3,7},{4,0},{5,1},{6,2},{7,3},{8,12},{9,13},{10,... | collective-permute-start | bytes 835592 | tf_op jit(solution)/shard_map/ppermute | solution.py:244
  15.1 4.9 %lift.1.pre_ref = f32[8,256,512]{2,1,0:T(8,128)S(1)} custom-call(bf16[8,256,512]{2,1,0:T(8,128)(2,1)S(1)} %bitcast.50, s32[8,1,256]{2,1,0:T(1,128)S(1)} %reshape.68.receiver_ref, bf16[256,512]{1,0:T(8,128)(2,1)S(1)} %bitcast.47, bf16[1536,512]{1,0:T(8,128)(2,1)S(1)} %copy-done.2, f32[1,512]{1,0:T(1,128)S(1)} %bitcast.54), custom_call_target="tpu_custom_call" | custom-call | flops 2684354560 | bytes 6291456 | tf_op jit(solution)/shard_map/lift/pallas_call | solution.py:389
  22.5 3.9 %collective-permute-done.5 = bf16[272,512]{1,0:T(8,128)(2,1)} collective-permute-done((bf16[272,512]{1,0:T(8,128)(2,1)S(1)}, bf16[272,512]{1,0:T(8,128)(2,1)}, u32[]{:S(2)}, u32[]{:S(2)}) %collective-permute-start.5) | collective-permute-done | bytes 278560 | tf_op jit(solution)/shard_map/ppermute | solution.py:244
  37.5 2.2 %copy-done.17 = f32[8,256,512]{2,1,0:T(8,128)S(1)} copy-done((f32[8,256,512]{2,1,0:T(8,128)S(1)}, f32[8,256,512]{2,1,0:T(8,128)}, u32[]{:S(2)}) %copy-start.17) | copy-done | bytes 4194328
  39.7 14.1 %forward.1 = (bf16[8,256,512]{2,1,0:T(8,128)(2,1)S(1)}, bf16[8,256,512]{2,1,0:T(8,128)(2,1)S(1)}, bf16[8,256,512]{2,1,0:T(8,128)(2,1)S(1)}, f32[8,256,1]{2,1,0:T...) custom-call(s32[8]{0:T(128)S(1)} %iota_xor_fusion.owner_ref, ...), custom_call_target="tpu_custom_call" | custom-call | flops 4294967296 | bytes 16777216 | tf_op jit(solution)/shard_map/forward/pallas_call | solution.py:416
  58.5 18.3 %backward.1 = (bf16[8,256,512]{2,1,0:T(8,128)(2,1)}, bf16[2,4,256,512]{3,2,1,0:T(8,128)(2,1)S(1)}, f32[256,512]{1,0:T(8,128)S(1)}, bf16[2048,512]{1,0:T(8,128)(2,1)S(1)}, f32[2,512]{1,0:T(2,128)S(1)}) custom-call(s32[8]{0:T(128)S(1)} %iota_xor_fusion.owner_ref, s32[8]{0:T(128)S(1)} %bitcast.60, s32[32]{0:T(128)S(1)} %fusion.7.order_ref.refs_0_, ...), custom_call_target="tpu_custom_call" | custom-call | flops 7516192768 | bytes 20971520 | tf_op jit(solution)/shard_map/backward/pallas_call | solution.py:482
  77.3 2.1 %collective-permute-start.11 = (bf16[192,512]{1,0:T(8,128)(2,1)S(1)}, bf16[192,512]{1,0:T(8,128)(2,1)S(1)}, u32[]{:S(2)}, u32[]{:S(2)}) collective-permute-start(bf16[192,512]{1,0:T(8,128)(2,1)S(1)} %get-tuple-element.50), channel_id=1, source_target_pairs={{0,8},{8,0},{16,24},{24,16},{1,9},{9,1},{17,25},{25,17},{2,10},{10... | collective-permute-start | bytes 589832 | tf_op jit(solution)/shard_map/ppermute | solution.py:244
  80.9 4.0 %collective-permute-done.11 = bf16[192,512]{1,0:T(8,128)(2,1)S(1)} collective-permute-done((bf16[192,512]{1,0:T(8,128)(2,1)S(1)}, bf16[192,512]{1,0:T(8,128)(2,1)S(1)}, u32[]{:S(2)}, u32[]{:S(2)}) %collective-permute-start.11) | collective-permute-done | bytes 196640 | tf_op jit(solution)/shard_map/ppermute | solution.py:244
  92.1 4.7 %collective-permute-done.16 = bf16[256,512]{1,0:T(8,128)(2,1)S(1)} collective-permute-done((bf16[256,512]{1,0:T(8,128)(2,1)S(1)}, bf16[256,512]{1,0:T(8,128)(2,1)S(1)}, u32[]{:S(2)}, u32[]{:S(2)}) %collective-permute-start.16) | collective-permute-done | bytes 262176 | tf_op jit(solution)/shard_map/ppermute | solution.py:244
  99.8 2.6 %collective-permute-done.19 = bf16[128,512]{1,0:T(8,128)(2,1)S(1)} collective-permute-done((bf16[128,512]{1,0:T(8,128)(2,1)S(1)}, bf16[128,512]{1,0:T(8,128)(2,1)S(1)}, u32[]{:S(2)}, u32[]{:S(2)}) %collective-permute-start.19) | collective-permute-done | bytes 131104 | tf_op jit(solution)/shard_map/ppermute | solution.py:244
  104.2 5.0 %collective-permute-start.20 = (bf16[224,512]{1,0:T(8,128)(2,1)S(1)}, bf16[224,512]{1,0:T(8,128)(2,1)S(1)}, u32[]{:S(2)}, u32[]{:S(2)}) collective-permute-start(bf16[224,512]{1,0:T(8,128)(2,1)S(1)} %pad_maximum_fusion), channel_id=1, source_target_pairs={{0,2},{1,3},{2,0},{3,1},{4,6},{5,7},{6,4},{7,5},{8,10},{9,11},{10,... | collective-permute-start | bytes 688136 | tf_op jit(solution)/shard_map/ppermute | solution.py:244
  109.1 4.0 %collective-permute-done.20 = bf16[224,512]{1,0:T(8,128)(2,1)S(1)} collective-permute-done((bf16[224,512]{1,0:T(8,128)(2,1)S(1)}, bf16[224,512]{1,0:T(8,128)(2,1)S(1)}, u32[]{:S(2)}, u32[]{:S(2)}) %collective-permute-start.20) | collective-permute-done | bytes 229408 | tf_op jit(solution)/shard_map/ppermute | solution.py:244
  113.2 6.1 %collective-permute-start.21 = (bf16[224,512]{1,0:T(8,128)(2,1)S(1)}, bf16[224,512]{1,0:T(8,128)(2,1)S(1)}, u32[]{:S(2)}, u32[]{:S(2)}) collective-permute-start(bf16[224,512]{1,0:T(8,128)(2,1)S(1)} %add_convert_fusion.6), channel_id=1, source_target_pairs={{0,4},{1,5},{2,6},{3,7},{4,0},{5,1},{6,2},{7,3},{8,12},{9,13},{10,... | collective-permute-start | bytes 688136 | tf_op jit(solution)/shard_map/ppermute | solution.py:244
  119.3 5.5 %collective-permute-done.21 = bf16[224,512]{1,0:T(8,128)(2,1)S(1)} collective-permute-done((bf16[224,512]{1,0:T(8,128)(2,1)S(1)}, bf16[224,512]{1,0:T(8,128)(2,1)S(1)}, u32[]{:S(2)}, u32[]{:S(2)}) %collective-permute-start.21) | collective-permute-done | bytes 229408 | tf_op jit(solution)/shard_map/ppermute | solution.py:244
  125.0 6.0 %collective-permute-done.22 = bf16[224,512]{1,0:T(8,128)(2,1)S(1)} collective-permute-done((bf16[224,512]{1,0:T(8,128)(2,1)S(1)}, bf16[224,512]{1,0:T(8,128)(2,1)S(1)}, u32[]{:S(2)}, u32[]{:S(2)}) %collective-permute-start.22) | collective-permute-done | bytes 229408 | tf_op jit(solution)/shard_map/ppermute | solution.py:244
  132.0 5.2 %collective-permute-done.23 = bf16[224,512]{1,0:T(8,128)(2,1)S(1)} collective-permute-done((bf16[224,512]{1,0:T(8,128)(2,1)S(1)}, bf16[224,512]{1,0:T(8,128)(2,1)S(1)}, u32[]{:S(2)}, u32[]{:S(2)}) %collective-permute-start.23) | collective-permute-done | bytes 229408 | tf_op jit(solution)/shard_map/ppermute | solution.py:244
  138.3 9.9 %collective-permute-done.24 = bf16[448,512]{1,0:T(8,128)(2,1)S(1)} collective-permute-done((bf16[448,512]{1,0:T(8,128)(2,1)S(1)}, bf16[448,512]{1,0:T(8,128)(2,1)S(1)}, u32[]{:S(2)}, u32[]{:S(2)}) %collective-permute-start.24) | collective-permute-done | bytes 458784 | tf_op jit(solution)/shard_map/ppermute | solution.py:244
  149.3 5.2 %collective-permute-done.25 = bf16[224,512]{1,0:T(8,128)(2,1)S(1)} collective-permute-done((bf16[224,512]{1,0:T(8,128)(2,1)S(1)}, bf16[224,512]{1,0:T(8,128)(2,1)S(1)}, u32[]{:S(2)}, u32[]{:S(2)}) %collective-permute-start.25) | collective-permute-done | bytes 229408 | tf_op jit(solution)/shard_map/ppermute | solution.py:244
  155.8 7.2 %collective-permute-done.26 = bf16[448,512]{1,0:T(8,128)(2,1)S(1)} collective-permute-done((bf16[448,512]{1,0:T(8,128)(2,1)S(1)}, bf16[448,512]{1,0:T(8,128)(2,1)S(1)}, u32[]{:S(2)}, u32[]{:S(2)}) %collective-permute-start.26) | collective-permute-done | bytes 458784 | tf_op jit(solution)/shard_map/ppermute | solution.py:244
  165.1 2.5 %collective-permute-start.9 = (bf16[256,512]{1,0:T(8,128)(2,1)S(1)}, bf16[256,512]{1,0:T(8,128)(2,1)S(1)}, u32[]{:S(2)}, u32[]{:S(2)}) collective-permute-start(bf16[256,512]{1,0:T(8,128)(2,1)S(1)} %slice_bitcast_fusion.1), channel_id=1, source_target_pairs={{0,4},{1,5},{2,6},{3,7},{4,0},{5,1},{6,2},{7,3},{8,12},{9,13},{10,... | collective-permute-start | bytes 786440 | tf_op jit(solution)/shard_map/ppermute | solution.py:244
  167.6 2.6 %collective-permute-start.29 = (f32[4,512]{1,0:T(4,128)S(1)}, f32[4,512]{1,0:T(4,128)S(1)}, u32[]{:S(2)}, u32[]{:S(2)}) collective-permute-start(f32[4,512]{1,0:T(4,128)S(1)} %fusion.8), channel_id=1, source_target_pairs={{0,8},{8,0},{16,24},{24,16},{1,9},{9,1},{17,25},{25,17},{2,10},{10... | collective-permute-start | bytes 24584 | tf_op jit(solution)/shard_map/ppermute | solution.py:244
  175.6 3.6 %collective-permute-done.31 = f32[4,512]{1,0:T(4,128)S(1)} collective-permute-done((f32[4,512]{1,0:T(4,128)S(1)}, f32[4,512]{1,0:T(4,128)S(1)}, u32[]{:S(2)}, u32[]{:S(2)}) %collective-permute-start.31) | collective-permute-done | bytes 8224 | tf_op jit(solution)/shard_map/ppermute | solution.py:244
  181.3 2.5 %collective-permute-done.32 = f32[4,512]{1,0:T(4,128)S(1)} collective-permute-done((f32[4,512]{1,0:T(4,128)S(1)}, f32[4,512]{1,0:T(4,128)S(1)}, u32[]{:S(2)}, u32[]{:S(2)}) %collective-permute-start.32) | collective-permute-done | bytes 8224 | tf_op jit(solution)/shard_map/ppermute | solution.py:244
  185.8 4.5 %unpack.1 = (f32[1536,512]{1,0:T(8,128)}, f32[512,512]{1,0:T(8,128)}, f32[1024,512]{1,0:T(8,128)}, f32[512,512]{1,0:T(8,128)}) custom-call(s32[32]{0:T(128)S(1)} %fusion.7.order_ref.refs_0_, bf16[1536,512]{1,0:T(8,128)(2,1)S(1)} %slice_dynamic-update-slice_fusion.1.refs_1_, bf16[2048,512]{1,0:T(8,128)(2,1)S(1)} %slice_dynamic-update-slice_fusion.refs_2_), custom_call_target="tpu_custom_call" | custom-call | tf_op jit(solution)/shard_map/unpack/pallas_call | solution.py:575
  (172 shorter events, 58.3 us)
Async XLA Ops:
  2.4 19.6 %collective-permute-start.3 = (bf16[272,512]{1,0:T(8,128)(2,1)S(1)}, bf16[272,512]{1,0:T(8,128)(2,1)}, u32[]{:S(2)}, u32[]{:S(2)}) collective-permute-start(bf16[272,512]{1,0:T(8,128)(2,1)S(1)} %fusion.5), channel_id=1, source_target_pairs={{0,4},{1,5},{2,6},{3,7},{4,0},{5,1},{6,2},{7,3},{8,12},{9,13},{10,... | collective-permute-start | bytes 835592 | tf_op jit(solution)/shard_map/ppermute | solution.py:244
  6.5 16.0 %collective-permute-start.1 = (bf16[272,512]{1,0:T(8,128)(2,1)S(1)}, bf16[272,512]{1,0:T(8,128)(2,1)}, u32[]{:S(2)}, u32[]{:S(2)}) collective-permute-start(bf16[272,512]{1,0:T(8,128)(2,1)S(1)} %fusion.5), channel_id=1, source_target_pairs={{0,2},{1,3},{2,0},{3,1},{4,6},{5,7},{6,4},{7,5},{8,10},{9,11},{10,... | collective-permute-start | bytes 835592 | tf_op jit(solution)/shard_map/ppermute | solution.py:244
  8.0 18.3 %collective-permute-start = (bf16[272,512]{1,0:T(8,128)(2,1)S(1)}, bf16[272,512]{1,0:T(8,128)(2,1)S(1)}, u32[]{:S(2)}, u32[]{:S(2)}) collective-permute-start(bf16[272,512]{1,0:T(8,128)(2,1)S(1)} %fusion.5), channel_id=1, source_target_pairs={{0,1},{1,0},{2,3},{3,2},{4,5},{5,4},{6,7},{7,6},{8,9},{9,8},{10,11... | collective-permute-start | bytes 835592 | tf_op jit(solution)/shard_map/ppermute | solution.py:244
  8.0 18.3 %collective-permute-start.5 = (bf16[272,512]{1,0:T(8,128)(2,1)S(1)}, bf16[272,512]{1,0:T(8,128)(2,1)}, u32[]{:S(2)}, u32[]{:S(2)}) collective-permute-start(bf16[272,512]{1,0:T(8,128)(2,1)S(1)} %fusion.5), channel_id=1, source_target_pairs={{0,6},{1,7},{2,4},{3,5},{4,2},{5,3},{6,0},{7,1},{8,14},{9,15},{10,... | collective-permute-start | bytes 835592 | tf_op jit(solution)/shard_map/ppermute | solution.py:244
  21.9 9.5 %collective-permute-start.4 = (bf16[272,512]{1,0:T(8,128)(2,1)}, bf16[272,512]{1,0:T(8,128)(2,1)S(1)}, u32[]{:S(2)}, u32[]{:S(2)}) collective-permute-start(bf16[272,512]{1,0:T(8,128)(2,1)} %collective-permute-done.3), channel_id=1, source_target_pairs={{0,1},{1,0},{2,3},{3,2},{4,5},{5,4},{6,7},{7,6},{8,9},{9,8},{10,11... | collective-permute-start | bytes 835592 | tf_op jit(solution)/shard_map/ppermute | solution.py:244
  22.4 6.6 %collective-permute-start.2 = (bf16[272,512]{1,0:T(8,128)(2,1)}, bf16[272,512]{1,0:T(8,128)(2,1)S(1)}, u32[]{:S(2)}, u32[]{:S(2)}) collective-permute-start(bf16[272,512]{1,0:T(8,128)(2,1)} %collective-permute-done.1), channel_id=1, source_target_pairs={{0,1},{1,0},{2,3},{3,2},{4,5},{5,4},{6,7},{7,6},{8,9},{9,8},{10,11... | collective-permute-start | bytes 835592 | tf_op jit(solution)/shard_map/ppermute | solution.py:244
  26.4 7.5 %collective-permute-start.6 = (bf16[272,512]{1,0:T(8,128)(2,1)}, bf16[272,512]{1,0:T(8,128)(2,1)S(1)}, u32[]{:S(2)}, u32[]{:S(2)}) collective-permute-start(bf16[272,512]{1,0:T(8,128)(2,1)} %collective-permute-done.5), channel_id=1, source_target_pairs={{0,1},{1,0},{2,3},{3,2},{4,5},{5,4},{6,7},{7,6},{8,9},{9,8},{10,11... | collective-permute-start | bytes 835592 | tf_op jit(solution)/shard_map/ppermute | solution.py:244
  57.9 19.1 %collective-permute-start.10 = (bf16[768,512]{1,0:T(8,128)(2,1)S(1)}, bf16[768,512]{1,0:T(8,128)(2,1)S(1)}, u32[]{:S(2)}, u32[]{:S(2)}) collective-permute-start(bf16[768,512]{1,0:T(8,128)(2,1)S(1)} %slice.211), channel_id=1, source_target_pairs={{0,1},{1,0},{2,3},{3,2},{4,5},{5,4},{6,7},{7,6},{8,9},{9,8},{10,11... | collective-permute-start | bytes 2359304 | tf_op jit(solution)/shard_map/ppermute | solution.py:244
  76.9 11.7 %collective-permute-start.15 = (bf16[1024,512]{1,0:T(8,128)(2,1)S(1)}, bf16[1024,512]{1,0:T(8,128)(2,1)S(1)}, u32[]{:S(2)}, u32[]{:S(2)}) collective-permute-start(bf16[1024,512]{1,0:T(8,128)(2,1)S(1)} %slice.223), channel_id=1, source_target_pairs={{0,1},{1,0},{2,3},{3,2},{4,5},{5,4},{6,7},{7,6},{8,9},{9,8},{10,11... | collective-permute-start | bytes 3145736 | tf_op jit(solution)/shard_map/ppermute | solution.py:244
  77.3 7.6 %collective-permute-start.11 = (bf16[192,512]{1,0:T(8,128)(2,1)S(1)}, bf16[192,512]{1,0:T(8,128)(2,1)S(1)}, u32[]{:S(2)}, u32[]{:S(2)}) collective-permute-start(bf16[192,512]{1,0:T(8,128)(2,1)S(1)} %get-tuple-element.50), channel_id=1, source_target_pairs={{0,8},{8,0},{16,24},{24,16},{1,9},{9,1},{17,25},{25,17},{2,10},{10... | collective-permute-start | bytes 589832 | tf_op jit(solution)/shard_map/ppermute | solution.py:244
  79.4 7.0 %collective-permute-start.13 = (bf16[192,512]{1,0:T(8,128)(2,1)S(1)}, bf16[192,512]{1,0:T(8,128)(2,1)S(1)}, u32[]{:S(2)}, u32[]{:S(2)}) collective-permute-start(bf16[192,512]{1,0:T(8,128)(2,1)S(1)} %get-tuple-element.51), channel_id=1, source_target_pairs={{0,16},{8,24},{16,0},{24,8},{1,17},{9,25},{17,1},{25,9},{2,18},{10... | collective-permute-start | bytes 589832 | tf_op jit(solution)/shard_map/ppermute | solution.py:244
  88.9 7.8 %collective-permute-start.16 = (bf16[256,512]{1,0:T(8,128)(2,1)S(1)}, bf16[256,512]{1,0:T(8,128)(2,1)S(1)}, u32[]{:S(2)}, u32[]{:S(2)}) collective-permute-start(bf16[256,512]{1,0:T(8,128)(2,1)S(1)} %get-tuple-element.46), channel_id=1, source_target_pairs={{0,8},{8,0},{16,24},{24,16},{1,9},{9,1},{17,25},{25,17},{2,10},{10... | collective-permute-start | bytes 786440 | tf_op jit(solution)/shard_map/ppermute | solution.py:244
  90.5 6.7 %collective-permute-start.18 = (bf16[256,512]{1,0:T(8,128)(2,1)S(1)}, bf16[256,512]{1,0:T(8,128)(2,1)S(1)}, u32[]{:S(2)}, u32[]{:S(2)}) collective-permute-start(bf16[256,512]{1,0:T(8,128)(2,1)S(1)} %get-tuple-element.47), channel_id=1, source_target_pairs={{0,16},{8,24},{16,0},{24,8},{1,17},{9,25},{17,1},{25,9},{2,18},{10... | collective-permute-start | bytes 786440 | tf_op jit(solution)/shard_map/ppermute | solution.py:244
  104.2 9.0 %collective-permute-start.20 = (bf16[224,512]{1,0:T(8,128)(2,1)S(1)}, bf16[224,512]{1,0:T(8,128)(2,1)S(1)}, u32[]{:S(2)}, u32[]{:S(2)}) collective-permute-start(bf16[224,512]{1,0:T(8,128)(2,1)S(1)} %pad_maximum_fusion), channel_id=1, source_target_pairs={{0,2},{1,3},{2,0},{3,1},{4,6},{5,7},{6,4},{7,5},{8,10},{9,11},{10,... | collective-permute-start | bytes 688136 | tf_op jit(solution)/shard_map/ppermute | solution.py:244
  113.2 11.7 %collective-permute-start.21 = (bf16[224,512]{1,0:T(8,128)(2,1)S(1)}, bf16[224,512]{1,0:T(8,128)(2,1)S(1)}, u32[]{:S(2)}, u32[]{:S(2)}) collective-permute-start(bf16[224,512]{1,0:T(8,128)(2,1)S(1)} %add_convert_fusion.6), channel_id=1, source_target_pairs={{0,4},{1,5},{2,6},{3,7},{4,0},{5,1},{6,2},{7,3},{8,12},{9,13},{10,... | collective-permute-start | bytes 688136 | tf_op jit(solution)/shard_map/ppermute | solution.py:244
  124.9 6.1 %collective-permute-start.22 = (bf16[224,512]{1,0:T(8,128)(2,1)S(1)}, bf16[224,512]{1,0:T(8,128)(2,1)S(1)}, u32[]{:S(2)}, u32[]{:S(2)}) collective-permute-start(bf16[224,512]{1,0:T(8,128)(2,1)S(1)} %add_convert_fusion.5), channel_id=1, source_target_pairs={{0,2},{1,3},{2,0},{3,1},{4,6},{5,7},{6,4},{7,5},{8,10},{9,11},{10,... | collective-permute-start | bytes 688136 | tf_op jit(solution)/shard_map/ppermute | solution.py:244
  131.1 6.1 %collective-permute-start.23 = (bf16[224,512]{1,0:T(8,128)(2,1)S(1)}, bf16[224,512]{1,0:T(8,128)(2,1)S(1)}, u32[]{:S(2)}, u32[]{:S(2)}) collective-permute-start(bf16[224,512]{1,0:T(8,128)(2,1)S(1)} %pad_maximum_fusion.1), channel_id=1, source_target_pairs={{0,16},{8,24},{16,0},{24,8},{1,17},{9,25},{17,1},{25,9},{2,18},{10... | collective-permute-start | bytes 688136 | tf_op jit(solution)/shard_map/ppermute | solution.py:244
  137.2 11.0 %collective-permute-start.24 = (bf16[448,512]{1,0:T(8,128)(2,1)S(1)}, bf16[448,512]{1,0:T(8,128)(2,1)S(1)}, u32[]{:S(2)}, u32[]{:S(2)}) collective-permute-start(bf16[448,512]{1,0:T(8,128)(2,1)S(1)} %constant_dynamic-update-slice_fusion), channel_id=1, source_target_pairs={{0,8},{8,0},{16,24},{24,16},{1,9},{9,1},{17,25},{25,17},{2,10},{10... | collective-permute-start | bytes 1376264 | tf_op jit(solution)/shard_map/ppermute | solution.py:244
  138.2 17.1 %collective-permute-start.7 = (bf16[4,256,512]{2,1,0:T(8,128)(2,1)S(1)}, bf16[4,256,512]{2,1,0:T(8,128)(2,1)S(1)}, u32[]{:S(2)}, u32[]{:S(2)}) collective-permute-start(bf16[4,256,512]{2,1,0:T(8,128)(2,1)S(1)} %slice_bitcast_fusion), channel_id=1, source_target_pairs={{0,1},{1,0},{2,3},{3,2},{4,5},{5,4},{6,7},{7,6},{8,9},{9,8},{10,11... | collective-permute-start | bytes 3145736 | tf_op jit(solution)/shard_map/ppermute | solution.py:244
  148.4 6.1 %collective-permute-start.25 = (bf16[224,512]{1,0:T(8,128)(2,1)S(1)}, bf16[224,512]{1,0:T(8,128)(2,1)S(1)}, u32[]{:S(2)}, u32[]{:S(2)}) collective-permute-start(bf16[224,512]{1,0:T(8,128)(2,1)S(1)} %pad_maximum_fusion.2), channel_id=1, source_target_pairs={{0,8},{8,0},{16,24},{24,16},{1,9},{9,1},{17,25},{25,17},{2,10},{10... | collective-permute-start | bytes 688136 | tf_op jit(solution)/shard_map/ppermute | solution.py:244
  154.5 8.5 %collective-permute-start.26 = (bf16[448,512]{1,0:T(8,128)(2,1)S(1)}, bf16[448,512]{1,0:T(8,128)(2,1)S(1)}, u32[]{:S(2)}, u32[]{:S(2)}) collective-permute-start(bf16[448,512]{1,0:T(8,128)(2,1)S(1)} %constant_dynamic-update-slice_fusion.5), channel_id=1, source_target_pairs={{0,16},{8,24},{16,0},{24,8},{1,17},{9,25},{17,1},{25,9},{2,18},{10... | collective-permute-start | bytes 1376264 | tf_op jit(solution)/shard_map/ppermute | solution.py:244
  155.7 9.2 %collective-permute-start.8 = (bf16[2,256,512]{2,1,0:T(8,128)(2,1)S(1)}, bf16[2,256,512]{2,1,0:T(8,128)(2,1)S(1)}, u32[]{:S(2)}, u32[]{:S(2)}) collective-permute-start(bf16[2,256,512]{2,1,0:T(8,128)(2,1)S(1)} %slice.206), channel_id=1, source_target_pairs={{0,2},{1,3},{2,0},{3,1},{4,6},{5,7},{6,4},{7,5},{8,10},{9,11},{10,... | collective-permute-start | bytes 1572872 | tf_op jit(solution)/shard_map/ppermute | solution.py:244
  163.3 22.4 %collective-permute-start.27 = (bf16[1792,512]{1,0:T(8,128)(2,1)S(1)}, bf16[1792,512]{1,0:T(8,128)(2,1)S(1)}, u32[]{:S(2)}, u32[]{:S(2)}) collective-permute-start(bf16[1792,512]{1,0:T(8,128)(2,1)S(1)} %get-tuple-element.53), channel_id=1, source_target_pairs={{0,1},{1,0},{2,3},{3,2},{4,5},{5,4},{6,7},{7,6},{8,9},{9,8},{10,11... | collective-permute-start | bytes 5505032 | tf_op jit(solution)/shard_map/ppermute | solution.py:244
  165.1 19.3 %collective-permute-start.9 = (bf16[256,512]{1,0:T(8,128)(2,1)S(1)}, bf16[256,512]{1,0:T(8,128)(2,1)S(1)}, u32[]{:S(2)}, u32[]{:S(2)}) collective-permute-start(bf16[256,512]{1,0:T(8,128)(2,1)S(1)} %slice_bitcast_fusion.1), channel_id=1, source_target_pairs={{0,4},{1,5},{2,6},{3,7},{4,0},{5,1},{6,2},{7,3},{8,12},{9,13},{10,... | collective-permute-start | bytes 786440 | tf_op jit(solution)/shard_map/ppermute | solution.py:244
  (30 other events, 160.3 us)

commit v2 on v0

v2 whole, which is shorter than its diff:
```python
import functools

import jax
import jax.numpy as jnp
from jax import lax
from jax.experimental import pallas as pl
from jax.experimental.pallas import tpu as pltpu
from jax.sharding import PartitionSpec as P

EPSILON = 1e-05
CHUNKS = 32
BF16 = jnp.bfloat16
F32 = jnp.float32


def matmul(left, right):
    return jnp.dot(left, right, preferred_element_type=F32)


def contract_rows(left, right):
    return lax.dot_general(left, right, (((0,), (0,)), ((), ())), preferred_element_type=F32)


def contract_features(left, right):
    return lax.dot_general(left, right, (((1,), (1,)), ((), ())), preferred_element_type=F32)


def one_hot(index_row, nodes):
    rows = lax.broadcasted_iota(jnp.int32, (nodes, index_row.shape[1]), 0)
    return jnp.where(rows == index_row, 1.0, 0.0).astype(BF16)


def silu_pair(values):
    gate = 0.5 * jnp.tanh(0.5 * values) + 0.5
    hidden = values * gate
    return hidden, gate + hidden * (1.0 - gate)


def norm_forward(values):
    centred = values - jnp.mean(values, axis=-1, keepdims=True)
    inverse = lax.rsqrt(jnp.mean(centred * centred, axis=-1, keepdims=True) + EPSILON)
    return centred * inverse, inverse


def norm_backward(grad_hat, normed, inverse):
    spread = jnp.mean(grad_hat * normed, axis=-1, keepdims=True)
    return inverse * (grad_hat - jnp.mean(grad_hat, axis=-1, keepdims=True) - normed * spread)


def pick_row(block, place):
    rows = lax.broadcasted_iota(jnp.int32, block.shape, 0)
    picked = jnp.sum(jnp.where(rows == place, block.astype(F32), 0.0), axis=0, keepdims=True)
    return picked.astype(jnp.int32)


def pack_kernel(nodes_ref, sender_ref, packed_ref):
    count, width = nodes_ref.shape
    peers, _, slots = sender_ref.shape
    packed_ref[:count] = nodes_ref[...]
    packed_ref[count:] = jnp.zeros((packed_ref.shape[0] - count, width), BF16)
    packed_ref[count : count + peers, :slots] = sender_ref[:, 0, :].astype(F32).astype(BF16)


def live_rows(count, shape):
    return lax.broadcasted_iota(jnp.int32, shape, 0) < count


def store_chunks(order_ref, source_ref, target_ref, mix_rows):
    mix_part = mix_rows // CHUNKS
    rows = source_ref.shape[0] // CHUNKS
    lift_part = rows - mix_part
    lift_rows = lift_part * CHUNKS

    def step(place, carry):
        chunk = order_ref[place]
        target = pl.multiple_of(place * rows, 16)
        lift_start = pl.multiple_of(chunk * lift_part, 16)
        mix_start = pl.multiple_of(lift_rows + chunk * mix_part, 16)
        target_ref[pl.ds(target, lift_part), :] = source_ref[
            pl.ds(lift_start, lift_part), :
        ].astype(BF16)
        target_ref[pl.ds(pl.multiple_of(target + lift_part, 16), mix_part), :] = source_ref[
            pl.ds(mix_start, mix_part), :
        ].astype(BF16)
        return carry

    lax.fori_loop(0, CHUNKS, step, 0)


def lift_kernel(edges_ref, receiver_ref, nodes_ref, lift_ref, bias_ref, pre_ref):
    width = nodes_ref.shape[1]
    table = one_hot(receiver_ref[pl.ds(pl.program_id(0), 1), :], nodes_ref.shape[0])
    receivers = contract_rows(table, nodes_ref[...]).astype(BF16)
    pre_ref[0] = (
        matmul(edges_ref[0], lift_ref[:width])
        + matmul(receivers, lift_ref[2 * width :])
        + bias_ref[...]
    )


def by_live(count, slots, body):
    part = slots // 4
    for quarter in range(1, 5):
        low = (quarter - 1) * part if quarter > 1 else -1

        @pl.when((count > low) & (count <= quarter * part))
        def _(rows=quarter * part):
            body(rows)


def load_pieces(step, sources, held_ref, sems):
    copies, start = [], 0
    for place, source in enumerate(sources):
        size = source.shape[0]
        copies.append(
            (start, pltpu.make_async_copy(source, held_ref.at[pl.ds(start, size)], sems.at[place]))
        )
        start += size

    @pl.when(step == 0)
    def _():
        for _, copy in copies:
            copy.start()

    for first, copy in copies:

        @pl.when(step == first)
        def _(copy=copy):
            copy.wait()


def forward_kernel(pieces, first, last, *refs):
    refs = list(refs)
    take = lambda size: [refs.pop(0) for _ in range(size)]
    owner_ref, live_ref, order_ref, mine_ref = take(4)
    sources = take(pieces)
    pre_ref, receiver_ref, nodes_ref, lift_ref, mix_ref, gain_ref = take(6)
    if not first:
        take(4)
        (carried_ref,) = take(1)
    if last:
        seed_ref, node_lift_hbm, node_bias_ref, node_mix_hbm, node_gain_ref = take(5)
    hidden_ref, normed_ref, slope_ref, inverse_ref = take(4)
    if last:
        base_ref, summed_grad_ref, packed_ref, small_ref = take(4)
    else:
        (summed_ref,) = take(1)
    held_ref, sems = take(2)
    if last:
        summed_ref, total_ref, node_lift_ref, node_mix_ref, weight_sems = take(5)
    step = pl.program_id(0)
    count, width = nodes_ref.shape
    load_pieces(step, sources, held_ref, sems)
    if last:
        loads = [
            pltpu.make_async_copy(node_lift_hbm, node_lift_ref, weight_sems.at[0]),
            pltpu.make_async_copy(node_mix_hbm, node_mix_ref, weight_sems.at[1]),
        ]

    @pl.when(step == 0)
    def _():
        if last:
            for load in loads:
                load.start()
        summed_ref[...] = jnp.zeros_like(summed_ref) if first else carried_ref[...]

    owner = owner_ref[step]
    live_count = live_ref[owner]

    def body(rows):
        index = pick_row(held_ref[step, count:, :rows], mine_ref[0])
        senders = contract_rows(one_hot(index, count), held_ref[step, :count]).astype(BF16)
        pre = pre_ref[0, :rows] + matmul(senders, lift_ref[...])
        hidden, slope = silu_pair(pre)
        hidden = hidden.astype(BF16)
        normed, inverse = norm_forward(matmul(hidden, mix_ref[...]))
        hidden_ref[0, :rows] = hidden
        slope_ref[0, :rows] = slope.astype(BF16)
        normed_ref[0, :rows] = normed.astype(BF16)
        inverse_ref[0, :rows] = inverse
        live = live_rows(live_count, normed.shape)
        message = jnp.where(live, normed * gain_ref[...], 0.0).astype(BF16)
        summed_ref[...] += matmul(one_hot(receiver_ref[pl.ds(owner, 1), :][:, :rows], count), message)

    by_live(live_count, pre_ref.shape[1], body)

    if not last:
        return

    @pl.when(step == pl.num_programs(0) - 1)
    def _():
        for load in loads:
            load.wait()
        nodes = nodes_ref[...]
        summed = summed_ref[...].astype(BF16)
        pre_node = (
            matmul(nodes, node_lift_ref[:width])
            + matmul(summed, node_lift_ref[width:])
            + node_bias_ref[...]
        )
        hidden_node, slope_node = silu_pair(pre_node)
        hidden_node = hidden_node.astype(BF16)
        normed_node, inverse_node = norm_forward(matmul(hidden_node, node_mix_ref[...]))
        seed = seed_ref[...].astype(F32)
        small_ref[1:2, :] = jnp.sum(seed * normed_node, axis=0, keepdims=True)
        grad_out = norm_backward(seed * node_gain_ref[...], normed_node, inverse_node).astype(BF16)
        total_ref[2 * width :, :] = contract_rows(hidden_node, grad_out)
        grad_pre = (contract_features(grad_out, node_mix_ref[...]) * slope_node).astype(BF16)
        small_ref[0:1, :] = jnp.sum(grad_pre.astype(F32), axis=0, keepdims=True)
        total_ref[:width, :] = contract_rows(nodes, grad_pre)
        total_ref[width : 2 * width, :] = contract_rows(summed, grad_pre)
        base_ref[...] = seed + contract_features(grad_pre, node_lift_ref[:width])
        summed_grad_ref[...] = contract_features(grad_pre, node_lift_ref[width:]).astype(BF16)
        store_chunks(order_ref, total_ref, packed_ref, width)


def backward_kernel(pieces, *refs):
    owner_ref, live_ref, order_ref, mine_ref = refs[:4]
    sources = refs[4 : 4 + pieces]
    (
        edges_ref,
        seed_ref,
        receiver_ref,
        hidden_ref,
        normed_ref,
        slope_ref,
        inverse_ref,
        nodes_ref,
        base_ref,
        summed_grad_ref,
        lift_ref,
        mix_ref,
        gain_ref,
        grad_edges_ref,
        partial_ref,
        grad_nodes_ref,
        packed_ref,
        small_ref,
        received_ref,
        total_ref,
        held_ref,
        sems,
    ) = refs[4 + pieces :]
    step = pl.program_id(0)
    count, width = nodes_ref.shape
    slots = edges_ref.shape[1]
    owner = owner_ref[step]
    live_count = live_ref[owner]
    load_pieces(step, sources, held_ref, sems)

    @pl.when(step == 0)
    def _():
        received_ref[...] = jnp.zeros_like(received_ref)
        total_ref[...] = jnp.zeros_like(total_ref)
        small_ref[...] = jnp.zeros_like(small_ref)

    def body(rows):
        seed = seed_ref[0, :rows].astype(F32)
        live = live_rows(live_count, seed.shape)
        receiver_table = one_hot(receiver_ref[pl.ds(owner, 1), :][:, :rows], count)
        grad_message = jnp.where(
            live, seed + contract_rows(receiver_table, summed_grad_ref[...]), 0.0
        )
        normed = normed_ref[0, :rows].astype(F32)
        small_ref[1:2, :] += jnp.sum(grad_message * normed, axis=0, keepdims=True)
        grad_out = norm_backward(
            grad_message * gain_ref[...], normed, inverse_ref[0, :rows]
        ).astype(BF16)
        total_ref[3 * width :, :] += contract_rows(hidden_ref[0, :rows], grad_out)
        grad_pre = (
            contract_features(grad_out, mix_ref[...]) * slope_ref[0, :rows].astype(F32)
        ).astype(BF16)
        small_ref[0:1, :] += jnp.sum(grad_pre.astype(F32), axis=0, keepdims=True)
        total_ref[:width, :] += contract_rows(edges_ref[0, :rows], grad_pre)
        index = pick_row(held_ref[step, count:, :rows], mine_ref[0])
        sent = matmul(one_hot(index, count), grad_pre).astype(BF16)
        partial_ref[0, 0] = sent
        total_ref[width : 2 * width, :] += contract_rows(held_ref[step, :count], sent)
        received_ref[...] += matmul(receiver_table, grad_pre)
        grad_edges_ref[0, :rows] = jnp.where(
            live, seed + contract_features(grad_pre, lift_ref[:width]), 0.0
        ).astype(BF16)
        if rows < slots:
            grad_edges_ref[0, rows:] = jnp.zeros((slots - rows, width), BF16)

    by_live(live_count, slots, body)

    @pl.when(step == pl.num_programs(0) - 1)
    def _():
        received = received_ref[...].astype(BF16)
        total_ref[2 * width : 3 * width, :] = contract_rows(nodes_ref[...], received)
        grad_nodes_ref[...] = base_ref[...] + contract_features(received, lift_ref[2 * width :])
        store_chunks(order_ref, total_ref, packed_ref, width)


def unpack_kernel(scale, pieces, place, *refs):
    order_ref = refs[0]
    sources = refs[1 : 1 + pieces]
    targets = refs[-9:-5]
    buffers = refs[-5:-1]
    sems = refs[-1]
    parts = [target.shape[0] // CHUNKS for target in targets]
    copies, slot = [], 0
    for source in sources:
        for start in range(0, source.shape[0], sum(parts)):
            for kind, rows in enumerate(parts):
                held = buffers[kind].at[pl.ds(slot * rows, rows)]
                held[...] = source[start : start + rows, :].astype(F32) * scale[kind // 2]
                target = pl.multiple_of(order_ref[place + slot] * rows, 16)
                copies.append(
                    pltpu.make_async_copy(
                        held, targets[kind].at[pl.ds(target, rows)], sems.at[kind, slot]
                    )
                )
                copies[-1].start()
                start += rows
            slot += 1
    for copy in copies:
        copy.wait()


def swap(values, axis, bit):
    size = lax.axis_size(axis)
    return lax.ppermute(values, axis, [(i, i ^ bit) for i in range(size)])


def add_rounded(left, right):
    return (left.astype(F32) + right.astype(F32)).astype(BF16)


def exchange(*moves):
    values = lax.optimization_barrier(tuple(move[0] for move in moves))
    moved = [swap(value, axis, bit) for value, (_, axis, bit) in zip(values, moves)]
    return lax.optimization_barrier(tuple(moved))


def halves(part):
    rows = part.shape[0] // 2
    return part[:rows], part[rows:]


def join(*parts):
    return jnp.concatenate(parts)


def reduce_all(edge_packed, node_packed, partial, small):
    side_a, side_b = halves(node_packed)
    keep_a, send_a = halves(side_a)
    keep_b, send_b = halves(side_b)
    got_a, got_b = swap(send_a, "grp", 1), swap(send_b, "grp", 2)
    node_a, node_b = add_rounded(keep_a, got_a), add_rounded(keep_b, got_b)

    keep, send = halves(edge_packed)
    got, got_small = exchange((send, "dev", 1), (small, "dev", 1))
    edge_a, edge_b = halves(add_rounded(keep, got))
    small = small + got_small

    keep_a, send_a = halves(edge_a)
    keep_b, send_b = halves(edge_b)
    node_keep_a, node_send_a = halves(node_a)
    node_keep_b, node_send_b = halves(node_b)
    got_a, got_b, got_node, got_small, got_partial = exchange(
        (send_a, "grp", 1),
        (send_b, "grp", 2),
        (join(node_send_a, node_send_b), "dev", 1),
        (small, "grp", 1),
        (partial[1], "dev", 1),
    )
    owned = add_rounded(partial[0], got_partial)
    edge_a, edge_b = add_rounded(keep_a, got_a), add_rounded(keep_b, got_b)
    got_node_a, got_node_b = halves(got_node)
    node_a, node_b = add_rounded(node_keep_a, got_node_a), add_rounded(node_keep_b, got_node_b)
    small = small + got_small

    pairs = [halves(part) for part in (edge_a, node_a, edge_b, node_b)]
    got_a, got_b, got_small = exchange(
        (join(pairs[0][1], pairs[1][1]), "grp", 2),
        (join(pairs[2][1], pairs[3][1]), "grp", 1),
        (small, "grp", 2),
    )
    small = small + got_small
    edge_rows = pairs[0][0].shape[0]
    parts = [
        add_rounded(pairs[0][0], got_a[:edge_rows]),
        add_rounded(pairs[1][0], got_a[edge_rows:]),
        add_rounded(pairs[2][0], got_b[:edge_rows]),
        add_rounded(pairs[3][0], got_b[edge_rows:]),
    ]
    pairs = [halves(part) for part in parts]
    got, got_small = exchange((join(*[pair[1] for pair in pairs]), "dev", 2), (small, "dev", 2))
    kept = add_rounded(join(*[pair[0] for pair in pairs]), got)
    small = small + got_small
    got, got_small, got_owned = exchange(
        (kept, "dev", 4), (small, "dev", 4), (owned[1::2], "dev", 2)
    )
    owned = add_rounded(owned[::2], got_owned)
    kept = add_rounded(kept, got)
    small = small + got_small
    early_rows, late_rows = halves(owned[1])
    other, got_early = exchange((kept, "dev", 2), (early_rows, "dev", 4))

    (own_a, own_b), (other_a, other_b) = halves(kept), halves(other)
    side_a, side_b = join(own_a, other_a), join(own_b, other_b)
    got_a, got_b, got_late = exchange(
        (side_a, "grp", 2), (side_b, "grp", 1), (late_rows, "dev", 4)
    )
    from_senders = owned[0].astype(F32) + join(got_early, got_late).astype(F32)
    side_a, side_b = join(side_a, got_a), join(side_b, got_b)
    got_a, got_b, swapped_a, swapped_b = exchange(
        (side_a, "grp", 1),
        (side_b, "grp", 2),
        (side_a, "dev", 1),
        (side_b, "dev", 1),
    )
    last_a, last_b = exchange((got_a, "dev", 1), (got_b, "dev", 1))
    ordered = [[side_a, got_a, side_b, got_b], [swapped_a, last_a, swapped_b, last_b]]
    return ordered, small, from_senders


def device_bits():
    group = lax.axis_index("grp")
    device = lax.axis_index("dev")
    return group & 1, group >> 1, device & 1, (device >> 1) & 1


def relative_places(place):
    x, y, core, z = device_bits()
    first = core * 16 + x * 4 + y * 2 + z
    second = core * 16 + y * 4 + x * 2 + z
    return place ^ jnp.where((place & 8) == 0, first, second)


def edge_order():
    return relative_places(jnp.arange(CHUNKS, dtype=jnp.int32))


def node_order():
    place = jnp.arange(CHUNKS, dtype=jnp.int32)
    return relative_places(((place & 4) << 2) | ((place & 24) >> 1) | (place & 3))


def shape(*dims, kind=F32):
    return jax.ShapeDtypeStruct(dims, kind)


def params(mebibytes):
    return pltpu.CompilerParams(vmem_limit_bytes=mebibytes << 20)


def whole(*dims):
    return pl.BlockSpec(dims, lambda *_: (0,) * len(dims), pipeline_mode=pl.Buffered(1))


def result(*dims):
    return pl.BlockSpec(dims, lambda *_: (0,) * len(dims))


def per_device(
    node_latent,
    edge_latent,
    node_cotangent,
    edge_cotangent,
    edge_sender,
    edge_receiver,
    live_counts,
    edge_lift,
    edge_bias,
    edge_mix,
    edge_gain,
    node_lift,
    node_bias,
    node_mix,
    node_gain,
):
    width = node_latent.shape[2]
    nodes = node_latent[0]
    count = nodes.shape[0]
    peers = edge_receiver.shape[1]
    slots = edge_receiver.shape[2]
    total_rows = peers * slots
    unit = total_rows * width * width
    edges = edge_latent.reshape(peers, slots, width)
    edge_seed = edge_cotangent.reshape(peers, slots, width)
    receivers = edge_receiver.reshape(peers, slots)
    live = live_counts.reshape(peers)
    mine = lax.axis_index("dev")
    paired = lax.axis_size("dev") == 8 and lax.axis_size("grp") == 4
    packed_rows = count + -(-peers // 16) * 16
    packed_nodes = pl.pallas_call(
        pack_kernel,
        out_shape=shape(packed_rows, width, kind=BF16),
        compiler_params=params(4),
        name="pack",
    )(nodes, edge_sender)
    if paired:
        owners = jnp.arange(peers, dtype=jnp.int32) ^ mine
        edge_places = edge_order()
        node_places = node_order()
        near = swap(packed_nodes, "dev", 2)
        far = [swap(packed_nodes, "dev", 4), swap(packed_nodes, "dev", 6)]
        pieces = [packed_nodes, swap(packed_nodes, "dev", 1), near, swap(near, "dev", 1)]
        pieces = [piece[None] for piece in pieces]
        ranges = [(0, 4), (4, 8)]
    else:
        owners = jnp.arange(peers, dtype=jnp.int32)
        edge_places = node_places = jnp.arange(CHUNKS, dtype=jnp.int32)
        pieces = [lax.all_gather(packed_nodes, "dev")]
        ranges = [(0, peers)]
    gathered_rows = pieces[0].shape[1]

    anywhere = pl.BlockSpec(memory_space=pl.ANY)
    bias_row = edge_bias.reshape(1, width)
    gain_row = edge_gain.reshape(1, width)

    owned = pl.BlockSpec((1, slots, width), lambda i: (i, 0, 0))
    pre = pl.pallas_call(
        lift_kernel,
        grid=(peers,),
        in_specs=[
            owned,
            whole(peers, slots),
            whole(count, width),
            whole(3 * width, width),
            whole(1, width),
        ],
        out_specs=owned,
        out_shape=shape(peers, slots, width),
        compiler_params=params(12),
        cost_estimate=pl.CostEstimate(
            flops=5 * unit, bytes_accessed=6 * total_rows * width, transcendentals=0
        ),
        name="lift",
    )(edges, receivers, nodes, edge_lift, bias_row)

    def by_owner(*dims):
        return pl.BlockSpec(
            (1,) + dims, lambda i, owner, *_: (owner[i],) + (0,) * len(dims)
        )

    def by_step(*dims):
        return pl.BlockSpec((1,) + dims, lambda i, *_: (i,) + (0,) * len(dims))

    saved = []
    summed = None
    for begin, end in ranges:
        first, last = begin == 0, end == peers
        if not first:
            *far, summed = lax.optimization_barrier((*far, summed))
            for piece in far:
                pieces += [piece[None], swap(piece, "dev", 1)[None]]
        chosen = pieces[begin:] if paired else pieces

        def saved_step(*dims, begin=begin):
            return pl.BlockSpec((1,) + dims, lambda i, *_: (i + begin,) + (0,) * len(dims))

        operands = chosen + [
            pre,
            receivers,
            nodes,
            edge_lift,
            edge_mix,
            gain_row,
        ]
        in_specs = [anywhere] * len(chosen) + [
            by_owner(slots, width),
            whole(peers, slots),
            whole(count, width),
            pl.BlockSpec((width, width), lambda *_: (1, 0), pipeline_mode=pl.Buffered(1)),
            whole(width, width),
            whole(1, width),
        ]
        aliases = {}
        if not first:
            aliases = {4 + len(operands) + j: j for j in range(4)}
            operands += saved + [summed]
            in_specs += [anywhere] * 4 + [whole(count, width)]
        out_specs = [saved_step(slots, width)] * 3 + [saved_step(slots, 1)]
        out_shape = [shape(peers, slots, width, kind=BF16)] * 3 + [shape(peers, slots, 1)]
        scratch = [
            pltpu.VMEM((end - begin, gathered_rows, width), BF16),
            pltpu.SemaphoreType.DMA((len(chosen),)),
        ]
        if last:
            operands += [
                node_cotangent[0],
                node_lift,
                node_bias.reshape(1, width),
                node_mix,
                node_gain.reshape(1, width),
            ]
            in_specs += [whole(count, width), anywhere, whole(1, width), anywhere, whole(1, width)]
            out_specs += [
                result(count, width),
                result(count, width),
                result(3 * width, width),
                result(2, width),
            ]
            out_shape += [
                shape(count, width),
                shape(count, width, kind=BF16),
                shape(3 * width, width, kind=BF16),
                shape(2, width),
            ]
            scratch += [
                pltpu.VMEM((count, width), F32),
                pltpu.VMEM((3 * width, width), F32),
                pltpu.VMEM((2 * width, width), BF16),
                pltpu.VMEM((width, width), BF16),
                pltpu.SemaphoreType.DMA((2,)),
            ]
        else:
            out_specs.append(result(count, width))
            out_shape.append(shape(count, width))
        results = pl.pallas_call(
            functools.partial(forward_kernel, len(chosen), first, last),
            grid_spec=pltpu.PrefetchScalarGridSpec(
                num_scalar_prefetch=4,
                grid=(end - begin,),
                in_specs=in_specs,
                out_specs=out_specs,
                scratch_shapes=scratch,
            ),
            out_shape=out_shape,
            input_output_aliases=aliases,
            compiler_params=params(24),
            cost_estimate=pl.CostEstimate(
                flops=4 * unit,
                bytes_accessed=8 * total_rows * width,
                transcendentals=total_rows * width,
            ),
            name="forward_" + ("all" if last else "near"),
        )(owners[begin:end], live, node_places, mine.reshape(1), *operands)
        saved = list(results[:4])
        if last:
            base, summed_grad, node_packed, node_small = results[4:]
        else:
            summed = results[4]
    hidden, normed, slope, inverse = saved

    grad_edges, partial, grad_nodes, edge_packed, edge_small = pl.pallas_call(
        functools.partial(backward_kernel, len(pieces)),
        grid_spec=pltpu.PrefetchScalarGridSpec(
            num_scalar_prefetch=4,
            grid=(peers,),
            in_specs=[anywhere] * len(pieces)
            + [
                by_owner(slots, width),
                by_owner(slots, width),
                whole(peers, slots),
                by_step(slots, width),
                by_step(slots, width),
                by_step(slots, width),
                by_step(slots, 1),
                whole(count, width),
                whole(count, width),
                whole(count, width),
                whole(3 * width, width),
                whole(width, width),
                whole(1, width),
            ],
            out_specs=[
                by_owner(slots, width),
                pl.BlockSpec((1, 1, count, width), lambda i, *_: (i % 2, i // 2, 0, 0)),
                result(count, width),
                result(4 * width, width),
                result(2, width),
            ],
            scratch_shapes=[
                pltpu.VMEM((count, width), F32),
                pltpu.VMEM((4 * width, width), F32),
                pltpu.VMEM((peers, gathered_rows, width), BF16),
                pltpu.SemaphoreType.DMA((len(pieces),)),
            ],
        ),
        out_shape=[
            shape(peers, slots, width, kind=BF16),
            shape(2, peers // 2, count, width, kind=BF16),
            shape(count, width),
            shape(4 * width, width, kind=BF16),
            shape(2, width),
        ],
        compiler_params=params(28),
        cost_estimate=pl.CostEstimate(
            flops=14 * unit, bytes_accessed=20 * total_rows * width, transcendentals=0
        ),
        name="backward",
    )(
        owners,
        live,
        edge_places,
        mine.reshape(1),
        *pieces,
        edges,
        edge_seed,
        receivers,
        hidden,
        normed,
        slope,
        inverse,
        nodes,
        base,
        summed_grad,
        edge_lift,
        edge_mix,
        gain_row,
    )

    small = jnp.concatenate([edge_small, node_small])
    if paired:
        sources, small, from_senders = reduce_all(edge_packed, node_packed, partial, small)
    else:
        node_sum, edge_sum, small = lax.psum(
            (node_packed.astype(F32), edge_packed.astype(F32), small), ("grp", "dev")
        )
        interleaved = jnp.concatenate(
            [
                edge_sum.reshape(CHUNKS, 4 * width // CHUNKS, width),
                node_sum.reshape(CHUNKS, 3 * width // CHUNKS, width),
            ],
            axis=1,
        )
        sources = [[interleaved.reshape(7 * width, width).astype(BF16)]]
        ordered = jnp.swapaxes(partial, 0, 1).reshape(peers, count, width)
        from_senders = lax.psum_scatter(ordered.astype(F32), "dev", scatter_dimension=0)
    grad_nodes = grad_nodes + contract_features(
        from_senders.astype(BF16), edge_lift[width : 2 * width]
    )
    groups = lax.axis_size("grp") * lax.axis_size("dev")
    edge_scale = float(total_rows * groups) ** (-0.5)
    node_scale = float(count * groups) ** (-0.5)
    totals = [3 * width, width, 2 * width, width]
    unpacked, place = [], 0
    for part in sources:
        places = sum(source.shape[0] for source in part) * CHUNKS // (7 * width)
        unpacked = pl.pallas_call(
            functools.partial(unpack_kernel, (edge_scale, node_scale), len(part), place),
            grid_spec=pltpu.PrefetchScalarGridSpec(
                num_scalar_prefetch=1,
                grid=(1,),
                in_specs=[whole(*source.shape) for source in part] + [anywhere] * len(unpacked),
                out_specs=[anywhere] * 4,
                scratch_shapes=[
                    pltpu.VMEM((places * total // CHUNKS, width), F32) for total in totals
                ]
                + [pltpu.SemaphoreType.DMA((4, places))],
            ),
            out_shape=[shape(total, width) for total in totals],
            input_output_aliases={1 + len(part) + j: j for j in range(len(unpacked))},
            compiler_params=params(20),
            cost_estimate=pl.CostEstimate(
                flops=0, bytes_accessed=42 * places * width * width // CHUNKS, transcendentals=0
            ),
            name="unpack_%d" % place,
        )(edge_places, *part, *unpacked)
        place += places
    edge_lift_grad, edge_mix_grad, node_lift_grad, node_mix_grad = unpacked
    return (
        grad_nodes[None],
        grad_edges.reshape(1, 1, peers, slots, width),
        edge_lift_grad,
        small[0] * edge_scale,
        edge_mix_grad,
        small[1] * edge_scale,
        node_lift_grad,
        small[2] * node_scale,
        node_mix_grad,
        small[3] * node_scale,
    )


def solution(mesh):
    return jax.shard_map(
        per_device,
        mesh=mesh,
        in_specs=(
            P("grp", "dev", None),
            P("grp", "dev", None, None, None),
            P("grp", "dev", None),
            P("grp", "dev", None, None, None),
            P(None, "dev", None),
            P("dev", None, None),
            P("dev", None),
            P(),
            P(),
            P(),
            P(),
            P(),
            P(),
            P(),
            P(),
        ),
        out_specs=(
            P("grp", "dev", None),
            P("grp", "dev", None, None, None),
            P(),
            P(),
            P(),
            P(),
            P(),
            P(),
            P(),
            P(),
        ),
        check_vma=False,
    )
```

time: 371 us -> 152 us (0.41)
  blocking collectives: 84.2 us -> 0 us
  waiting for transfers between devices: 131 us -> 65.3 us
  local copies, waits for them, and re-layouts: 55.5 us -> 7.53 us
  matrix products: 42.5 us -> 0.35 us
  Pallas kernels: 0 us -> 39.6 us
  other arithmetic: 31.9 us -> 3.14 us
  starting transfers between devices: 10.9 us -> 34.8 us
  between operations: 14.5 us -> 1.36 us
    psum x1 -> x0, waiting for transfers between devices: 99.6 us -> none  [per_device(): lax.psum((edge_lift_grad, edge_bias_grad, edge_mix_grad, edge_gain_grad,...]
    psum x1 -> x0, blocking collectives: 84.2 us -> none  [per_device(): lax.psum((edge_lift_grad, edge_bias_grad, edge_mix_grad, edge_gain_grad,...]
    ppermute x0 -> x35, waiting for transfers between devices: none -> 65.3 us  [swap(): return lax.ppermute(values, axis, [(i, i ^ bit) for i in range(size)])]
    pallas_call x0 -> x7, Pallas kernels: none -> 39.6 us  [the longest x1 16.3 us: per_device(): pl.pallas_call(functools.partial(backward_kernel, len(pieces)), grid_spec...]
    ppermute x0 -> x35, starting transfers between devices: none -> 34.8 us  [swap(): return lax.ppermute(values, axis, [(i, i ^ bit) for i in range(size)])]
    gather x4 -> x0, local copies, waits for them, and re-layouts: 33.8 us -> none  [the longest x2 14.4 us: per_device(): jnp.take(grad_joined[:, width:], receiver_index, axis=0)]
    dot_general x15 -> x0, matrix products: 33.3 us -> none  [the longest x8 19 us: matmul(): return jnp.dot(left, right, preferred_element_type=jnp.float32)]
    all_to_all x2 -> x0, waiting for transfers between devices: 31.2 us -> none  [the longest x1 31.2 us: per_device(): lax.all_to_all(outgoing, 'dev', split_axis=0, concat_axis=0, tiled=True)]
  transfers between devices with their start and end apart: 3 -> 35, of which waited for: 2 -> 19; matrix products, arithmetic and copies ran while one was open for 13% -> 2% of each run, Pallas kernels for 0% -> 8%
where the time goes in v2:
time: 152 us
  waiting for transfers between devices  65.3 us (43%)
  Pallas kernels  39.6 us (26%)
  starting transfers between devices  34.8 us (23%)
  local copies, waits for them, and re-layouts  7.53 us (5%)
  other arithmetic  3.14 us (2%)
    ppermute x35, waiting for transfers between devices, swap(): return lax.ppermute(values, axis, [(i, i ^ bit) for i in range(size)])  65.3 us
    ppermute x35, starting transfers between devices, swap(): return lax.ppermute(values, axis, [(i, i ^ bit) for i in range(size)])  34.8 us
    pallas_call x1, Pallas kernels, per_device(): pl.pallas_call(functools.partial(backward_kernel, len(pieces)), grid_spec...  16.3 us
    pallas_call x2, Pallas kernels, per_device(): pl.pallas_call(functools.partial(forward_kernel, len(chosen), first, last...  12.6 us
    unnamed x40, local copies, waits for them, and re-layouts  7.04 us
    pallas_call x2, Pallas kernels, per_device(): pl.pallas_call(functools.partial(unpack_kernel, (edge_scale, node_scale),...  5.83 us
    pallas_call x1, Pallas kernels, per_device(): pl.pallas_call(lift_kernel, grid=(peers,), in_specs=[owned, whole(peers,...  4.84 us
  transfers between devices with their start and end apart: 35, of which 19 were waited for; matrix products, arithmetic and copies ran while one was open for 2% of the time, Pallas kernels for 8%

profile of v2, /device:TPU:0, one launch (start us, length us, event | category | flops | bytes accessed | tf_op | source)
XLA Modules:
  0.0 152.1 jit_solution(7364255754266457677)
XLA Ops:
  2.3 5.1 %collective-permute-start.4 = (bf16[272,512]{1,0:T(8,128)(2,1)S(1)}, bf16[272,512]{1,0:T(8,128)(2,1)S(1)}, u32[]{:S(2)}, u32[]{:S(2)}) collective-permute-start(bf16[272,512]{1,0:T(8,128)(2,1)S(1)} %pack.1), channel_id=1, source_target_pairs={{0,6},{1,7},{2,4},{3,5},{4,2},{5,3},{6,0},{7,1},{8,14},{9,15},{10,... | collective-permute-start | bytes 835592 | tf_op jit(solution)/shard_map/ppermute | solution.py:324
  13.5 4.8 %lift.1.refs_8_ = f32[8,256,512]{2,1,0:T(8,128)S(1)} custom-call(bf16[8,256,512]{2,1,0:T(8,128)(2,1)S(1)} %bitcast.69, s32[8,256]{1,0:T(8,128)S(1)} %bitcast.57, bf16[256,512]{1,0:T(8,128)(2,1)S(1)} %bitcast.42, bf16[1536,512]{1,0:T(8,128)(2,1)S(1)} %copy-done, f32[1,512]{1,0:T(1,128)S(1)} %bitcast.78), custom_call_target="tpu_custom_call" | custom-call | flops 2684354560 | bytes 6291456 | tf_op jit(solution)/shard_map/lift/pallas_call | solution.py:516
  18.3 7.1 %collective-permute-done.1 = bf16[272,512]{1,0:T(8,128)(2,1)S(1)} collective-permute-done((bf16[272,512]{1,0:T(8,128)(2,1)S(1)}, bf16[272,512]{1,0:T(8,128)(2,1)S(1)}, u32[]{:S(2)}, u32[]{:S(2)}) %collective-permute-start.1) | collective-permute-done | bytes 278560 | tf_op jit(solution)/shard_map/ppermute | solution.py:324
  27.0 5.1 %forward_near.1 = (bf16[8,256,512]{2,1,0:T(8,128)(2,1)S(1)}, bf16[8,256,512]{2,1,0:T(8,128)(2,1)S(1)}, bf16[8,256,512]{2,1,0:T(8,128)(2,1)S(1)}, f32[8,256,1]{2,1,0:T(8,128)S(1)}, f32[256,512]{1,0:T(8,128)S(1)}) custom-call(s32[4]{0:T(128)S(1)} %get-tuple-element.201.refs_0_, s32[8]{0:T(128)S(1)} %bitcast.66, s32[32]{0:T(128)S(1)} %fusion.13.refs_2_, ...), custom_call_target="tpu_custom_call" | custom-call | flops 2147483648 | bytes 8388608 | tf_op jit(solution)/shard_map/forward_near/pallas_call | solution.py:614
  34.6 7.5 %forward_all.1 = (bf16[8,256,512]{2,1,0:T(8,128)(2,1)S(1)}, bf16[8,256,512]{2,1,0:T(8,128)(2,1)S(1)}, bf16[8,256,512]{2,1,0:T(8,128)(2,1)S(1)}, f32[8,256,1]{2,1...) custom-call(s32[4]{0:T(128)S(1)} %get-tuple-element.200.refs_0_, ...), custom_call_target="tpu_custom_call", output_to_operand_aliasing={{0}: (14, {}), {1}: (15, {}), {2}: (16, {}), {3}: (17, {})} | custom-call | flops 2147483648 | bytes 8388608 | tf_op jit(solution)/shard_map/forward_all/pallas_call | solution.py:614
  42.2 16.3 %backward.1 = (bf16[8,256,512]{2,1,0:T(8,128)(2,1)}, bf16[2,4,256,512]{3,2,1,0:T(8,128)(2,1)S(1)}, f32[256,512]{1,0:T(8,128)S(1)}, bf16[2048,512]{1,0:T(8,128)(2,1)S(1)}, f32[2,512]{1,0:T(2,128)S(1)}) custom-call(s32[8]{0:T(128)S(1)} %iota_xor_fusion.refs_0_, s32[8]{0:T(128)S(1)} %bitcast.68, s32[32]{0:T(128)S(1)} %fusion.12.refs_2_.refs_0_, ...), custom_call_target="tpu_custom_call" | custom-call | flops 7516192768 | bytes 20971520 | tf_op jit(solution)/shard_map/backward/pallas_call | solution.py:640
  63.2 7.9 %collective-permute-done.9 = bf16[384,512]{1,0:T(8,128)(2,1)S(1)} collective-permute-done((bf16[384,512]{1,0:T(8,128)(2,1)S(1)}, bf16[384,512]{1,0:T(8,128)(2,1)S(1)}, u32[]{:S(2)}, u32[]{:S(2)}) %collective-permute-start.9) | collective-permute-done | bytes 393248 | tf_op jit(solution)/shard_map/ppermute | solution.py:324
  77.2 4.9 %collective-permute-done.14 = f32[4,512]{1,0:T(4,128)S(1)} collective-permute-done((f32[4,512]{1,0:T(4,128)S(1)}, f32[4,512]{1,0:T(4,128)S(1)}, u32[]{:S(2)}, u32[]{:S(2)}) %collective-permute-start.14) | collective-permute-done | bytes 8224 | tf_op jit(solution)/shard_map/ppermute | solution.py:324
  82.6 1.6 %collective-permute-start.16 = (bf16[224,512]{1,0:T(8,128)(2,1)S(1)}, bf16[224,512]{1,0:T(8,128)(2,1)S(1)}, u32[]{:S(2)}, u32[]{:S(2)}) collective-permute-start(bf16[224,512]{1,0:T(8,128)(2,1)S(1)} %pad_maximum_fusion.3), channel_id=1, source_target_pairs={{0,16},{8,24},{16,0},{24,8},{1,17},{9,25},{17,1},{25,9},{2,18},{10... | collective-permute-start | bytes 688136 | tf_op jit(solution)/shard_map/ppermute | solution.py:324
  86.2 3.3 %collective-permute-done.18 = f32[4,512]{1,0:T(4,128)S(1)} collective-permute-done((f32[4,512]{1,0:T(4,128)S(1)}, f32[4,512]{1,0:T(4,128)S(1)}, u32[]{:S(2)}, u32[]{:S(2)}) %collective-permute-start.18) | collective-permute-done | bytes 8224 | tf_op jit(solution)/shard_map/ppermute | solution.py:324
  90.8 2.6 %collective-permute-start.20 = (f32[4,512]{1,0:T(4,128)S(1)}, f32[4,512]{1,0:T(4,128)S(1)}, u32[]{:S(2)}, u32[]{:S(2)}) collective-permute-start(f32[4,512]{1,0:T(4,128)S(1)} %add.110), channel_id=1, source_target_pairs={{0,2},{1,3},{2,0},{3,1},{4,6},{5,7},{6,4},{7,5},{8,10},{9,11},{10,... | collective-permute-start | bytes 24584 | tf_op jit(solution)/shard_map/ppermute | solution.py:324
  95.1 7.4 %collective-permute-done.19 = bf16[224,512]{1,0:T(8,128)(2,1)S(1)} collective-permute-done((bf16[224,512]{1,0:T(8,128)(2,1)S(1)}, bf16[224,512]{1,0:T(8,128)(2,1)S(1)}, u32[]{:S(2)}, u32[]{:S(2)}) %collective-permute-start.19) | collective-permute-done | bytes 229408 | tf_op jit(solution)/shard_map/ppermute | solution.py:324
  102.8 2.9 %collective-permute-start.22 = (f32[4,512]{1,0:T(4,128)S(1)}, f32[4,512]{1,0:T(4,128)S(1)}, u32[]{:S(2)}, u32[]{:S(2)}) collective-permute-start(f32[4,512]{1,0:T(4,128)S(1)} %add.112), channel_id=1, source_target_pairs={{0,4},{1,5},{2,6},{3,7},{4,0},{5,1},{6,2},{7,3},{8,12},{9,13},{10,... | collective-permute-start | bytes 24584 | tf_op jit(solution)/shard_map/ppermute | solution.py:324
  105.7 8.1 %collective-permute-done.22 = f32[4,512]{1,0:T(4,128)S(1)} collective-permute-done((f32[4,512]{1,0:T(4,128)S(1)}, f32[4,512]{1,0:T(4,128)S(1)}, u32[]{:S(2)}, u32[]{:S(2)}) %collective-permute-start.22) | collective-permute-done | bytes 8224 | tf_op jit(solution)/shard_map/ppermute | solution.py:324
  113.8 2.5 %collective-permute-done.23 = bf16[2,256,512]{2,1,0:T(8,128)(2,1)S(1)} collective-permute-done((bf16[2,256,512]{2,1,0:T(8,128)(2,1)S(1)}, bf16[2,256,512]{2,1,0:T(8,128)(2,1)S(1)}, u32[]{:S(2)}, u32[]{:S(2)}) %collective-permute-start.23) | collective-permute-done | bytes 524320 | tf_op jit(solution)/shard_map/ppermute | solution.py:324
  117.5 5.3 %collective-permute-done.25 = bf16[128,512]{1,0:T(8,128)(2,1)S(1)} collective-permute-done((bf16[128,512]{1,0:T(8,128)(2,1)S(1)}, bf16[128,512]{1,0:T(8,128)(2,1)S(1)}, u32[]{:S(2)}, u32[]{:S(2)}) %collective-permute-start.25) | collective-permute-done | bytes 131104 | tf_op jit(solution)/shard_map/ppermute | solution.py:324
  122.7 2.1 %collective-permute-done.24 = bf16[224,512]{1,0:T(8,128)(2,1)S(1)} collective-permute-done((bf16[224,512]{1,0:T(8,128)(2,1)S(1)}, bf16[224,512]{1,0:T(8,128)(2,1)S(1)}, u32[]{:S(2)}, u32[]{:S(2)}) %collective-permute-start.24) | collective-permute-done | bytes 229408 | tf_op jit(solution)/shard_map/ppermute | solution.py:324
  125.6 2.0 %collective-permute-start.27 = (bf16[224,512]{1,0:T(8,128)(2,1)S(1)}, bf16[224,512]{1,0:T(8,128)(2,1)S(1)}, u32[]{:S(2)}, u32[]{:S(2)}) collective-permute-start(bf16[224,512]{1,0:T(8,128)(2,1)S(1)} %pad_maximum_fusion.7), channel_id=1, source_target_pairs={{0,8},{8,0},{16,24},{24,16},{1,9},{9,1},{17,25},{25,17},{2,10},{10... | collective-permute-start | bytes 688136 | tf_op jit(solution)/shard_map/ppermute | solution.py:324
  127.6 2.0 %collective-permute-start.28 = (bf16[128,512]{1,0:T(8,128)(2,1)S(1)}, bf16[128,512]{1,0:T(8,128)(2,1)S(1)}, u32[]{:S(2)}, u32[]{:S(2)}) collective-permute-start(bf16[128,512]{1,0:T(8,128)(2,1)S(1)} %get-tuple-element.146), channel_id=1, source_target_pairs={{0,4},{1,5},{2,6},{3,7},{4,0},{5,1},{6,2},{7,3},{8,12},{9,13},{10,... | collective-permute-start | bytes 393224 | tf_op jit(solution)/shard_map/ppermute | solution.py:324
  129.6 4.7 %collective-permute-done.28 = bf16[128,512]{1,0:T(8,128)(2,1)S(1)} collective-permute-done((bf16[128,512]{1,0:T(8,128)(2,1)S(1)}, bf16[128,512]{1,0:T(8,128)(2,1)S(1)}, u32[]{:S(2)}, u32[]{:S(2)}) %collective-permute-start.28) | collective-permute-done | bytes 131104 | tf_op jit(solution)/shard_map/ppermute | solution.py:324
  134.8 3.1 %collective-permute-start.30 = (bf16[448,512]{1,0:T(8,128)(2,1)S(1)}, bf16[448,512]{1,0:T(8,128)(2,1)S(1)}, u32[]{:S(2)}, u32[]{:S(2)}) collective-permute-start(bf16[448,512]{1,0:T(8,128)(2,1)S(1)} %pad_maximum_fusion.1.refs_3_), channel_id=1, source_target_pairs={{0,16},{8,24},{16,0},{24,8},{1,17},{9,25},{17,1},{25,9},{2,18},{10... | collective-permute-start | bytes 1376264 | tf_op jit(solution)/shard_map/ppermute | solution.py:324
  139.0 3.9 %collective-permute-done.29.refs_2_ = bf16[448,512]{1,0:T(8,128)(2,1)S(1)} collective-permute-done((bf16[448,512]{1,0:T(8,128)(2,1)S(1)}, bf16[448,512]{1,0:T(8,128)(2,1)S(1)}, u32[]{:S(2)}, u32[]{:S(2)}) %collective-permute-start.29) | collective-permute-done | bytes 458784 | tf_op jit(solution)/shard_map/ppermute | solution.py:324
  146.1 2.9 %unpack_0.1 = (f32[1536,512]{1,0:T(8,128)}, f32[512,512]{1,0:T(8,128)}, f32[1024,512]{1,0:T(8,128)}, f32[512,512]{1,0:T(8,128)}) custom-call(s32[32]{0:T(128)S(1)} %fusion.12.refs_2_.refs_0_, bf16[448,512]{1,0:T(8,128)(2,1)S(1)} %pad_maximum_fusion.refs_1_, bf16[448,512]{1,0:T(8,128)(2,1)S(1)} %collective-permute-done.29.refs_2_, ...), custom_call_target="tpu_custom_call" | custom-call | bytes 5505024 | tf_op jit(solution)/shard_map/unpack_0/pallas_call | solution.py:735
  149.0 2.9 %unpack_16.1 = (f32[1536,512]{1,0:T(8,128)}, f32[512,512]{1,0:T(8,128)}, f32[1024,512]{1,0:T(8,128)}, f32[512,512]{1,0:T(8,128)}) custom-call(s32[32]{0:T(128)S(1)} %fusion.12.refs_2_.refs_0_, bf16[448,512]{1,0:T(8,128)(2,1)S(1)} %collective-permute-done.31.refs_1_, ...), custom_call_target="tpu_custom_call", output_to_operand_aliasing={{0}: (5, {}), {1}: (6, {}), {2}: (7, {}), {3}: (8, {})} | custom-call | bytes 5505024 | tf_op jit(solution)/shard_map/unpack_16/pallas_call | solution.py:735
  (142 shorter events, 34.7 us)
Async XLA Ops:
  2.3 29.8 %collective-permute-start.4 = (bf16[272,512]{1,0:T(8,128)(2,1)S(1)}, bf16[272,512]{1,0:T(8,128)(2,1)S(1)}, u32[]{:S(2)}, u32[]{:S(2)}) collective-permute-start(bf16[272,512]{1,0:T(8,128)(2,1)S(1)} %pack.1), channel_id=1, source_target_pairs={{0,6},{1,7},{2,4},{3,5},{4,2},{5,3},{6,0},{7,1},{8,14},{9,15},{10,... | collective-permute-start | bytes 835592 | tf_op jit(solution)/shard_map/ppermute | solution.py:324
  7.4 24.7 %collective-permute-start.3 = (bf16[272,512]{1,0:T(8,128)(2,1)S(1)}, bf16[272,512]{1,0:T(8,128)(2,1)S(1)}, u32[]{:S(2)}, u32[]{:S(2)}) collective-permute-start(bf16[272,512]{1,0:T(8,128)(2,1)S(1)} %pack.1), channel_id=1, source_target_pairs={{0,4},{1,5},{2,6},{3,7},{4,0},{5,1},{6,2},{7,3},{8,12},{9,13},{10,... | collective-permute-start | bytes 835592 | tf_op jit(solution)/shard_map/ppermute | solution.py:324
  7.4 17.9 %collective-permute-start.1 = (bf16[272,512]{1,0:T(8,128)(2,1)S(1)}, bf16[272,512]{1,0:T(8,128)(2,1)S(1)}, u32[]{:S(2)}, u32[]{:S(2)}) collective-permute-start(bf16[272,512]{1,0:T(8,128)(2,1)S(1)} %pack.1), channel_id=1, source_target_pairs={{0,2},{1,3},{2,0},{3,1},{4,6},{5,7},{6,4},{7,5},{8,10},{9,11},{10,... | collective-permute-start | bytes 835592 | tf_op jit(solution)/shard_map/ppermute | solution.py:324
  8.1 17.4 %collective-permute-start = (bf16[272,512]{1,0:T(8,128)(2,1)S(1)}, bf16[272,512]{1,0:T(8,128)(2,1)S(1)}, u32[]{:S(2)}, u32[]{:S(2)}) collective-permute-start(bf16[272,512]{1,0:T(8,128)(2,1)S(1)} %pack.1), channel_id=1, source_target_pairs={{0,1},{1,0},{2,3},{3,2},{4,5},{5,4},{6,7},{7,6},{8,9},{9,8},{10,11... | collective-permute-start | bytes 835592 | tf_op jit(solution)/shard_map/ppermute | solution.py:324
  58.6 14.1 %collective-permute-start.7 = (bf16[1024,512]{1,0:T(8,128)(2,1)S(1)}, bf16[1024,512]{1,0:T(8,128)(2,1)S(1)}, u32[]{:S(2)}, u32[]{:S(2)}) collective-permute-start(bf16[1024,512]{1,0:T(8,128)(2,1)S(1)} %slice.187), channel_id=1, source_target_pairs={{0,1},{1,0},{2,3},{3,2},{4,5},{5,4},{6,7},{7,6},{8,9},{9,8},{10,11... | collective-permute-start | bytes 3145736 | tf_op jit(solution)/shard_map/ppermute | solution.py:324
  60.1 11.1 %collective-permute-start.9 = (bf16[384,512]{1,0:T(8,128)(2,1)S(1)}, bf16[384,512]{1,0:T(8,128)(2,1)S(1)}, u32[]{:S(2)}, u32[]{:S(2)}) collective-permute-start(bf16[384,512]{1,0:T(8,128)(2,1)S(1)} %get-tuple-element.174), channel_id=1, source_target_pairs={{0,8},{8,0},{16,24},{24,16},{1,9},{9,1},{17,25},{25,17},{2,10},{10... | collective-permute-start | bytes 1179656 | tf_op jit(solution)/shard_map/ppermute | solution.py:324
  61.6 10.8 %collective-permute-start.10 = (bf16[384,512]{1,0:T(8,128)(2,1)S(1)}, bf16[384,512]{1,0:T(8,128)(2,1)S(1)}, u32[]{:S(2)}, u32[]{:S(2)}) collective-permute-start(bf16[384,512]{1,0:T(8,128)(2,1)S(1)} %get-tuple-element.175), channel_id=1, source_target_pairs={{0,16},{8,24},{16,0},{24,8},{1,17},{9,25},{17,1},{25,9},{2,18},{10... | collective-permute-start | bytes 1179656 | tf_op jit(solution)/shard_map/ppermute | solution.py:324
  63.1 9.5 %collective-permute-start.8 = (f32[4,512]{1,0:T(4,128)S(1)}, f32[4,512]{1,0:T(4,128)S(1)}, u32[]{:S(2)}, u32[]{:S(2)}) collective-permute-start(f32[4,512]{1,0:T(4,128)S(1)} %pad_maximum_fusion.8), channel_id=1, source_target_pairs={{0,1},{1,0},{2,3},{3,2},{4,5},{5,4},{6,7},{7,6},{8,9},{9,8},{10,11... | collective-permute-start | bytes 24584 | tf_op jit(solution)/shard_map/ppermute | solution.py:324
  73.1 9.1 %collective-permute-start.15 = (bf16[4,256,512]{2,1,0:T(8,128)(2,1)S(1)}, bf16[4,256,512]{2,1,0:T(8,128)(2,1)S(1)}, u32[]{:S(2)}, u32[]{:S(2)}) collective-permute-start(bf16[4,256,512]{2,1,0:T(8,128)(2,1)S(1)} %slice_bitcast_fusion), channel_id=1, source_target_pairs={{0,1},{1,0},{2,3},{3,2},{4,5},{5,4},{6,7},{7,6},{8,9},{9,8},{10,11... | collective-permute-start | bytes 3145736 | tf_op jit(solution)/shard_map/ppermute | solution.py:324
  73.1 9.0 %collective-permute-start.13 = (bf16[384,512]{1,0:T(8,128)(2,1)S(1)}, bf16[384,512]{1,0:T(8,128)(2,1)S(1)}, u32[]{:S(2)}, u32[]{:S(2)}) collective-permute-start(bf16[384,512]{1,0:T(8,128)(2,1)S(1)} %pad_maximum_fusion.2), channel_id=1, source_target_pairs={{0,1},{1,0},{2,3},{3,2},{4,5},{5,4},{6,7},{7,6},{8,9},{9,8},{10,11... | collective-permute-start | bytes 1179656 | tf_op jit(solution)/shard_map/ppermute | solution.py:324
  73.6 8.5 %collective-permute-start.11 = (bf16[256,512]{1,0:T(8,128)(2,1)S(1)}, bf16[256,512]{1,0:T(8,128)(2,1)S(1)}, u32[]{:S(2)}, u32[]{:S(2)}) collective-permute-start(bf16[256,512]{1,0:T(8,128)(2,1)S(1)} %get-tuple-element.115), channel_id=1, source_target_pairs={{0,8},{8,0},{16,24},{24,16},{1,9},{9,1},{17,25},{25,17},{2,10},{10... | collective-permute-start | bytes 786440 | tf_op jit(solution)/shard_map/ppermute | solution.py:324
  74.2 8.0 %collective-permute-start.12 = (bf16[256,512]{1,0:T(8,128)(2,1)S(1)}, bf16[256,512]{1,0:T(8,128)(2,1)S(1)}, u32[]{:S(2)}, u32[]{:S(2)}) collective-permute-start(bf16[256,512]{1,0:T(8,128)(2,1)S(1)} %get-tuple-element.116), channel_id=1, source_target_pairs={{0,16},{8,24},{16,0},{24,8},{1,17},{9,25},{17,1},{25,9},{2,18},{10... | collective-permute-start | bytes 786440 | tf_op jit(solution)/shard_map/ppermute | solution.py:324
  82.6 6.9 %collective-permute-start.16 = (bf16[224,512]{1,0:T(8,128)(2,1)S(1)}, bf16[224,512]{1,0:T(8,128)(2,1)S(1)}, u32[]{:S(2)}, u32[]{:S(2)}) collective-permute-start(bf16[224,512]{1,0:T(8,128)(2,1)S(1)} %pad_maximum_fusion.3), channel_id=1, source_target_pairs={{0,16},{8,24},{16,0},{24,8},{1,17},{9,25},{17,1},{25,9},{2,18},{10... | collective-permute-start | bytes 688136 | tf_op jit(solution)/shard_map/ppermute | solution.py:324
  93.4 9.2 %collective-permute-start.19 = (bf16[224,512]{1,0:T(8,128)(2,1)S(1)}, bf16[224,512]{1,0:T(8,128)(2,1)S(1)}, u32[]{:S(2)}, u32[]{:S(2)}) collective-permute-start(bf16[224,512]{1,0:T(8,128)(2,1)S(1)} %pad_maximum_fusion.5), channel_id=1, source_target_pairs={{0,2},{1,3},{2,0},{3,1},{4,6},{5,7},{6,4},{7,5},{8,10},{9,11},{10,... | collective-permute-start | bytes 688136 | tf_op jit(solution)/shard_map/ppermute | solution.py:324
  102.6 13.6 %collective-permute-start.23 = (bf16[2,256,512]{2,1,0:T(8,128)(2,1)S(1)}, bf16[2,256,512]{2,1,0:T(8,128)(2,1)S(1)}, u32[]{:S(2)}, u32[]{:S(2)}) collective-permute-start(bf16[2,256,512]{2,1,0:T(8,128)(2,1)S(1)} %slice.224), channel_id=1, source_target_pairs={{0,2},{1,3},{2,0},{3,1},{4,6},{5,7},{6,4},{7,5},{8,10},{9,11},{10,... | collective-permute-start | bytes 1572872 | tf_op jit(solution)/shard_map/ppermute | solution.py:324
  102.7 11.1 %collective-permute-start.21 = (bf16[224,512]{1,0:T(8,128)(2,1)S(1)}, bf16[224,512]{1,0:T(8,128)(2,1)S(1)}, u32[]{:S(2)}, u32[]{:S(2)}) collective-permute-start(bf16[224,512]{1,0:T(8,128)(2,1)S(1)} %add_convert_fusion.7), channel_id=1, source_target_pairs={{0,4},{1,5},{2,6},{3,7},{4,0},{5,1},{6,2},{7,3},{8,12},{9,13},{10,... | collective-permute-start | bytes 688136 | tf_op jit(solution)/shard_map/ppermute | solution.py:324
  102.8 11.0 %collective-permute-start.22 = (f32[4,512]{1,0:T(4,128)S(1)}, f32[4,512]{1,0:T(4,128)S(1)}, u32[]{:S(2)}, u32[]{:S(2)}) collective-permute-start(f32[4,512]{1,0:T(4,128)S(1)} %add.112), channel_id=1, source_target_pairs={{0,4},{1,5},{2,6},{3,7},{4,0},{5,1},{6,2},{7,3},{8,12},{9,13},{10,... | collective-permute-start | bytes 24584 | tf_op jit(solution)/shard_map/ppermute | solution.py:324
  117.5 7.4 %collective-permute-start.24 = (bf16[224,512]{1,0:T(8,128)(2,1)S(1)}, bf16[224,512]{1,0:T(8,128)(2,1)S(1)}, u32[]{:S(2)}, u32[]{:S(2)}) collective-permute-start(bf16[224,512]{1,0:T(8,128)(2,1)S(1)} %add_convert_fusion.6), channel_id=1, source_target_pairs={{0,2},{1,3},{2,0},{3,1},{4,6},{5,7},{6,4},{7,5},{8,10},{9,11},{10,... | collective-permute-start | bytes 688136 | tf_op jit(solution)/shard_map/ppermute | solution.py:324
  125.0 9.3 %collective-permute-start.26 = (bf16[224,512]{1,0:T(8,128)(2,1)S(1)}, bf16[224,512]{1,0:T(8,128)(2,1)S(1)}, u32[]{:S(2)}, u32[]{:S(2)}) collective-permute-start(bf16[224,512]{1,0:T(8,128)(2,1)S(1)} %pad_maximum_fusion.6), channel_id=1, source_target_pairs={{0,16},{8,24},{16,0},{24,8},{1,17},{9,25},{17,1},{25,9},{2,18},{10... | collective-permute-start | bytes 688136 | tf_op jit(solution)/shard_map/ppermute | solution.py:324
  125.6 8.6 %collective-permute-start.27 = (bf16[224,512]{1,0:T(8,128)(2,1)S(1)}, bf16[224,512]{1,0:T(8,128)(2,1)S(1)}, u32[]{:S(2)}, u32[]{:S(2)}) collective-permute-start(bf16[224,512]{1,0:T(8,128)(2,1)S(1)} %pad_maximum_fusion.7), channel_id=1, source_target_pairs={{0,8},{8,0},{16,24},{24,16},{1,9},{9,1},{17,25},{25,17},{2,10},{10... | collective-permute-start | bytes 688136 | tf_op jit(solution)/shard_map/ppermute | solution.py:324
  127.6 6.6 %collective-permute-start.28 = (bf16[128,512]{1,0:T(8,128)(2,1)S(1)}, bf16[128,512]{1,0:T(8,128)(2,1)S(1)}, u32[]{:S(2)}, u32[]{:S(2)}) collective-permute-start(bf16[128,512]{1,0:T(8,128)(2,1)S(1)} %get-tuple-element.146), channel_id=1, source_target_pairs={{0,4},{1,5},{2,6},{3,7},{4,0},{5,1},{6,2},{7,3},{8,12},{9,13},{10,... | collective-permute-start | bytes 393224 | tf_op jit(solution)/shard_map/ppermute | solution.py:324
  134.3 8.5 %collective-permute-start.29 = (bf16[448,512]{1,0:T(8,128)(2,1)S(1)}, bf16[448,512]{1,0:T(8,128)(2,1)S(1)}, u32[]{:S(2)}, u32[]{:S(2)}) collective-permute-start(bf16[448,512]{1,0:T(8,128)(2,1)S(1)} %pad_maximum_fusion.refs_1_), channel_id=1, source_target_pairs={{0,8},{8,0},{16,24},{24,16},{1,9},{9,1},{17,25},{25,17},{2,10},{10... | collective-permute-start | bytes 1376264 | tf_op jit(solution)/shard_map/ppermute | solution.py:324
  134.8 9.6 %collective-permute-start.30 = (bf16[448,512]{1,0:T(8,128)(2,1)S(1)}, bf16[448,512]{1,0:T(8,128)(2,1)S(1)}, u32[]{:S(2)}, u32[]{:S(2)}) collective-permute-start(bf16[448,512]{1,0:T(8,128)(2,1)S(1)} %pad_maximum_fusion.1.refs_3_), channel_id=1, source_target_pairs={{0,16},{8,24},{16,0},{24,8},{1,17},{9,25},{17,1},{25,9},{2,18},{10... | collective-permute-start | bytes 1376264 | tf_op jit(solution)/shard_map/ppermute | solution.py:324
  137.9 6.5 %collective-permute-start.32 = (bf16[448,512]{1,0:T(8,128)(2,1)S(1)}, bf16[448,512]{1,0:T(8,128)(2,1)S(1)}, u32[]{:S(2)}, u32[]{:S(2)}) collective-permute-start(bf16[448,512]{1,0:T(8,128)(2,1)S(1)} %pad_maximum_fusion.1.refs_3_), channel_id=1, source_target_pairs={{0,1},{1,0},{2,3},{3,2},{4,5},{5,4},{6,7},{7,6},{8,9},{9,8},{10,11... | collective-permute-start | bytes 1376264 | tf_op jit(solution)/shard_map/ppermute | solution.py:324
  (31 other events, 189.3 us)

commit v3 on v2

--- a/solution.py
+++ b/solution.py
@@ -293,20 +293,20 @@
         store_chunks(order_ref, total_ref, packed_ref, width)
 
 
-def unpack_kernel(scale, pieces, place, *refs):
+def unpack_kernel(scale, places, *refs):
     order_ref = refs[0]
-    sources = refs[1 : 1 + pieces]
+    sources = refs[1 : 1 + len(places)]
     targets = refs[-9:-5]
     buffers = refs[-5:-1]
     sems = refs[-1]
     parts = [target.shape[0] // CHUNKS for target in targets]
     copies, slot = [], 0
-    for source in sources:
+    for source, place in zip(sources, places):
         for start in range(0, source.shape[0], sum(parts)):
             for kind, rows in enumerate(parts):
                 held = buffers[kind].at[pl.ds(slot * rows, rows)]
                 held[...] = source[start : start + rows, :].astype(F32) * scale[kind // 2]
-                target = pl.multiple_of(order_ref[place + slot] * rows, 16)
+                target = pl.multiple_of(order_ref[place] * rows, 16)
                 copies.append(
                     pltpu.make_async_copy(
                         held, targets[kind].at[pl.ds(target, rows)], sems.at[kind, slot]
@@ -315,6 +315,7 @@
                 copies[-1].start()
                 start += rows
             slot += 1
+            place += 1
     for copy in copies:
         copy.wait()
 
@@ -339,72 +340,89 @@
     return part[:rows], part[rows:]
 
 
+def halves_inner(blocks):
+    rows = blocks.shape[1] // 2
+    return blocks[:, :rows], blocks[:, rows:]
+
+
 def join(*parts):
     return jnp.concatenate(parts)
 
 
-def reduce_all(edge_packed, node_packed, partial, small):
-    side_a, side_b = halves(node_packed)
-    keep_a, send_a = halves(side_a)
-    keep_b, send_b = halves(side_b)
-    got_a, got_b = swap(send_a, "grp", 1), swap(send_b, "grp", 2)
-    node_a, node_b = add_rounded(keep_a, got_a), add_rounded(keep_b, got_b)
+def node_start(node_packed):
+    sides = [halves(side) for side in halves(node_packed)]
+    got = [swap(sides[0][1], "grp", 1), swap(sides[1][1], "grp", 2)]
+    return [side[0] for side in sides], got
+
+
+def reduce_all(edge_packed, node_kept, node_got, partial, small):
+    node_a, node_b = [add_rounded(kept, got) for kept, got in zip(node_kept, node_got)]
 
     keep, send = halves(edge_packed)
-    got, got_small = exchange((send, "dev", 1), (small, "dev", 1))
+    got, got_small, got_partial = exchange(
+        (send, "dev", 1), (small, "dev", 1), (partial[1], "dev", 1)
+    )
     edge_a, edge_b = halves(add_rounded(keep, got))
     small = small + got_small
+    owned = add_rounded(partial[0], got_partial)
+    owned_early, owned_late = halves_inner(owned)
 
     keep_a, send_a = halves(edge_a)
     keep_b, send_b = halves(edge_b)
     node_keep_a, node_send_a = halves(node_a)
     node_keep_b, node_send_b = halves(node_b)
-    got_a, got_b, got_node, got_small, got_partial = exchange(
+    got_a, got_b, got_node, got_small, got_owned = exchange(
         (send_a, "grp", 1),
         (send_b, "grp", 2),
         (join(node_send_a, node_send_b), "dev", 1),
         (small, "grp", 1),
-        (partial[1], "dev", 1),
-    )
-    owned = add_rounded(partial[0], got_partial)
+        (owned_early[1::2], "dev", 2),
+    )
     edge_a, edge_b = add_rounded(keep_a, got_a), add_rounded(keep_b, got_b)
     got_node_a, got_node_b = halves(got_node)
     node_a, node_b = add_rounded(node_keep_a, got_node_a), add_rounded(node_keep_b, got_node_b)
     small = small + got_small
+    owned_early = add_rounded(owned_early[::2], got_owned)
 
     pairs = [halves(part) for part in (edge_a, node_a, edge_b, node_b)]
-    got_a, got_b, got_small = exchange(
+    got_a, got_b, got_small, got_owned, got_early = exchange(
         (join(pairs[0][1], pairs[1][1]), "grp", 2),
         (join(pairs[2][1], pairs[3][1]), "grp", 1),
         (small, "grp", 2),
+        (owned_late[1::2], "dev", 2),
+        (owned_early[1], "dev", 4),
     )
     small = small + got_small
+    owned_late = add_rounded(owned_late[::2], got_owned)
     edge_rows = pairs[0][0].shape[0]
     parts = [
-        add_rounded(pairs[0][0], got_a[:edge_rows]),
-        add_rounded(pairs[1][0], got_a[edge_rows:]),
-        add_rounded(pairs[2][0], got_b[:edge_rows]),
-        add_rounded(pairs[3][0], got_b[edge_rows:]),
+        halves(add_rounded(pairs[0][0], got_a[:edge_rows])),
+        halves(add_rounded(pairs[1][0], got_a[edge_rows:])),
+        halves(add_rounded(pairs[2][0], got_b[:edge_rows])),
+        halves(add_rounded(pairs[3][0], got_b[edge_rows:])),
     ]
-    pairs = [halves(part) for part in parts]
-    got, got_small = exchange((join(*[pair[1] for pair in pairs]), "dev", 2), (small, "dev", 2))
-    kept = add_rounded(join(*[pair[0] for pair in pairs]), got)
+    got_1, got_2, got_3, got_small = exchange(
+        (join(parts[0][1], parts[1][1]), "dev", 2),
+        (join(parts[2][0], parts[3][0]), "dev", 4),
+        (join(parts[2][1], parts[3][1]), "dev", 6),
+        (small, "dev", 2),
+    )
     small = small + got_small
-    got, got_small, got_owned = exchange(
-        (kept, "dev", 4), (small, "dev", 4), (owned[1::2], "dev", 2)
-    )
-    owned = add_rounded(owned[::2], got_owned)
-    kept = add_rounded(kept, got)
+    kept = sum(
+        (got.astype(F32) for got in (got_1, got_2, got_3)),
+        join(parts[0][0], parts[1][0]).astype(F32),
+    ).astype(BF16)
+    got_1, got_2, got_small = exchange((kept, "dev", 2), (kept, "dev", 4), (small, "dev", 4))
+    (got_3,) = exchange((got_2, "dev", 2))
     small = small + got_small
-    early_rows, late_rows = halves(owned[1])
-    other, got_early = exchange((kept, "dev", 2), (early_rows, "dev", 4))
-
-    (own_a, own_b), (other_a, other_b) = halves(kept), halves(other)
-    side_a, side_b = join(own_a, other_a), join(own_b, other_b)
+
+    side_a, side_b = join(kept, got_1), join(got_2, got_3)
     got_a, got_b, got_late = exchange(
-        (side_a, "grp", 2), (side_b, "grp", 1), (late_rows, "dev", 4)
-    )
-    from_senders = owned[0].astype(F32) + join(got_early, got_late).astype(F32)
+        (side_a, "grp", 2), (side_b, "grp", 1), (owned_late[1], "dev", 4)
+    )
+    from_senders = join(owned_early[0], owned_late[0]).astype(F32) + join(
+        got_early, got_late
+    ).astype(F32)
     side_a, side_b = join(side_a, got_a), join(side_b, got_b)
     got_a, got_b, swapped_a, swapped_b = exchange(
         (side_a, "grp", 1),
@@ -413,21 +431,25 @@
         (side_b, "dev", 1),
     )
     last_a, last_b = exchange((got_a, "dev", 1), (got_b, "dev", 1))
-    ordered = [[side_a, got_a, side_b, got_b], [swapped_a, last_a, swapped_b, last_b]]
-    return ordered, small, from_senders
+    sources = [
+        [(side_a, 0), (side_b, 8)],
+        [(got_a, 4), (got_b, 12), (swapped_a, 16), (swapped_b, 24)],
+        [(last_a, 20), (last_b, 28)],
+    ]
+    return sources, small, from_senders
 
 
 def device_bits():
     group = lax.axis_index("grp")
     device = lax.axis_index("dev")
-    return group & 1, group >> 1, device & 1, (device >> 1) & 1
+    return group & 1, group >> 1, device & 1, (device >> 1) & 1, (device >> 2) & 1
 
 
 def relative_places(place):
-    x, y, core, z = device_bits()
-    first = core * 16 + x * 4 + y * 2 + z
-    second = core * 16 + y * 4 + x * 2 + z
-    return place ^ jnp.where((place & 8) == 0, first, second)
+    x, y, core, z, far = device_bits()
+    mirrored = (place & 25) | ((place & 4) >> 1) | ((place & 2) << 1)
+    plain = jnp.where((place & 8) == 0, place, mirrored)
+    return plain ^ (core * 16 + far * 8 + x * 4 + y * 2 + z)
 
 
 def edge_order():
@@ -497,10 +519,12 @@
         edge_places = edge_order()
         node_places = node_order()
         near = swap(packed_nodes, "dev", 2)
-        far = [swap(packed_nodes, "dev", 4), swap(packed_nodes, "dev", 6)]
-        pieces = [packed_nodes, swap(packed_nodes, "dev", 1), near, swap(near, "dev", 1)]
+        across = swap(packed_nodes, "dev", 4)
+        beside, across = lax.optimization_barrier((swap(packed_nodes, "dev", 1), across))
+        far = [near, across, swap(across, "dev", 2)]
+        pieces = [packed_nodes, beside]
         pieces = [piece[None] for piece in pieces]
-        ranges = [(0, 4), (4, 8)]
+        ranges = [(0, 2), (2, 8)]
     else:
         owners = jnp.arange(peers, dtype=jnp.int32)
         edge_places = node_places = jnp.arange(CHUNKS, dtype=jnp.int32)
@@ -637,6 +661,8 @@
             summed = results[4]
     hidden, normed, slope, inverse = saved
 
+    if paired:
+        node_kept, node_got = node_start(node_packed)
     grad_edges, partial, grad_nodes, edge_packed, edge_small = pl.pallas_call(
         functools.partial(backward_kernel, len(pieces)),
         grid_spec=pltpu.PrefetchScalarGridSpec(
@@ -705,9 +731,15 @@
         gain_row,
     )
 
+    if paired:
+        edge_packed, edge_small, *node_got = lax.optimization_barrier(
+            (edge_packed, edge_small, *node_got)
+        )
     small = jnp.concatenate([edge_small, node_small])
     if paired:
-        sources, small, from_senders = reduce_all(edge_packed, node_packed, partial, small)
+        sources, small, from_senders = reduce_all(
+            edge_packed, node_kept, node_got, partial, small
+        )
     else:
         node_sum, edge_sum, small = lax.psum(
             (node_packed.astype(F32), edge_packed.astype(F32), small), ("grp", "dev")
@@ -719,7 +751,7 @@
             ],
             axis=1,
         )
-        sources = [[interleaved.reshape(7 * width, width).astype(BF16)]]
+        sources = [[(interleaved.reshape(7 * width, width).astype(BF16), 0)]]
         ordered = jnp.swapaxes(partial, 0, 1).reshape(peers, count, width)
         from_senders = lax.psum_scatter(ordered.astype(F32), "dev", scatter_dimension=0)
     grad_nodes = grad_nodes + contract_features(
@@ -729,11 +761,12 @@
     edge_scale = float(total_rows * groups) ** (-0.5)
     node_scale = float(count * groups) ** (-0.5)
     totals = [3 * width, width, 2 * width, width]
-    unpacked, place = [], 0
+    unpacked = []
     for part in sources:
+        part, starts = zip(*part)
         places = sum(source.shape[0] for source in part) * CHUNKS // (7 * width)
         unpacked = pl.pallas_call(
-            functools.partial(unpack_kernel, (edge_scale, node_scale), len(part), place),
+            functools.partial(unpack_kernel, (edge_scale, node_scale), starts),
             grid_spec=pltpu.PrefetchScalarGridSpec(
                 num_scalar_prefetch=1,
                 grid=(1,),
@@ -750,9 +783,8 @@
             cost_estimate=pl.CostEstimate(
                 flops=0, bytes_accessed=42 * places * width * width // CHUNKS, transcendentals=0
             ),
-            name="unpack_%d" % place,
+            name="unpack_%d" % starts[0],
         )(edge_places, *part, *unpacked)
-        place += places
     edge_lift_grad, edge_mix_grad, node_lift_grad, node_mix_grad = unpacked
     return (
         grad_nodes[None],

time: 152 us -> 138 us (0.908)
  waiting for transfers between devices: 65.3 us -> 42.5 us
  starting transfers between devices: 34.8 us -> 40.7 us
  Pallas kernels: 39.6 us -> 41.7 us
    ppermute x35 -> x39, waiting for transfers between devices: 65.3 us -> 42.5 us  [swap(): return lax.ppermute(values, axis, [(i, i ^ bit) for i in range(size)])]
    ppermute x35 -> x39, starting transfers between devices: 34.8 us -> 40.7 us  [swap(): return lax.ppermute(values, axis, [(i, i ^ bit) for i in range(size)])]
    pallas_call x2 -> x3, Pallas kernels: 5.83 us -> 6.98 us  [per_device(): pl.pallas_call(functools.partial(unpack_kernel, (edge_scale, node_scale),...]
  transfers between devices with their start and end apart: 35 -> 39, of which waited for: 19 -> 18; matrix products, arithmetic and copies ran while one was open for 2% -> 2% of each run, Pallas kernels for 8% -> 22%
where the time goes in v3:
time: 138 us; the launch traced here: 137 us
  waiting for transfers between devices  42.5 us (31%)
  Pallas kernels  41.7 us (30%)
  starting transfers between devices  40.7 us (29%)
  local copies, waits for them, and re-layouts  7.59 us (6%)
  other arithmetic  3.14 us (2%)
  between operations  1.42 us (1%)
    ppermute x39, waiting for transfers between devices, swap(): return lax.ppermute(values, axis, [(i, i ^ bit) for i in range(size)])  42.5 us
    ppermute x39, starting transfers between devices, swap(): return lax.ppermute(values, axis, [(i, i ^ bit) for i in range(size)])  40.7 us
    pallas_call x1, Pallas kernels, per_device(): pl.pallas_call(functools.partial(backward_kernel, len(pieces)), grid_spec...  16.7 us
    pallas_call x2, Pallas kernels, per_device(): pl.pallas_call(functools.partial(forward_kernel, len(chosen), first, last...  13.1 us
    unnamed x40, local copies, waits for them, and re-layouts  7.04 us
    pallas_call x3, Pallas kernels, per_device(): pl.pallas_call(functools.partial(unpack_kernel, (edge_scale, node_scale),...  6.98 us
    pallas_call x1, Pallas kernels, per_device(): pl.pallas_call(lift_kernel, grid=(peers,), in_specs=[owned, whole(peers,...  4.85 us
  transfers between devices with their start and end apart: 39, of which 18 were waited for; matrix products, arithmetic and copies ran while one was open for 2% of the time, Pallas kernels for 22%

profile of v3, /device:TPU:0, one launch (start us, length us, event | category | flops | bytes accessed | tf_op | source)
XLA Modules:
  0.0 137.4 jit_solution(11734733005144804943)
XLA Ops:
  2.3 3.1 %collective-permute-start.2 = (bf16[272,512]{1,0:T(8,128)(2,1)S(1)}, bf16[272,512]{1,0:T(8,128)(2,1)S(1)}, u32[]{:S(2)}, u32[]{:S(2)}) collective-permute-start(bf16[272,512]{1,0:T(8,128)(2,1)S(1)} %pack.1), channel_id=1, source_target_pairs={{0,2},{1,3},{2,0},{3,1},{4,6},{5,7},{6,4},{7,5},{8,10},{9,11},{10,... | collective-permute-start | bytes 835592 | tf_op jit(solution)/shard_map/ppermute | solution.py:325
  5.4 2.6 %collective-permute-start.1 = (bf16[272,512]{1,0:T(8,128)(2,1)S(1)}, bf16[272,512]{1,0:T(8,128)(2,1)S(1)}, u32[]{:S(2)}, u32[]{:S(2)}) collective-permute-start(bf16[272,512]{1,0:T(8,128)(2,1)S(1)} %pack.1), channel_id=1, source_target_pairs={{0,4},{1,5},{2,6},{3,7},{4,0},{5,1},{6,2},{7,3},{8,12},{9,13},{10,... | collective-permute-start | bytes 835592 | tf_op jit(solution)/shard_map/ppermute | solution.py:325
  13.4 4.8 %lift.1.refs_6_.refs_10_ = f32[8,256,512]{2,1,0:T(8,128)S(1)} custom-call(bf16[8,256,512]{2,1,0:T(8,128)(2,1)S(1)} %bitcast.72, s32[8,256]{1,0:T(8,128)S(1)} %bitcast.60, bf16[256,512]{1,0:T(8,128)(2,1)S(1)} %bitcast.41, bf16[1536,512]{1,0:T(8,128)(2,1)S(1)} %copy-done, f32[1,512]{1,0:T(1,128)S(1)} %bitcast.77), custom_call_target="tpu_custom_call" | custom-call | flops 2684354560 | bytes 6291456 | tf_op jit(solution)/shard_map/lift/pallas_call | solution.py:540
  18.2 2.2 %collective-permute-done.1 = bf16[272,512]{1,0:T(8,128)(2,1)S(1)} collective-permute-done((bf16[272,512]{1,0:T(8,128)(2,1)S(1)}, bf16[272,512]{1,0:T(8,128)(2,1)S(1)}, u32[]{:S(2)}, u32[]{:S(2)}) %collective-permute-start.1) | collective-permute-done | bytes 278560 | tf_op jit(solution)/shard_map/ppermute | solution.py:325
  21.0 3.1 %forward_near.1 = (bf16[8,256,512]{2,1,0:T(8,128)(2,1)S(1)}, bf16[8,256,512]{2,1,0:T(8,128)(2,1)S(1)}, bf16[8,256,512]{2,1,0:T(8,128)(2,1)S(1)}, f32[8,256,1]{2,1,0:T(8,128)S(1)}, f32[256,512]{1,0:T(8,128)S(1)}) custom-call(s32[2]{0:T(128)S(1)} %bitcast.78, s32[8]{0:T(128)S(1)} %bitcast.69, s32[32]{0:T(128)S(1)} %fusion.18.refs_2_, s32[1]{0:T(128)} %bitcast.1.refs_3_, ...), custom_call_target="tpu_custom_call" | custom-call | flops 2147483648 | bytes 8388608 | tf_op jit(solution)/shard_map/forward_near/pallas_call | solution.py:638
  24.1 3.3 %collective-permute-done.3 = bf16[272,512]{1,0:T(8,128)(2,1)S(1)} collective-permute-done((bf16[272,512]{1,0:T(8,128)(2,1)S(1)}, bf16[272,512]{1,0:T(8,128)(2,1)S(1)}, u32[]{:S(2)}, u32[]{:S(2)}) %collective-permute-start.3) | collective-permute-done | bytes 278560 | tf_op jit(solution)/shard_map/ppermute | solution.py:325
  29.8 10.0 %forward_all.1 = (bf16[8,256,512]{2,1,0:T(8,128)(2,1)S(1)}, bf16[8,256,512]{2,1,0:T(8,128)(2,1)S(1)}, bf16[8,256,512]{2,1,0:T(8,128)(2,1)S(1)}, f32[8,256,1]{2,1...) custom-call(s32[6]{0:T(128)S(1)} %slice.178.refs_0_, ...), custom_call_target="tpu_custom_call", output_to_operand_aliasing={{0}: (16, {}), {1}: (17, {}), {2}: (18, {}), {3}: (19, {})} | custom-call | flops 2147483648 | bytes 8388608 | tf_op jit(solution)/shard_map/forward_all/pallas_call | solution.py:638
  43.0 16.7 %backward.1 = (bf16[8,256,512]{2,1,0:T(8,128)(2,1)}, bf16[2,4,256,512]{3,2,1,0:T(8,128)(2,1)S(1)}, f32[256,512]{1,0:T(8,128)S(1)}, bf16[2048,512]{1,0:T(8,128)(2,1)S(1)}, f32[2,512]{1,0:T(2,128)S(1)}) custom-call(s32[8]{0:T(128)S(1)} %iota_xor_fusion.refs_0_, s32[8]{0:T(128)S(1)} %bitcast.71, s32[32]{0:T(128)S(1)} %fusion.17.refs_2_.refs_0_, ...), custom_call_target="tpu_custom_call" | custom-call | flops 7516192768 | bytes 20971520 | tf_op jit(solution)/shard_map/backward/pallas_call | solution.py:666
  60.9 3.2 %collective-permute-done.10 = f32[4,512]{1,0:T(4,128)S(1)} collective-permute-done((f32[4,512]{1,0:T(4,128)S(1)}, f32[4,512]{1,0:T(4,128)S(1)}, u32[]{:S(2)}, u32[]{:S(2)}) %collective-permute-start.10) | collective-permute-done | bytes 8224 | tf_op jit(solution)/shard_map/ppermute | solution.py:325
  68.1 5.9 %collective-permute-done.15 = f32[4,512]{1,0:T(4,128)S(1)} collective-permute-done((f32[4,512]{1,0:T(4,128)S(1)}, f32[4,512]{1,0:T(4,128)S(1)}, u32[]{:S(2)}, u32[]{:S(2)}) %collective-permute-start.15) | collective-permute-done | bytes 8224 | tf_op jit(solution)/shard_map/ppermute | solution.py:325
  80.1 3.2 %collective-permute-done.19 = f32[4,512]{1,0:T(4,128)S(1)} collective-permute-done((f32[4,512]{1,0:T(4,128)S(1)}, f32[4,512]{1,0:T(4,128)S(1)}, u32[]{:S(2)}, u32[]{:S(2)}) %collective-permute-start.19) | collective-permute-done | bytes 8224 | tf_op jit(solution)/shard_map/ppermute | solution.py:325
  83.2 2.8 %collective-permute-done.21 = bf16[128,512]{1,0:T(8,128)(2,1)S(1)} collective-permute-done((bf16[128,512]{1,0:T(8,128)(2,1)S(1)}, bf16[128,512]{1,0:T(8,128)(2,1)S(1)}, u32[]{:S(2)}, u32[]{:S(2)}) %collective-permute-start.21) | collective-permute-done | bytes 131104 | tf_op jit(solution)/shard_map/ppermute | solution.py:325
  86.3 2.0 %collective-permute-start.22 = (bf16[112,512]{1,0:T(8,128)(2,1)S(1)}, bf16[112,512]{1,0:T(8,128)(2,1)S(1)}, u32[]{:S(2)}, u32[]{:S(2)}) collective-permute-start(bf16[112,512]{1,0:T(8,128)(2,1)S(1)} %pad_maximum_fusion.7), channel_id=1, source_target_pairs={{0,2},{1,3},{2,0},{3,1},{4,6},{5,7},{6,4},{7,5},{8,10},{9,11},{10,... | collective-permute-start | bytes 344072 | tf_op jit(solution)/shard_map/ppermute | solution.py:325
  88.8 2.0 %collective-permute-start.24 = (bf16[112,512]{1,0:T(8,128)(2,1)S(1)}, bf16[112,512]{1,0:T(8,128)(2,1)S(1)}, u32[]{:S(2)}, u32[]{:S(2)}) collective-permute-start(bf16[112,512]{1,0:T(8,128)(2,1)S(1)} %pad_maximum_fusion.9), channel_id=1, source_target_pairs={{0,6},{1,7},{2,4},{3,5},{4,2},{5,3},{6,0},{7,1},{8,14},{9,15},{10,... | collective-permute-start | bytes 344072 | tf_op jit(solution)/shard_map/ppermute | solution.py:325
  92.5 4.2 %collective-permute-done.23 = bf16[112,512]{1,0:T(8,128)(2,1)S(1)} collective-permute-done((bf16[112,512]{1,0:T(8,128)(2,1)S(1)}, bf16[112,512]{1,0:T(8,128)(2,1)S(1)}, u32[]{:S(2)}, u32[]{:S(2)}) %collective-permute-start.23) | collective-permute-done | bytes 114720 | tf_op jit(solution)/shard_map/ppermute | solution.py:325
  96.8 3.9 %collective-permute-start.28 = (f32[4,512]{1,0:T(4,128)S(1)}, f32[4,512]{1,0:T(4,128)S(1)}, u32[]{:S(2)}, u32[]{:S(2)}) collective-permute-start(f32[4,512]{1,0:T(4,128)S(1)} %add.112), channel_id=1, source_target_pairs={{0,4},{1,5},{2,6},{3,7},{4,0},{5,1},{6,2},{7,3},{8,12},{9,13},{10,... | collective-permute-start | bytes 24584 | tf_op jit(solution)/shard_map/ppermute | solution.py:325
  100.8 2.8 %collective-permute-start.27 = (bf16[112,512]{1,0:T(8,128)(2,1)S(1)}, bf16[112,512]{1,0:T(8,128)(2,1)S(1)}, u32[]{:S(2)}, u32[]{:S(2)}) collective-permute-start(bf16[112,512]{1,0:T(8,128)(2,1)S(1)} %add_convert_fusion.13), channel_id=1, source_target_pairs={{0,4},{1,5},{2,6},{3,7},{4,0},{5,1},{6,2},{7,3},{8,12},{9,13},{10,... | collective-permute-start | bytes 344072 | tf_op jit(solution)/shard_map/ppermute | solution.py:325
  103.7 3.0 %collective-permute-done.26 = bf16[112,512]{1,0:T(8,128)(2,1)S(1)} collective-permute-done((bf16[112,512]{1,0:T(8,128)(2,1)S(1)}, bf16[112,512]{1,0:T(8,128)(2,1)S(1)}, u32[]{:S(2)}, u32[]{:S(2)}) %collective-permute-start.26) | collective-permute-done | bytes 114720 | tf_op jit(solution)/shard_map/ppermute | solution.py:325
  108.4 3.3 %collective-permute-done.29 = bf16[112,512]{1,0:T(8,128)(2,1)S(1)} collective-permute-done((bf16[112,512]{1,0:T(8,128)(2,1)S(1)}, bf16[112,512]{1,0:T(8,128)(2,1)S(1)}, u32[]{:S(2)}, u32[]{:S(2)}) %collective-permute-start.29) | collective-permute-done | bytes 114720 | tf_op jit(solution)/shard_map/ppermute | solution.py:325
  111.9 3.7 %collective-permute-start.32 = (bf16[128,512]{1,0:T(8,128)(2,1)S(1)}, bf16[128,512]{1,0:T(8,128)(2,1)S(1)}, u32[]{:S(2)}, u32[]{:S(2)}) collective-permute-start(bf16[128,512]{1,0:T(8,128)(2,1)S(1)} %get-tuple-element.176), channel_id=1, source_target_pairs={{0,4},{1,5},{2,6},{3,7},{4,0},{5,1},{6,2},{7,3},{8,12},{9,13},{10,... | collective-permute-start | bytes 393224 | tf_op jit(solution)/shard_map/ppermute | solution.py:325
  115.6 4.3 %collective-permute-done.32 = bf16[128,512]{1,0:T(8,128)(2,1)S(1)} collective-permute-done((bf16[128,512]{1,0:T(8,128)(2,1)S(1)}, bf16[128,512]{1,0:T(8,128)(2,1)S(1)}, u32[]{:S(2)}, u32[]{:S(2)}) %collective-permute-start.32) | collective-permute-done | bytes 131104 | tf_op jit(solution)/shard_map/ppermute | solution.py:325
  125.1 2.0 %unpack_0.1 = (f32[1536,512]{1,0:T(8,128)}, f32[512,512]{1,0:T(8,128)}, f32[1024,512]{1,0:T(8,128)}, f32[512,512]{1,0:T(8,128)}) custom-call(s32[32]{0:T(128)S(1)} %fusion.17.refs_2_.refs_0_, bf16[448,512]{1,0:T(8,128)(2,1)S(1)} %pad_maximum_fusion.refs_1_, bf16[448,512]{1,0:T(8,128)(2,1)S(1)} %pad_maximum_fusion.1.refs_2_), custom_call_target="tpu_custom_call" | custom-call | bytes 2752512 | tf_op jit(solution)/shard_map/unpack_0/pallas_call | solution.py:768
  132.2 2.9 %unpack_4.1 = (f32[1536,512]{1,0:T(8,128)}, f32[512,512]{1,0:T(8,128)}, f32[1024,512]{1,0:T(8,128)}, f32[512,512]{1,0:T(8,128)}) custom-call(s32[32]{0:T(128)S(1)} %fusion.17.refs_2_.refs_0_, bf16[448,512]{1,0:T(8,128)(2,1)S(1)} %collective-permute-done.33.refs_1_, ...), custom_call_target="tpu_custom_call", output_to_operand_aliasing={{0}: (5, {}), {1}: (6, {}), {2}: (7, {}), {3}: (8, {})} | custom-call | bytes 5505024 | tf_op jit(solution)/shard_map/unpack_4/pallas_call | solution.py:768
  135.2 2.0 %unpack_20.1 = (f32[1536,512]{1,0:T(8,128)}, f32[512,512]{1,0:T(8,128)}, f32[1024,512]{1,0:T(8,128)}, f32[512,512]{1,0:T(8,128)}) custom-call(s32[32]{0:T(128)S(1)} %fusion.17.refs_2_.refs_0_, bf16[448,512]{1,0:T(8,128)(2,1)S(1)} %collective-permute-done.37.refs_1_, ...), custom_call_target="tpu_custom_call", output_to_operand_aliasing={{0}: (3, {}), {1}: (4, {}), {2}: (5, {}), {3}: (6, {})} | custom-call | bytes 2752512 | tf_op jit(solution)/shard_map/unpack_20/pallas_call | solution.py:768
  (154 shorter events, 38.9 us)
Async XLA Ops:
  2.3 21.8 %collective-permute-start.2 = (bf16[272,512]{1,0:T(8,128)(2,1)S(1)}, bf16[272,512]{1,0:T(8,128)(2,1)S(1)}, u32[]{:S(2)}, u32[]{:S(2)}) collective-permute-start(bf16[272,512]{1,0:T(8,128)(2,1)S(1)} %pack.1), channel_id=1, source_target_pairs={{0,2},{1,3},{2,0},{3,1},{4,6},{5,7},{6,4},{7,5},{8,10},{9,11},{10,... | collective-permute-start | bytes 835592 | tf_op jit(solution)/shard_map/ppermute | solution.py:325
  5.4 15.0 %collective-permute-start.1 = (bf16[272,512]{1,0:T(8,128)(2,1)S(1)}, bf16[272,512]{1,0:T(8,128)(2,1)S(1)}, u32[]{:S(2)}, u32[]{:S(2)}) collective-permute-start(bf16[272,512]{1,0:T(8,128)(2,1)S(1)} %pack.1), channel_id=1, source_target_pairs={{0,4},{1,5},{2,6},{3,7},{4,0},{5,1},{6,2},{7,3},{8,12},{9,13},{10,... | collective-permute-start | bytes 835592 | tf_op jit(solution)/shard_map/ppermute | solution.py:325
  8.0 12.4 %collective-permute-start = (bf16[272,512]{1,0:T(8,128)(2,1)S(1)}, bf16[272,512]{1,0:T(8,128)(2,1)S(1)}, u32[]{:S(2)}, u32[]{:S(2)}) collective-permute-start(bf16[272,512]{1,0:T(8,128)(2,1)S(1)} %pack.1), channel_id=1, source_target_pairs={{0,1},{1,0},{2,3},{3,2},{4,5},{5,4},{6,7},{7,6},{8,9},{9,8},{10,11... | collective-permute-start | bytes 835592 | tf_op jit(solution)/shard_map/ppermute | solution.py:325
  20.5 6.9 %collective-permute-start.3 = (bf16[272,512]{1,0:T(8,128)(2,1)S(1)}, bf16[272,512]{1,0:T(8,128)(2,1)S(1)}, u32[]{:S(2)}, u32[]{:S(2)}) collective-permute-start(bf16[272,512]{1,0:T(8,128)(2,1)S(1)} %collective-permute-done.1), channel_id=1, source_target_pairs={{0,2},{1,3},{2,0},{3,1},{4,6},{5,7},{6,4},{7,5},{8,10},{9,11},{10,... | collective-permute-start | bytes 835592 | tf_op jit(solution)/shard_map/ppermute | solution.py:325
  39.9 19.9 %collective-permute-start.8 = (bf16[384,512]{1,0:T(8,128)(2,1)S(1)}, bf16[384,512]{1,0:T(8,128)(2,1)S(1)}, u32[]{:S(2)}, u32[]{:S(2)}) collective-permute-start(bf16[384,512]{1,0:T(8,128)(2,1)S(1)} %get-tuple-element.208), channel_id=1, source_target_pairs={{0,16},{8,24},{16,0},{24,8},{1,17},{9,25},{17,1},{25,9},{2,18},{10... | collective-permute-start | bytes 1179656 | tf_op jit(solution)/shard_map/ppermute | solution.py:325
  41.5 18.3 %collective-permute-start.7 = (bf16[384,512]{1,0:T(8,128)(2,1)S(1)}, bf16[384,512]{1,0:T(8,128)(2,1)S(1)}, u32[]{:S(2)}, u32[]{:S(2)}) collective-permute-start(bf16[384,512]{1,0:T(8,128)(2,1)S(1)} %get-tuple-element.209), channel_id=1, source_target_pairs={{0,8},{8,0},{16,24},{24,16},{1,9},{9,1},{17,25},{25,17},{2,10},{10... | collective-permute-start | bytes 1179656 | tf_op jit(solution)/shard_map/ppermute | solution.py:325
  65.0 9.3 %collective-permute-start.14 = (bf16[384,512]{1,0:T(8,128)(2,1)S(1)}, bf16[384,512]{1,0:T(8,128)(2,1)S(1)}, u32[]{:S(2)}, u32[]{:S(2)}) collective-permute-start(bf16[384,512]{1,0:T(8,128)(2,1)S(1)} %pad_maximum_fusion.2), channel_id=1, source_target_pairs={{0,1},{1,0},{2,3},{3,2},{4,5},{5,4},{6,7},{7,6},{8,9},{9,8},{10,11... | collective-permute-start | bytes 1179656 | tf_op jit(solution)/shard_map/ppermute | solution.py:325
  65.2 8.8 %collective-permute-start.12 = (bf16[256,512]{1,0:T(8,128)(2,1)S(1)}, bf16[256,512]{1,0:T(8,128)(2,1)S(1)}, u32[]{:S(2)}, u32[]{:S(2)}) collective-permute-start(bf16[256,512]{1,0:T(8,128)(2,1)S(1)} %get-tuple-element.141), channel_id=1, source_target_pairs={{0,8},{8,0},{16,24},{24,16},{1,9},{9,1},{17,25},{25,17},{2,10},{10... | collective-permute-start | bytes 786440 | tf_op jit(solution)/shard_map/ppermute | solution.py:325
  65.7 8.3 %collective-permute-start.13 = (bf16[256,512]{1,0:T(8,128)(2,1)S(1)}, bf16[256,512]{1,0:T(8,128)(2,1)S(1)}, u32[]{:S(2)}, u32[]{:S(2)}) collective-permute-start(bf16[256,512]{1,0:T(8,128)(2,1)S(1)} %get-tuple-element.142), channel_id=1, source_target_pairs={{0,16},{8,24},{16,0},{24,8},{1,17},{9,25},{17,1},{25,9},{2,18},{10... | collective-permute-start | bytes 786440 | tf_op jit(solution)/shard_map/ppermute | solution.py:325
  66.2 8.0 %collective-permute-start.16 = (bf16[2,128,512]{2,1,0:T(8,128)(2,1)S(1)}, bf16[2,128,512]{2,1,0:T(8,128)(2,1)S(1)}, u32[]{:S(2)}, u32[]{:S(2)}) collective-permute-start(bf16[2,128,512]{2,1,0:T(8,128)(2,1)S(1)} %slice.193), channel_id=1, source_target_pairs={{0,2},{1,3},{2,0},{3,1},{4,6},{5,7},{6,4},{7,5},{8,10},{9,11},{10,... | collective-permute-start | bytes 786440 | tf_op jit(solution)/shard_map/ppermute | solution.py:325
  66.6 7.4 %collective-permute-start.15 = (f32[4,512]{1,0:T(4,128)S(1)}, f32[4,512]{1,0:T(4,128)S(1)}, u32[]{:S(2)}, u32[]{:S(2)}) collective-permute-start(f32[4,512]{1,0:T(4,128)S(1)} %fusion.20), channel_id=1, source_target_pairs={{0,8},{8,0},{16,24},{24,16},{1,9},{9,1},{17,25},{25,17},{2,10},{10... | collective-permute-start | bytes 24584 | tf_op jit(solution)/shard_map/ppermute | solution.py:325
  74.7 11.3 %collective-permute-start.20 = (bf16[2,128,512]{2,1,0:T(8,128)(2,1)S(1)}, bf16[2,128,512]{2,1,0:T(8,128)(2,1)S(1)}, u32[]{:S(2)}, u32[]{:S(2)}) collective-permute-start(bf16[2,128,512]{2,1,0:T(8,128)(2,1)S(1)} %slice.207), channel_id=1, source_target_pairs={{0,2},{1,3},{2,0},{3,1},{4,6},{5,7},{6,4},{7,5},{8,10},{9,11},{10,... | collective-permute-start | bytes 786440 | tf_op jit(solution)/shard_map/ppermute | solution.py:325
  75.1 10.9 %collective-permute-start.17 = (bf16[224,512]{1,0:T(8,128)(2,1)S(1)}, bf16[224,512]{1,0:T(8,128)(2,1)S(1)}, u32[]{:S(2)}, u32[]{:S(2)}) collective-permute-start(bf16[224,512]{1,0:T(8,128)(2,1)S(1)} %pad_maximum_fusion.3), channel_id=1, source_target_pairs={{0,16},{8,24},{16,0},{24,8},{1,17},{9,25},{17,1},{25,9},{2,18},{10... | collective-permute-start | bytes 688136 | tf_op jit(solution)/shard_map/ppermute | solution.py:325
  76.6 9.3 %collective-permute-start.18 = (bf16[224,512]{1,0:T(8,128)(2,1)S(1)}, bf16[224,512]{1,0:T(8,128)(2,1)S(1)}, u32[]{:S(2)}, u32[]{:S(2)}) collective-permute-start(bf16[224,512]{1,0:T(8,128)(2,1)S(1)} %pad_maximum_fusion.4), channel_id=1, source_target_pairs={{0,8},{8,0},{16,24},{24,16},{1,9},{9,1},{17,25},{25,17},{2,10},{10... | collective-permute-start | bytes 688136 | tf_op jit(solution)/shard_map/ppermute | solution.py:325
  78.2 7.8 %collective-permute-start.21 = (bf16[128,512]{1,0:T(8,128)(2,1)S(1)}, bf16[128,512]{1,0:T(8,128)(2,1)S(1)}, u32[]{:S(2)}, u32[]{:S(2)}) collective-permute-start(bf16[128,512]{1,0:T(8,128)(2,1)S(1)} %get-tuple-element.155), channel_id=1, source_target_pairs={{0,4},{1,5},{2,6},{3,7},{4,0},{5,1},{6,2},{7,3},{8,12},{9,13},{10,... | collective-permute-start | bytes 393224 | tf_op jit(solution)/shard_map/ppermute | solution.py:325
  88.4 8.3 %collective-permute-start.23 = (bf16[112,512]{1,0:T(8,128)(2,1)S(1)}, bf16[112,512]{1,0:T(8,128)(2,1)S(1)}, u32[]{:S(2)}, u32[]{:S(2)}) collective-permute-start(bf16[112,512]{1,0:T(8,128)(2,1)S(1)} %pad_maximum_fusion.8), channel_id=1, source_target_pairs={{0,4},{1,5},{2,6},{3,7},{4,0},{5,1},{6,2},{7,3},{8,12},{9,13},{10,... | collective-permute-start | bytes 344072 | tf_op jit(solution)/shard_map/ppermute | solution.py:325
  88.8 7.9 %collective-permute-start.24 = (bf16[112,512]{1,0:T(8,128)(2,1)S(1)}, bf16[112,512]{1,0:T(8,128)(2,1)S(1)}, u32[]{:S(2)}, u32[]{:S(2)}) collective-permute-start(bf16[112,512]{1,0:T(8,128)(2,1)S(1)} %pad_maximum_fusion.9), channel_id=1, source_target_pairs={{0,6},{1,7},{2,4},{3,5},{4,2},{5,3},{6,0},{7,1},{8,14},{9,15},{10,... | collective-permute-start | bytes 344072 | tf_op jit(solution)/shard_map/ppermute | solution.py:325
  96.8 6.9 %collective-permute-start.28 = (f32[4,512]{1,0:T(4,128)S(1)}, f32[4,512]{1,0:T(4,128)S(1)}, u32[]{:S(2)}, u32[]{:S(2)}) collective-permute-start(f32[4,512]{1,0:T(4,128)S(1)} %add.112), channel_id=1, source_target_pairs={{0,4},{1,5},{2,6},{3,7},{4,0},{5,1},{6,2},{7,3},{8,12},{9,13},{10,... | collective-permute-start | bytes 24584 | tf_op jit(solution)/shard_map/ppermute | solution.py:325
  111.7 8.2 %collective-permute-start.30 = (bf16[224,512]{1,0:T(8,128)(2,1)S(1)}, bf16[224,512]{1,0:T(8,128)(2,1)S(1)}, u32[]{:S(2)}, u32[]{:S(2)}) collective-permute-start(bf16[224,512]{1,0:T(8,128)(2,1)S(1)} %pad_maximum_fusion.5), channel_id=1, source_target_pairs={{0,16},{8,24},{16,0},{24,8},{1,17},{9,25},{17,1},{25,9},{2,18},{10... | collective-permute-start | bytes 688136 | tf_op jit(solution)/shard_map/ppermute | solution.py:325
  111.8 8.2 %collective-permute-start.31 = (bf16[224,512]{1,0:T(8,128)(2,1)S(1)}, bf16[224,512]{1,0:T(8,128)(2,1)S(1)}, u32[]{:S(2)}, u32[]{:S(2)}) collective-permute-start(bf16[224,512]{1,0:T(8,128)(2,1)S(1)} %pad_maximum_fusion.6), channel_id=1, source_target_pairs={{0,8},{8,0},{16,24},{24,16},{1,9},{9,1},{17,25},{25,17},{2,10},{10... | collective-permute-start | bytes 688136 | tf_op jit(solution)/shard_map/ppermute | solution.py:325
  111.9 8.1 %collective-permute-start.32 = (bf16[128,512]{1,0:T(8,128)(2,1)S(1)}, bf16[128,512]{1,0:T(8,128)(2,1)S(1)}, u32[]{:S(2)}, u32[]{:S(2)}) collective-permute-start(bf16[128,512]{1,0:T(8,128)(2,1)S(1)} %get-tuple-element.176), channel_id=1, source_target_pairs={{0,4},{1,5},{2,6},{3,7},{4,0},{5,1},{6,2},{7,3},{8,12},{9,13},{10,... | collective-permute-start | bytes 393224 | tf_op jit(solution)/shard_map/ppermute | solution.py:325
  120.0 8.5 %collective-permute-start.33 = (bf16[448,512]{1,0:T(8,128)(2,1)S(1)}, bf16[448,512]{1,0:T(8,128)(2,1)S(1)}, u32[]{:S(2)}, u32[]{:S(2)}) collective-permute-start(bf16[448,512]{1,0:T(8,128)(2,1)S(1)} %pad_maximum_fusion.refs_1_), channel_id=1, source_target_pairs={{0,8},{8,0},{16,24},{24,16},{1,9},{9,1},{17,25},{25,17},{2,10},{10... | collective-permute-start | bytes 1376264 | tf_op jit(solution)/shard_map/ppermute | solution.py:325
  122.0 8.5 %collective-permute-start.34 = (bf16[448,512]{1,0:T(8,128)(2,1)S(1)}, bf16[448,512]{1,0:T(8,128)(2,1)S(1)}, u32[]{:S(2)}, u32[]{:S(2)}) collective-permute-start(bf16[448,512]{1,0:T(8,128)(2,1)S(1)} %pad_maximum_fusion.1.refs_2_), channel_id=1, source_target_pairs={{0,16},{8,24},{16,0},{24,8},{1,17},{9,25},{17,1},{25,9},{2,18},{10... | collective-permute-start | bytes 1376264 | tf_op jit(solution)/shard_map/ppermute | solution.py:325
  124.0 6.5 %collective-permute-start.35 = (bf16[448,512]{1,0:T(8,128)(2,1)S(1)}, bf16[448,512]{1,0:T(8,128)(2,1)S(1)}, u32[]{:S(2)}, u32[]{:S(2)}) collective-permute-start(bf16[448,512]{1,0:T(8,128)(2,1)S(1)} %pad_maximum_fusion.refs_1_), channel_id=1, source_target_pairs={{0,1},{1,0},{2,3},{3,2},{4,5},{5,4},{6,7},{7,6},{8,9},{9,8},{10,11... | collective-permute-start | bytes 1376264 | tf_op jit(solution)/shard_map/ppermute | solution.py:325
  (35 other events, 187.1 us)

commit v4 on v3

--- a/solution.py
+++ b/solution.py
@@ -166,6 +166,7 @@
 
     owner = owner_ref[step]
     live_count = live_ref[owner]
+    slots = pre_ref.shape[1]
 
     def body(rows):
         index = pick_row(held_ref[step, count:, :rows], mine_ref[0])
@@ -178,11 +179,14 @@
         slope_ref[0, :rows] = slope.astype(BF16)
         normed_ref[0, :rows] = normed.astype(BF16)
         inverse_ref[0, :rows] = inverse
+        if rows < slots:
+            for saved_ref in (hidden_ref, slope_ref, normed_ref, inverse_ref):
+                saved_ref[0, rows:] = jnp.zeros_like(saved_ref[0, rows:])
         live = live_rows(live_count, normed.shape)
         message = jnp.where(live, normed * gain_ref[...], 0.0).astype(BF16)
         summed_ref[...] += matmul(one_hot(receiver_ref[pl.ds(owner, 1), :][:, :rows], count), message)
 
-    by_live(live_count, pre_ref.shape[1], body)
+    by_live(live_count, slots, body)
 
     if not last:
         return
@@ -215,7 +219,7 @@
 
 
 def backward_kernel(pieces, *refs):
-    owner_ref, live_ref, order_ref, mine_ref = refs[:4]
+    arrival_ref, live_ref, order_ref, mine_ref = refs[:4]
     sources = refs[4 : 4 + pieces]
     (
         edges_ref,
@@ -239,51 +243,80 @@
         received_ref,
         total_ref,
         held_ref,
+        out_ref,
+        pre_ref,
+        sent_ref,
         sems,
     ) = refs[4 + pieces :]
     step = pl.program_id(0)
     count, width = nodes_ref.shape
-    slots = edges_ref.shape[1]
-    owner = owner_ref[step]
-    live_count = live_ref[owner]
-    load_pieces(step, sources, held_ref, sems)
+    group, slots = edges_ref.shape[:2]
+    rows = group * slots
+    copies, start = [], 0
+    for place, source in enumerate(sources):
+        size = source.shape[0]
+        copies.append(
+            pltpu.make_async_copy(source, held_ref.at[pl.ds(start, size)], sems.at[place])
+        )
+        start += size
 
     @pl.when(step == 0)
     def _():
+        for copy in copies:
+            copy.start()
         received_ref[...] = jnp.zeros_like(received_ref)
         total_ref[...] = jnp.zeros_like(total_ref)
         small_ref[...] = jnp.zeros_like(small_ref)
 
-    def body(rows):
-        seed = seed_ref[0, :rows].astype(F32)
-        live = live_rows(live_count, seed.shape)
-        receiver_table = one_hot(receiver_ref[pl.ds(owner, 1), :][:, :rows], count)
+    tables = []
+    for member in range(group):
+        owner = step * group + member
+        seed = seed_ref[member].astype(F32)
+        live = live_rows(live_ref[owner], seed.shape)
+        table = one_hot(receiver_ref[pl.ds(owner, 1), :], count)
+        tables.append(table)
         grad_message = jnp.where(
-            live, seed + contract_rows(receiver_table, summed_grad_ref[...]), 0.0
+            live, seed + contract_rows(table, summed_grad_ref[...]), 0.0
         )
-        normed = normed_ref[0, :rows].astype(F32)
+        normed = normed_ref[member].astype(F32)
         small_ref[1:2, :] += jnp.sum(grad_message * normed, axis=0, keepdims=True)
         grad_out = norm_backward(
-            grad_message * gain_ref[...], normed, inverse_ref[0, :rows]
+            grad_message * gain_ref[...], normed, inverse_ref[member]
         ).astype(BF16)
-        total_ref[3 * width :, :] += contract_rows(hidden_ref[0, :rows], grad_out)
         grad_pre = (
-            contract_features(grad_out, mix_ref[...]) * slope_ref[0, :rows].astype(F32)
+            contract_features(grad_out, mix_ref[...]) * slope_ref[member].astype(F32)
         ).astype(BF16)
+        out_ref[member * slots : (member + 1) * slots, :] = grad_out
+        pre_ref[member * slots : (member + 1) * slots, :] = grad_pre
         small_ref[0:1, :] += jnp.sum(grad_pre.astype(F32), axis=0, keepdims=True)
-        total_ref[:width, :] += contract_rows(edges_ref[0, :rows], grad_pre)
-        index = pick_row(held_ref[step, count:, :rows], mine_ref[0])
-        sent = matmul(one_hot(index, count), grad_pre).astype(BF16)
-        partial_ref[0, 0] = sent
-        total_ref[width : 2 * width, :] += contract_rows(held_ref[step, :count], sent)
-        received_ref[...] += matmul(receiver_table, grad_pre)
-        grad_edges_ref[0, :rows] = jnp.where(
+        grad_edges_ref[member] = jnp.where(
             live, seed + contract_features(grad_pre, lift_ref[:width]), 0.0
         ).astype(BF16)
-        if rows < slots:
-            grad_edges_ref[0, rows:] = jnp.zeros((slots - rows, width), BF16)
-
-    by_live(live_count, slots, body)
+
+    @pl.when(step == 0)
+    def _():
+        for copy in copies:
+            copy.wait()
+
+    first_arrival = (arrival_ref[step * group] // group) * group
+    for member in range(group):
+        arrival = arrival_ref[step * group + member]
+        place = arrival - first_arrival
+        index = pick_row(held_ref[arrival, count:, :slots], mine_ref[0])
+        sent = matmul(
+            one_hot(index, count), pre_ref[member * slots : (member + 1) * slots, :]
+        ).astype(BF16)
+        partial_ref[place % 2, place // 2] = sent
+        sent_ref[place] = sent
+    received_ref[...] += matmul(jnp.concatenate(tables, axis=1), pre_ref[...])
+    total_ref[3 * width :, :] += contract_rows(
+        hidden_ref[...].reshape(rows, width), out_ref[...]
+    )
+    total_ref[:width, :] += contract_rows(edges_ref[...].reshape(rows, width), pre_ref[...])
+    total_ref[width : 2 * width, :] += contract_rows(
+        held_ref[pl.ds(first_arrival, group), :count].reshape(group * count, width),
+        sent_ref[...].reshape(group * count, width),
+    )
 
     @pl.when(step == pl.num_programs(0) - 1)
     def _():
@@ -433,8 +466,14 @@
     last_a, last_b = exchange((got_a, "dev", 1), (got_b, "dev", 1))
     sources = [
         [(side_a, 0), (side_b, 8)],
-        [(got_a, 4), (got_b, 12), (swapped_a, 16), (swapped_b, 24)],
-        [(last_a, 20), (last_b, 28)],
+        [
+            (got_a, 4),
+            (got_b, 12),
+            (swapped_a, 16),
+            (swapped_b, 24),
+            (last_a, 20),
+            (last_b, 28),
+        ],
     ]
     return sources, small, from_senders
 
@@ -521,10 +560,10 @@
         near = swap(packed_nodes, "dev", 2)
         across = swap(packed_nodes, "dev", 4)
         beside, across = lax.optimization_barrier((swap(packed_nodes, "dev", 1), across))
-        far = [near, across, swap(across, "dev", 2)]
+        behind = swap(across, "dev", 2)
         pieces = [packed_nodes, beside]
         pieces = [piece[None] for piece in pieces]
-        ranges = [(0, 2), (2, 8)]
+        ranges = [(0, 2), (2, 6), (6, 8)]
     else:
         owners = jnp.arange(peers, dtype=jnp.int32)
         edge_places = node_places = jnp.arange(CHUNKS, dtype=jnp.int32)
@@ -561,21 +600,21 @@
             (1,) + dims, lambda i, owner, *_: (owner[i],) + (0,) * len(dims)
         )
 
-    def by_step(*dims):
-        return pl.BlockSpec((1,) + dims, lambda i, *_: (i,) + (0,) * len(dims))
+    group = 2
+
+    def grouped(*dims):
+        return pl.BlockSpec((group,) + dims, lambda i, *_: (i,) + (0,) * len(dims))
 
     saved = []
     summed = None
     for begin, end in ranges:
         first, last = begin == 0, end == peers
+        if last and not first:
+            behind, summed = lax.optimization_barrier((behind, summed))
         if not first:
-            *far, summed = lax.optimization_barrier((*far, summed))
-            for piece in far:
+            for piece in [behind] if last else [near, across]:
                 pieces += [piece[None], swap(piece, "dev", 1)[None]]
         chosen = pieces[begin:] if paired else pieces
-
-        def saved_step(*dims, begin=begin):
-            return pl.BlockSpec((1,) + dims, lambda i, *_: (i + begin,) + (0,) * len(dims))
 
         operands = chosen + [
             pre,
@@ -598,7 +637,7 @@
             aliases = {4 + len(operands) + j: j for j in range(4)}
             operands += saved + [summed]
             in_specs += [anywhere] * 4 + [whole(count, width)]
-        out_specs = [saved_step(slots, width)] * 3 + [saved_step(slots, 1)]
+        out_specs = [by_owner(slots, width)] * 3 + [by_owner(slots, 1)]
         out_shape = [shape(peers, slots, width, kind=BF16)] * 3 + [shape(peers, slots, 1)]
         scratch = [
             pltpu.VMEM((end - begin, gathered_rows, width), BF16),
@@ -652,7 +691,7 @@
                 bytes_accessed=8 * total_rows * width,
                 transcendentals=total_rows * width,
             ),
-            name="forward_" + ("all" if last else "near"),
+            name="forward_%d" % begin,
         )(owners[begin:end], live, node_places, mine.reshape(1), *operands)
         saved = list(results[:4])
         if last:
@@ -667,16 +706,16 @@
         functools.partial(backward_kernel, len(pieces)),
         grid_spec=pltpu.PrefetchScalarGridSpec(
             num_scalar_prefetch=4,
-            grid=(peers,),
+            grid=(peers // group,),
             in_specs=[anywhere] * len(pieces)
             + [
-                by_owner(slots, width),
-                by_owner(slots, width),
+                grouped(slots, width),
+                grouped(slots, width),
                 whole(peers, slots),
-                by_step(slots, width),
-                by_step(slots, width),
-                by_step(slots, width),
-                by_step(slots, 1),
+                grouped(slots, width),
+                grouped(slots, width),
+                grouped(slots, width),
+                grouped(slots, 1),
                 whole(count, width),
                 whole(count, width),
                 whole(count, width),
@@ -685,8 +724,11 @@
                 whole(1, width),
             ],
             out_specs=[
-                by_owner(slots, width),
-                pl.BlockSpec((1, 1, count, width), lambda i, *_: (i % 2, i // 2, 0, 0)),
+                grouped(slots, width),
+                pl.BlockSpec(
+                    (2, group // 2, count, width),
+                    lambda i, arrival, *_: (0, arrival[i * group] // group, 0, 0),
+                ),
                 result(count, width),
                 result(4 * width, width),
                 result(2, width),
@@ -695,6 +737,9 @@
                 pltpu.VMEM((count, width), F32),
                 pltpu.VMEM((4 * width, width), F32),
                 pltpu.VMEM((peers, gathered_rows, width), BF16),
+                pltpu.VMEM((group * slots, width), BF16),
+                pltpu.VMEM((group * slots, width), BF16),
+                pltpu.VMEM((group, count, width), BF16),
                 pltpu.SemaphoreType.DMA((len(pieces),)),
             ],
         ),
@@ -705,7 +750,7 @@
             shape(4 * width, width, kind=BF16),
             shape(2, width),
         ],
-        compiler_params=params(28),
+        compiler_params=params(30),
         cost_estimate=pl.CostEstimate(
             flops=14 * unit, bytes_accessed=20 * total_rows * width, transcendentals=0
         ),

time: 138 us -> 135 us (0.978)
  waiting for transfers between devices: 42.5 us -> 40.5 us
  Pallas kernels: 41.7 us -> 40.3 us
    ppermute x39, waiting for transfers between devices: 42.5 us -> 40.5 us  [swap(): return lax.ppermute(values, axis, [(i, i ^ bit) for i in range(size)])]
    pallas_call x3 -> x2, Pallas kernels: 6.98 us -> 5.79 us  [per_device(): pl.pallas_call(functools.partial(unpack_kernel, (edge_scale, node_scale),...]
    pallas_call x2 -> x3, Pallas kernels: 13.1 us -> 13.6 us  [per_device(): pl.pallas_call(functools.partial(forward_kernel, len(chosen), first, last...]
  transfers between devices with their start and end apart: 39 -> 39, of which waited for: 18 -> 19; matrix products, arithmetic and copies ran while one was open for 2% -> 2% of each run, Pallas kernels for 22% -> 23%
where the time goes in v4:
time: 135 us
  starting transfers between devices  41.9 us (31%)
  waiting for transfers between devices  40.5 us (30%)
  Pallas kernels  40.3 us (30%)
  local copies, waits for them, and re-layouts  7.66 us (6%)
  other arithmetic  3.15 us (2%)
  between operations  1.39 us (1%)
    ppermute x39, starting transfers between devices, swap(): return lax.ppermute(values, axis, [(i, i ^ bit) for i in range(size)])  41.9 us
    ppermute x39, waiting for transfers between devices, swap(): return lax.ppermute(values, axis, [(i, i ^ bit) for i in range(size)])  40.5 us
    pallas_call x1, Pallas kernels, per_device(): pl.pallas_call(functools.partial(backward_kernel, len(pieces)), grid_spec...  16 us
    pallas_call x3, Pallas kernels, per_device(): pl.pallas_call(functools.partial(forward_kernel, len(chosen), first, last...  13.6 us
    unnamed x40, local copies, waits for them, and re-layouts  7.04 us
    pallas_call x2, Pallas kernels, per_device(): pl.pallas_call(functools.partial(unpack_kernel, (edge_scale, node_scale),...  5.79 us
    pallas_call x1, Pallas kernels, per_device(): pl.pallas_call(lift_kernel, grid=(peers,), in_specs=[owned, whole(peers,...  4.84 us
  transfers between devices with their start and end apart: 39, of which 19 were waited for; matrix products, arithmetic and copies ran while one was open for 2% of the time, Pallas kernels for 23%

profile of v4, /device:TPU:0, one launch (start us, length us, event | category | flops | bytes accessed | tf_op | source)
XLA Modules:
  0.0 135.2 jit_solution(17650777623558010232)
XLA Ops:
  2.3 3.1 %collective-permute-start.2 = (bf16[272,512]{1,0:T(8,128)(2,1)S(1)}, bf16[272,512]{1,0:T(8,128)(2,1)S(1)}, u32[]{:S(2)}, u32[]{:S(2)}) collective-permute-start(bf16[272,512]{1,0:T(8,128)(2,1)S(1)} %pack.1), channel_id=1, source_target_pairs={{0,2},{1,3},{2,0},{3,1},{4,6},{5,7},{6,4},{7,5},{8,10},{9,11},{10,... | collective-permute-start | bytes 835592 | tf_op jit(solution)/shard_map/ppermute | solution.py:358
  5.4 2.6 %collective-permute-start.1 = (bf16[272,512]{1,0:T(8,128)(2,1)S(1)}, bf16[272,512]{1,0:T(8,128)(2,1)S(1)}, u32[]{:S(2)}, u32[]{:S(2)}) collective-permute-start(bf16[272,512]{1,0:T(8,128)(2,1)S(1)} %pack.1), channel_id=1, source_target_pairs={{0,4},{1,5},{2,6},{3,7},{4,0},{5,1},{6,2},{7,3},{8,12},{9,13},{10,... | collective-permute-start | bytes 835592 | tf_op jit(solution)/shard_map/ppermute | solution.py:358
  13.5 4.8 %lift.1.refs_6_.refs_8_ = f32[8,256,512]{2,1,0:T(8,128)S(1)} custom-call(bf16[8,256,512]{2,1,0:T(8,128)(2,1)S(1)} %bitcast.75, s32[8,256]{1,0:T(8,128)S(1)} %bitcast.60, bf16[256,512]{1,0:T(8,128)(2,1)S(1)} %bitcast.40, bf16[1536,512]{1,0:T(8,128)(2,1)S(1)} %copy-done, f32[1,512]{1,0:T(1,128)S(1)} %bitcast.80), custom_call_target="tpu_custom_call" | custom-call | flops 2684354560 | bytes 6291456 | tf_op jit(solution)/shard_map/lift/pallas_call | solution.py:579
  18.4 2.1 %collective-permute-done.1 = bf16[272,512]{1,0:T(8,128)(2,1)S(1)} collective-permute-done((bf16[272,512]{1,0:T(8,128)(2,1)S(1)}, bf16[272,512]{1,0:T(8,128)(2,1)S(1)}, u32[]{:S(2)}, u32[]{:S(2)}) %collective-permute-start.1) | collective-permute-done | bytes 278560 | tf_op jit(solution)/shard_map/ppermute | solution.py:358
  21.5 3.0 %forward_0.1 = (bf16[8,256,512]{2,1,0:T(8,128)(2,1)S(1)}, bf16[8,256,512]{2,1,0:T(8,128)(2,1)S(1)}, bf16[8,256,512]{2,1,0:T(8,128)(2,1)S(1)}, f32[8,256,1]{2,1,0:T(8,128)S(1)}, f32[256,512]{1,0:T(8,128)S(1)}) custom-call(s32[2]{0:T(128)S(1)} %get-tuple-element.233.refs_0_, s32[8]{0:T(128)S(1)} %bitcast.69, s32[32]{0:T(128)S(1)} %fusion.18.refs_2_, ...), custom_call_target="tpu_custom_call" | custom-call | flops 2147483648 | bytes 8388608 | tf_op jit(solution)/shard_map/forward_0/pallas_call | solution.py:677
  24.6 4.9 %forward_2.1 = (bf16[8,256,512]{2,1,0:T(8,128)(2,1)S(1)}, bf16[8,256,512]{2,1,0:T(8,128)(2,1)S(1)}, bf16[8,256,512]{2,1,0:T(8,128)(2,1)S(1)}, f32[8,256,1]{2,1,0:T(8,128)S(1)}, f32[256,512]{1,0:T(8,128)S(1)}) custom-call(s32[4]{0:T(128)S(1)} %slice.180.refs_0_, ...), custom_call_target="tpu_custom_call", output_to_operand_aliasing={{0}: (14, {}), {1}: (15, {}), {2}: (16, {}), {3}: (17, {})} | custom-call | flops 2147483648 | bytes 8388608 | tf_op jit(solution)/shard_map/forward_2/pallas_call | solution.py:677
  31.3 5.7 %forward_6.1 = (bf16[8,256,512]{2,1,0:T(8,128)(2,1)S(1)}, bf16[8,256,512]{2,1,0:T(8,128)(2,1)S(1)}, bf16[8,256,512]{2,1,0:T(8,128)(2,1)S(1)}, f32[8,256,1]{2,1,0...) custom-call(s32[2]{0:T(128)S(1)} %get-tuple-element.232.refs_0_, ...), custom_call_target="tpu_custom_call", output_to_operand_aliasing={{0}: (12, {}), {1}: (13, {}), {2}: (14, {}), {3}: (15, {})} | custom-call | flops 2147483648 | bytes 8388608 | tf_op jit(solution)/shard_map/forward_6/pallas_call | solution.py:677
  40.1 16.0 %backward.1 = (bf16[8,256,512]{2,1,0:T(8,128)(2,1)}, bf16[2,4,256,512]{3,2,1,0:T(8,128)(2,1)S(1)}, f32[256,512]{1,0:T(8,128)S(1)}, bf16[2048,512]{1,0:T(8,128)(2,1)S(1)}, f32[2,512]{1,0:T(2,128)S(1)}) custom-call(s32[8]{0:T(128)S(1)} %iota_xor_fusion.refs_0_, s32[8]{0:T(128)S(1)} %bitcast.72, s32[32]{0:T(128)S(1)} %fusion.17.refs_2_.refs_0_, ...), custom_call_target="tpu_custom_call" | custom-call | flops 7516192768 | bytes 20971520 | tf_op jit(solution)/shard_map/backward/pallas_call | solution.py:705
  57.3 3.2 %collective-permute-done.10 = f32[4,512]{1,0:T(4,128)S(1)} collective-permute-done((f32[4,512]{1,0:T(4,128)S(1)}, f32[4,512]{1,0:T(4,128)S(1)}, u32[]{:S(2)}, u32[]{:S(2)}) %collective-permute-start.10) | collective-permute-done | bytes 8224 | tf_op jit(solution)/shard_map/ppermute | solution.py:358
  65.8 4.5 %collective-permute-done.15 = f32[4,512]{1,0:T(4,128)S(1)} collective-permute-done((f32[4,512]{1,0:T(4,128)S(1)}, f32[4,512]{1,0:T(4,128)S(1)}, u32[]{:S(2)}, u32[]{:S(2)}) %collective-permute-start.15) | collective-permute-done | bytes 8224 | tf_op jit(solution)/shard_map/ppermute | solution.py:358
  77.7 3.1 %collective-permute-done.19 = f32[4,512]{1,0:T(4,128)S(1)} collective-permute-done((f32[4,512]{1,0:T(4,128)S(1)}, f32[4,512]{1,0:T(4,128)S(1)}, u32[]{:S(2)}, u32[]{:S(2)}) %collective-permute-start.19) | collective-permute-done | bytes 8224 | tf_op jit(solution)/shard_map/ppermute | solution.py:358
  80.8 3.1 %collective-permute-done.21 = bf16[128,512]{1,0:T(8,128)(2,1)S(1)} collective-permute-done((bf16[128,512]{1,0:T(8,128)(2,1)S(1)}, bf16[128,512]{1,0:T(8,128)(2,1)S(1)}, u32[]{:S(2)}, u32[]{:S(2)}) %collective-permute-start.21) | collective-permute-done | bytes 131104 | tf_op jit(solution)/shard_map/ppermute | solution.py:358
  86.9 2.2 %collective-permute-start.24 = (bf16[112,512]{1,0:T(8,128)(2,1)S(1)}, bf16[112,512]{1,0:T(8,128)(2,1)S(1)}, u32[]{:S(2)}, u32[]{:S(2)}) collective-permute-start(bf16[112,512]{1,0:T(8,128)(2,1)S(1)} %pad_maximum_fusion.9), channel_id=1, source_target_pairs={{0,6},{1,7},{2,4},{3,5},{4,2},{5,3},{6,0},{7,1},{8,14},{9,15},{10,... | collective-permute-start | bytes 344072 | tf_op jit(solution)/shard_map/ppermute | solution.py:358
  90.7 4.1 %collective-permute-done.23 = bf16[112,512]{1,0:T(8,128)(2,1)S(1)} collective-permute-done((bf16[112,512]{1,0:T(8,128)(2,1)S(1)}, bf16[112,512]{1,0:T(8,128)(2,1)S(1)}, u32[]{:S(2)}, u32[]{:S(2)}) %collective-permute-start.23) | collective-permute-done | bytes 114720 | tf_op jit(solution)/shard_map/ppermute | solution.py:358
  94.9 4.0 %collective-permute-start.28 = (f32[4,512]{1,0:T(4,128)S(1)}, f32[4,512]{1,0:T(4,128)S(1)}, u32[]{:S(2)}, u32[]{:S(2)}) collective-permute-start(f32[4,512]{1,0:T(4,128)S(1)} %add.112), channel_id=1, source_target_pairs={{0,4},{1,5},{2,6},{3,7},{4,0},{5,1},{6,2},{7,3},{8,12},{9,13},{10,... | collective-permute-start | bytes 24584 | tf_op jit(solution)/shard_map/ppermute | solution.py:358
  98.9 2.5 %collective-permute-start.27 = (bf16[112,512]{1,0:T(8,128)(2,1)S(1)}, bf16[112,512]{1,0:T(8,128)(2,1)S(1)}, u32[]{:S(2)}, u32[]{:S(2)}) collective-permute-start(bf16[112,512]{1,0:T(8,128)(2,1)S(1)} %add_convert_fusion.13), channel_id=1, source_target_pairs={{0,4},{1,5},{2,6},{3,7},{4,0},{5,1},{6,2},{7,3},{8,12},{9,13},{10,... | collective-permute-start | bytes 344072 | tf_op jit(solution)/shard_map/ppermute | solution.py:358
  101.4 3.5 %collective-permute-done.26 = bf16[112,512]{1,0:T(8,128)(2,1)S(1)} collective-permute-done((bf16[112,512]{1,0:T(8,128)(2,1)S(1)}, bf16[112,512]{1,0:T(8,128)(2,1)S(1)}, u32[]{:S(2)}, u32[]{:S(2)}) %collective-permute-start.26) | collective-permute-done | bytes 114720 | tf_op jit(solution)/shard_map/ppermute | solution.py:358
  106.6 4.1 %collective-permute-done.29 = bf16[112,512]{1,0:T(8,128)(2,1)S(1)} collective-permute-done((bf16[112,512]{1,0:T(8,128)(2,1)S(1)}, bf16[112,512]{1,0:T(8,128)(2,1)S(1)}, u32[]{:S(2)}, u32[]{:S(2)}) %collective-permute-start.29) | collective-permute-done | bytes 114720 | tf_op jit(solution)/shard_map/ppermute | solution.py:358
  110.9 3.4 %collective-permute-start.32 = (bf16[128,512]{1,0:T(8,128)(2,1)S(1)}, bf16[128,512]{1,0:T(8,128)(2,1)S(1)}, u32[]{:S(2)}, u32[]{:S(2)}) collective-permute-start(bf16[128,512]{1,0:T(8,128)(2,1)S(1)} %get-tuple-element.178), channel_id=1, source_target_pairs={{0,4},{1,5},{2,6},{3,7},{4,0},{5,1},{6,2},{7,3},{8,12},{9,13},{10,... | collective-permute-start | bytes 393224 | tf_op jit(solution)/shard_map/ppermute | solution.py:358
  114.3 4.3 %collective-permute-done.32 = bf16[128,512]{1,0:T(8,128)(2,1)S(1)} collective-permute-done((bf16[128,512]{1,0:T(8,128)(2,1)S(1)}, bf16[128,512]{1,0:T(8,128)(2,1)S(1)}, u32[]{:S(2)}, u32[]{:S(2)}) %collective-permute-start.32) | collective-permute-done | bytes 131104 | tf_op jit(solution)/shard_map/ppermute | solution.py:358
  120.4 1.9 %collective-permute-start.34 = (bf16[448,512]{1,0:T(8,128)(2,1)S(1)}, bf16[448,512]{1,0:T(8,128)(2,1)S(1)}, u32[]{:S(2)}, u32[]{:S(2)}) collective-permute-start(bf16[448,512]{1,0:T(8,128)(2,1)S(1)} %pad_maximum_fusion.1.refs_2_), channel_id=1, source_target_pairs={{0,16},{8,24},{16,0},{24,8},{1,17},{9,25},{17,1},{25,9},{2,18},{10... | collective-permute-start | bytes 1376264 | tf_op jit(solution)/shard_map/ppermute | solution.py:358
  123.4 2.0 %unpack_0.1 = (f32[1536,512]{1,0:T(8,128)}, f32[512,512]{1,0:T(8,128)}, f32[1024,512]{1,0:T(8,128)}, f32[512,512]{1,0:T(8,128)}) custom-call(s32[32]{0:T(128)S(1)} %fusion.17.refs_2_.refs_0_, bf16[448,512]{1,0:T(8,128)(2,1)S(1)} %pad_maximum_fusion.refs_1_, bf16[448,512]{1,0:T(8,128)(2,1)S(1)} %pad_maximum_fusion.1.refs_2_), custom_call_target="tpu_custom_call" | custom-call | bytes 2752512 | tf_op jit(solution)/shard_map/unpack_0/pallas_call | solution.py:813
  125.5 2.6 %collective-permute-done.33.refs_1_ = bf16[448,512]{1,0:T(8,128)(2,1)S(1)} collective-permute-done((bf16[448,512]{1,0:T(8,128)(2,1)S(1)}, bf16[448,512]{1,0:T(8,128)(2,1)S(1)}, u32[]{:S(2)}, u32[]{:S(2)}) %collective-permute-start.33) | collective-permute-done | bytes 458784 | tf_op jit(solution)/shard_map/ppermute | solution.py:358
  131.3 3.8 %unpack_4.1 = (f32[1536,512]{1,0:T(8,128)}, f32[512,512]{1,0:T(8,128)}, f32[1024,512]{1,0:T(8,128)}, f32[512,512]{1,0:T(8,128)}) custom-call(s32[32]{0:T(128)S(1)} %fusion.17.refs_2_.refs_0_, bf16[448,512]{1,0:T(8,128)(2,1)S(1)} %collective-permute-done.33.refs_1_, ...), custom_call_target="tpu_custom_call", output_to_operand_aliasing={{0}: (7, {}), {1}: (8, {}), {2}: (9, {}), {3}: (10, {})} | custom-call | bytes 8257536 | tf_op jit(solution)/shard_map/unpack_4/pallas_call | solution.py:813
  (155 shorter events, 39.3 us)
Async XLA Ops:
  2.3 18.1 %collective-permute-start.2 = (bf16[272,512]{1,0:T(8,128)(2,1)S(1)}, bf16[272,512]{1,0:T(8,128)(2,1)S(1)}, u32[]{:S(2)}, u32[]{:S(2)}) collective-permute-start(bf16[272,512]{1,0:T(8,128)(2,1)S(1)} %pack.1), channel_id=1, source_target_pairs={{0,2},{1,3},{2,0},{3,1},{4,6},{5,7},{6,4},{7,5},{8,10},{9,11},{10,... | collective-permute-start | bytes 835592 | tf_op jit(solution)/shard_map/ppermute | solution.py:358
  5.4 15.0 %collective-permute-start.1 = (bf16[272,512]{1,0:T(8,128)(2,1)S(1)}, bf16[272,512]{1,0:T(8,128)(2,1)S(1)}, u32[]{:S(2)}, u32[]{:S(2)}) collective-permute-start(bf16[272,512]{1,0:T(8,128)(2,1)S(1)} %pack.1), channel_id=1, source_target_pairs={{0,4},{1,5},{2,6},{3,7},{4,0},{5,1},{6,2},{7,3},{8,12},{9,13},{10,... | collective-permute-start | bytes 835592 | tf_op jit(solution)/shard_map/ppermute | solution.py:358
  8.0 12.4 %collective-permute-start = (bf16[272,512]{1,0:T(8,128)(2,1)S(1)}, bf16[272,512]{1,0:T(8,128)(2,1)S(1)}, u32[]{:S(2)}, u32[]{:S(2)}) collective-permute-start(bf16[272,512]{1,0:T(8,128)(2,1)S(1)} %pack.1), channel_id=1, source_target_pairs={{0,1},{1,0},{2,3},{3,2},{4,5},{5,4},{6,7},{7,6},{8,9},{9,8},{10,11... | collective-permute-start | bytes 835592 | tf_op jit(solution)/shard_map/ppermute | solution.py:358
  21.0 8.7 %collective-permute-start.5 = (bf16[272,512]{1,0:T(8,128)(2,1)S(1)}, bf16[272,512]{1,0:T(8,128)(2,1)S(1)}, u32[]{:S(2)}, u32[]{:S(2)}) collective-permute-start(bf16[272,512]{1,0:T(8,128)(2,1)S(1)} %collective-permute-done.1), channel_id=1, source_target_pairs={{0,2},{1,3},{2,0},{3,1},{4,6},{5,7},{6,4},{7,5},{8,10},{9,11},{10,... | collective-permute-start | bytes 835592 | tf_op jit(solution)/shard_map/ppermute | solution.py:358
  37.0 19.2 %collective-permute-start.8 = (bf16[384,512]{1,0:T(8,128)(2,1)S(1)}, bf16[384,512]{1,0:T(8,128)(2,1)S(1)}, u32[]{:S(2)}, u32[]{:S(2)}) collective-permute-start(bf16[384,512]{1,0:T(8,128)(2,1)S(1)} %get-tuple-element.206), channel_id=1, source_target_pairs={{0,16},{8,24},{16,0},{24,8},{1,17},{9,25},{17,1},{25,9},{2,18},{10... | collective-permute-start | bytes 1179656 | tf_op jit(solution)/shard_map/ppermute | solution.py:358
  38.6 17.6 %collective-permute-start.7 = (bf16[384,512]{1,0:T(8,128)(2,1)S(1)}, bf16[384,512]{1,0:T(8,128)(2,1)S(1)}, u32[]{:S(2)}, u32[]{:S(2)}) collective-permute-start(bf16[384,512]{1,0:T(8,128)(2,1)S(1)} %get-tuple-element.207), channel_id=1, source_target_pairs={{0,8},{8,0},{16,24},{24,16},{1,9},{9,1},{17,25},{25,17},{2,10},{10... | collective-permute-start | bytes 1179656 | tf_op jit(solution)/shard_map/ppermute | solution.py:358
  61.4 9.3 %collective-permute-start.14 = (bf16[384,512]{1,0:T(8,128)(2,1)S(1)}, bf16[384,512]{1,0:T(8,128)(2,1)S(1)}, u32[]{:S(2)}, u32[]{:S(2)}) collective-permute-start(bf16[384,512]{1,0:T(8,128)(2,1)S(1)} %pad_maximum_fusion.2), channel_id=1, source_target_pairs={{0,1},{1,0},{2,3},{3,2},{4,5},{5,4},{6,7},{7,6},{8,9},{9,8},{10,11... | collective-permute-start | bytes 1179656 | tf_op jit(solution)/shard_map/ppermute | solution.py:358
  61.6 8.8 %collective-permute-start.12 = (bf16[256,512]{1,0:T(8,128)(2,1)S(1)}, bf16[256,512]{1,0:T(8,128)(2,1)S(1)}, u32[]{:S(2)}, u32[]{:S(2)}) collective-permute-start(bf16[256,512]{1,0:T(8,128)(2,1)S(1)} %get-tuple-element.143), channel_id=1, source_target_pairs={{0,8},{8,0},{16,24},{24,16},{1,9},{9,1},{17,25},{25,17},{2,10},{10... | collective-permute-start | bytes 786440 | tf_op jit(solution)/shard_map/ppermute | solution.py:358
  62.1 8.3 %collective-permute-start.13 = (bf16[256,512]{1,0:T(8,128)(2,1)S(1)}, bf16[256,512]{1,0:T(8,128)(2,1)S(1)}, u32[]{:S(2)}, u32[]{:S(2)}) collective-permute-start(bf16[256,512]{1,0:T(8,128)(2,1)S(1)} %get-tuple-element.144), channel_id=1, source_target_pairs={{0,16},{8,24},{16,0},{24,8},{1,17},{9,25},{17,1},{25,9},{2,18},{10... | collective-permute-start | bytes 786440 | tf_op jit(solution)/shard_map/ppermute | solution.py:358
  62.6 8.0 %collective-permute-start.16 = (bf16[2,128,512]{2,1,0:T(8,128)(2,1)S(1)}, bf16[2,128,512]{2,1,0:T(8,128)(2,1)S(1)}, u32[]{:S(2)}, u32[]{:S(2)}) collective-permute-start(bf16[2,128,512]{2,1,0:T(8,128)(2,1)S(1)} %slice.197), channel_id=1, source_target_pairs={{0,2},{1,3},{2,0},{3,1},{4,6},{5,7},{6,4},{7,5},{8,10},{9,11},{10,... | collective-permute-start | bytes 786440 | tf_op jit(solution)/shard_map/ppermute | solution.py:358
  71.1 12.8 %collective-permute-start.20 = (bf16[2,128,512]{2,1,0:T(8,128)(2,1)S(1)}, bf16[2,128,512]{2,1,0:T(8,128)(2,1)S(1)}, u32[]{:S(2)}, u32[]{:S(2)}) collective-permute-start(bf16[2,128,512]{2,1,0:T(8,128)(2,1)S(1)} %slice.211), channel_id=1, source_target_pairs={{0,2},{1,3},{2,0},{3,1},{4,6},{5,7},{6,4},{7,5},{8,10},{9,11},{10,... | collective-permute-start | bytes 786440 | tf_op jit(solution)/shard_map/ppermute | solution.py:358
  72.9 11.1 %collective-permute-start.17 = (bf16[224,512]{1,0:T(8,128)(2,1)S(1)}, bf16[224,512]{1,0:T(8,128)(2,1)S(1)}, u32[]{:S(2)}, u32[]{:S(2)}) collective-permute-start(bf16[224,512]{1,0:T(8,128)(2,1)S(1)} %pad_maximum_fusion.3), channel_id=1, source_target_pairs={{0,16},{8,24},{16,0},{24,8},{1,17},{9,25},{17,1},{25,9},{2,18},{10... | collective-permute-start | bytes 688136 | tf_op jit(solution)/shard_map/ppermute | solution.py:358
  74.4 9.5 %collective-permute-start.18 = (bf16[224,512]{1,0:T(8,128)(2,1)S(1)}, bf16[224,512]{1,0:T(8,128)(2,1)S(1)}, u32[]{:S(2)}, u32[]{:S(2)}) collective-permute-start(bf16[224,512]{1,0:T(8,128)(2,1)S(1)} %pad_maximum_fusion.4), channel_id=1, source_target_pairs={{0,8},{8,0},{16,24},{24,16},{1,9},{9,1},{17,25},{25,17},{2,10},{10... | collective-permute-start | bytes 688136 | tf_op jit(solution)/shard_map/ppermute | solution.py:358
  75.9 8.0 %collective-permute-start.21 = (bf16[128,512]{1,0:T(8,128)(2,1)S(1)}, bf16[128,512]{1,0:T(8,128)(2,1)S(1)}, u32[]{:S(2)}, u32[]{:S(2)}) collective-permute-start(bf16[128,512]{1,0:T(8,128)(2,1)S(1)} %get-tuple-element.157), channel_id=1, source_target_pairs={{0,4},{1,5},{2,6},{3,7},{4,0},{5,1},{6,2},{7,3},{8,12},{9,13},{10,... | collective-permute-start | bytes 393224 | tf_op jit(solution)/shard_map/ppermute | solution.py:358
  86.3 8.5 %collective-permute-start.23 = (bf16[112,512]{1,0:T(8,128)(2,1)S(1)}, bf16[112,512]{1,0:T(8,128)(2,1)S(1)}, u32[]{:S(2)}, u32[]{:S(2)}) collective-permute-start(bf16[112,512]{1,0:T(8,128)(2,1)S(1)} %pad_maximum_fusion.8), channel_id=1, source_target_pairs={{0,4},{1,5},{2,6},{3,7},{4,0},{5,1},{6,2},{7,3},{8,12},{9,13},{10,... | collective-permute-start | bytes 344072 | tf_op jit(solution)/shard_map/ppermute | solution.py:358
  86.9 7.9 %collective-permute-start.24 = (bf16[112,512]{1,0:T(8,128)(2,1)S(1)}, bf16[112,512]{1,0:T(8,128)(2,1)S(1)}, u32[]{:S(2)}, u32[]{:S(2)}) collective-permute-start(bf16[112,512]{1,0:T(8,128)(2,1)S(1)} %pad_maximum_fusion.9), channel_id=1, source_target_pairs={{0,6},{1,7},{2,4},{3,5},{4,2},{5,3},{6,0},{7,1},{8,14},{9,15},{10,... | collective-permute-start | bytes 344072 | tf_op jit(solution)/shard_map/ppermute | solution.py:358
  94.9 6.5 %collective-permute-start.28 = (f32[4,512]{1,0:T(4,128)S(1)}, f32[4,512]{1,0:T(4,128)S(1)}, u32[]{:S(2)}, u32[]{:S(2)}) collective-permute-start(f32[4,512]{1,0:T(4,128)S(1)} %add.112), channel_id=1, source_target_pairs={{0,4},{1,5},{2,6},{3,7},{4,0},{5,1},{6,2},{7,3},{8,12},{9,13},{10,... | collective-permute-start | bytes 24584 | tf_op jit(solution)/shard_map/ppermute | solution.py:358
  110.8 7.9 %collective-permute-start.30 = (bf16[224,512]{1,0:T(8,128)(2,1)S(1)}, bf16[224,512]{1,0:T(8,128)(2,1)S(1)}, u32[]{:S(2)}, u32[]{:S(2)}) collective-permute-start(bf16[224,512]{1,0:T(8,128)(2,1)S(1)} %pad_maximum_fusion.5), channel_id=1, source_target_pairs={{0,16},{8,24},{16,0},{24,8},{1,17},{9,25},{17,1},{25,9},{2,18},{10... | collective-permute-start | bytes 688136 | tf_op jit(solution)/shard_map/ppermute | solution.py:358
  110.8 8.5 %collective-permute-start.31 = (bf16[224,512]{1,0:T(8,128)(2,1)S(1)}, bf16[224,512]{1,0:T(8,128)(2,1)S(1)}, u32[]{:S(2)}, u32[]{:S(2)}) collective-permute-start(bf16[224,512]{1,0:T(8,128)(2,1)S(1)} %pad_maximum_fusion.6), channel_id=1, source_target_pairs={{0,8},{8,0},{16,24},{24,16},{1,9},{9,1},{17,25},{25,17},{2,10},{10... | collective-permute-start | bytes 688136 | tf_op jit(solution)/shard_map/ppermute | solution.py:358
  110.9 7.8 %collective-permute-start.32 = (bf16[128,512]{1,0:T(8,128)(2,1)S(1)}, bf16[128,512]{1,0:T(8,128)(2,1)S(1)}, u32[]{:S(2)}, u32[]{:S(2)}) collective-permute-start(bf16[128,512]{1,0:T(8,128)(2,1)S(1)} %get-tuple-element.178), channel_id=1, source_target_pairs={{0,4},{1,5},{2,6},{3,7},{4,0},{5,1},{6,2},{7,3},{8,12},{9,13},{10,... | collective-permute-start | bytes 393224 | tf_op jit(solution)/shard_map/ppermute | solution.py:358
  119.5 8.5 %collective-permute-start.33 = (bf16[448,512]{1,0:T(8,128)(2,1)S(1)}, bf16[448,512]{1,0:T(8,128)(2,1)S(1)}, u32[]{:S(2)}, u32[]{:S(2)}) collective-permute-start(bf16[448,512]{1,0:T(8,128)(2,1)S(1)} %pad_maximum_fusion.refs_1_), channel_id=1, source_target_pairs={{0,8},{8,0},{16,24},{24,16},{1,9},{9,1},{17,25},{25,17},{2,10},{10... | collective-permute-start | bytes 1376264 | tf_op jit(solution)/shard_map/ppermute | solution.py:358
  120.4 8.5 %collective-permute-start.34 = (bf16[448,512]{1,0:T(8,128)(2,1)S(1)}, bf16[448,512]{1,0:T(8,128)(2,1)S(1)}, u32[]{:S(2)}, u32[]{:S(2)}) collective-permute-start(bf16[448,512]{1,0:T(8,128)(2,1)S(1)} %pad_maximum_fusion.1.refs_2_), channel_id=1, source_target_pairs={{0,16},{8,24},{16,0},{24,8},{1,17},{9,25},{17,1},{25,9},{2,18},{10... | collective-permute-start | bytes 1376264 | tf_op jit(solution)/shard_map/ppermute | solution.py:358
  122.3 6.5 %collective-permute-start.35 = (bf16[448,512]{1,0:T(8,128)(2,1)S(1)}, bf16[448,512]{1,0:T(8,128)(2,1)S(1)}, u32[]{:S(2)}, u32[]{:S(2)}) collective-permute-start(bf16[448,512]{1,0:T(8,128)(2,1)S(1)} %pad_maximum_fusion.refs_1_), channel_id=1, source_target_pairs={{0,1},{1,0},{2,3},{3,2},{4,5},{5,4},{6,7},{7,6},{8,9},{9,8},{10,11... | collective-permute-start | bytes 1376264 | tf_op jit(solution)/shard_map/ppermute | solution.py:358
  122.3 6.5 %collective-permute-start.36 = (bf16[448,512]{1,0:T(8,128)(2,1)S(1)}, bf16[448,512]{1,0:T(8,128)(2,1)S(1)}, u32[]{:S(2)}, u32[]{:S(2)}) collective-permute-start(bf16[448,512]{1,0:T(8,128)(2,1)S(1)} %pad_maximum_fusion.1.refs_2_), channel_id=1, source_target_pairs={{0,1},{1,0},{2,3},{3,2},{4,5},{5,4},{6,7},{7,6},{8,9},{9,8},{10,11... | collective-permute-start | bytes 1376264 | tf_op jit(solution)/shard_map/ppermute | solution.py:358
  (35 other events, 170.2 us)

commit v5 on v4

--- a/solution.py
+++ b/solution.py
@@ -445,8 +445,9 @@
         (got.astype(F32) for got in (got_1, got_2, got_3)),
         join(parts[0][0], parts[1][0]).astype(F32),
     ).astype(BF16)
-    got_1, got_2, got_small = exchange((kept, "dev", 2), (kept, "dev", 4), (small, "dev", 4))
-    (got_3,) = exchange((got_2, "dev", 2))
+    got_1, got_2, got_3, got_small = exchange(
+        (kept, "dev", 2), (kept, "dev", 4), (kept, "dev", 6), (small, "dev", 4)
+    )
     small = small + got_small
 
     side_a, side_b = join(kept, got_1), join(got_2, got_3)

time: 135 us -> 137 us (1.015)
  waiting for transfers between devices: 40.5 us -> 41.9 us
    ppermute x39, waiting for transfers between devices: 40.5 us -> 41.9 us  [swap(): return lax.ppermute(values, axis, [(i, i ^ bit) for i in range(size)])]
    unnamed x40 -> x42, local copies, waits for them, and re-layouts: 7.04 us -> 7.06 us
  transfers between devices with their start and end apart: 39 -> 39, of which waited for: 19 -> 20; matrix products, arithmetic and copies ran while one was open for 2% -> 2% of each run, Pallas kernels for 23% -> 23%
where the time goes in v5:
time: 137 us
  waiting for transfers between devices  41.9 us (31%)
  starting transfers between devices  41.8 us (31%)
  Pallas kernels  40.3 us (29%)
  local copies, waits for them, and re-layouts  7.7 us (6%)
  other arithmetic  3.11 us (2%)
  between operations  1.39 us (1%)
    ppermute x39, waiting for transfers between devices, swap(): return lax.ppermute(values, axis, [(i, i ^ bit) for i in range(size)])  41.9 us
    ppermute x39, starting transfers between devices, swap(): return lax.ppermute(values, axis, [(i, i ^ bit) for i in range(size)])  41.8 us
    pallas_call x1, Pallas kernels, per_device(): pl.pallas_call(functools.partial(backward_kernel, len(pieces)), grid_spec...  16 us
    pallas_call x3, Pallas kernels, per_device(): pl.pallas_call(functools.partial(forward_kernel, len(chosen), first, last...  13.6 us
    unnamed x42, local copies, waits for them, and re-layouts  7.06 us
    pallas_call x2, Pallas kernels, per_device(): pl.pallas_call(functools.partial(unpack_kernel, (edge_scale, node_scale),...  5.79 us
    pallas_call x1, Pallas kernels, per_device(): pl.pallas_call(lift_kernel, grid=(peers,), in_specs=[owned, whole(peers,...  4.84 us
  transfers between devices with their start and end apart: 39, of which 20 were waited for; matrix products, arithmetic and copies ran while one was open for 2% of the time, Pallas kernels for 23%

profile of v5, /device:TPU:0, one launch (start us, length us, event | category | flops | bytes accessed | tf_op | source)
XLA Modules:
  0.0 136.6 jit_solution(12333540490954569777)
XLA Ops:
  2.3 3.1 %collective-permute-start.2 = (bf16[272,512]{1,0:T(8,128)(2,1)S(1)}, bf16[272,512]{1,0:T(8,128)(2,1)S(1)}, u32[]{:S(2)}, u32[]{:S(2)}) collective-permute-start(bf16[272,512]{1,0:T(8,128)(2,1)S(1)} %pack.1), channel_id=1, source_target_pairs={{0,2},{1,3},{2,0},{3,1},{4,6},{5,7},{6,4},{7,5},{8,10},{9,11},{10,... | collective-permute-start | bytes 835592 | tf_op jit(solution)/shard_map/ppermute | solution.py:358
  5.4 2.6 %collective-permute-start.1 = (bf16[272,512]{1,0:T(8,128)(2,1)S(1)}, bf16[272,512]{1,0:T(8,128)(2,1)S(1)}, u32[]{:S(2)}, u32[]{:S(2)}) collective-permute-start(bf16[272,512]{1,0:T(8,128)(2,1)S(1)} %pack.1), channel_id=1, source_target_pairs={{0,4},{1,5},{2,6},{3,7},{4,0},{5,1},{6,2},{7,3},{8,12},{9,13},{10,... | collective-permute-start | bytes 835592 | tf_op jit(solution)/shard_map/ppermute | solution.py:358
  13.5 4.8 %lift.1.refs_6_.refs_8_ = f32[8,256,512]{2,1,0:T(8,128)S(1)} custom-call(bf16[8,256,512]{2,1,0:T(8,128)(2,1)S(1)} %bitcast.75, s32[8,256]{1,0:T(8,128)S(1)} %bitcast.60, bf16[256,512]{1,0:T(8,128)(2,1)S(1)} %bitcast.40, bf16[1536,512]{1,0:T(8,128)(2,1)S(1)} %copy-done, f32[1,512]{1,0:T(1,128)S(1)} %bitcast.80), custom_call_target="tpu_custom_call" | custom-call | flops 2684354560 | bytes 6291456 | tf_op jit(solution)/shard_map/lift/pallas_call | solution.py:580
  18.4 2.1 %collective-permute-done.1 = bf16[272,512]{1,0:T(8,128)(2,1)S(1)} collective-permute-done((bf16[272,512]{1,0:T(8,128)(2,1)S(1)}, bf16[272,512]{1,0:T(8,128)(2,1)S(1)}, u32[]{:S(2)}, u32[]{:S(2)}) %collective-permute-start.1) | collective-permute-done | bytes 278560 | tf_op jit(solution)/shard_map/ppermute | solution.py:358
  21.5 3.0 %forward_0.1 = (bf16[8,256,512]{2,1,0:T(8,128)(2,1)S(1)}, bf16[8,256,512]{2,1,0:T(8,128)(2,1)S(1)}, bf16[8,256,512]{2,1,0:T(8,128)(2,1)S(1)}, f32[8,256,1]{2,1,0:T(8,128)S(1)}, f32[256,512]{1,0:T(8,128)S(1)}) custom-call(s32[2]{0:T(128)S(1)} %get-tuple-element.237.refs_0_, s32[8]{0:T(128)S(1)} %bitcast.69, s32[32]{0:T(128)S(1)} %fusion.18.refs_2_, ...), custom_call_target="tpu_custom_call" | custom-call | flops 2147483648 | bytes 8388608 | tf_op jit(solution)/shard_map/forward_0/pallas_call | solution.py:678
  24.6 4.9 %forward_2.1 = (bf16[8,256,512]{2,1,0:T(8,128)(2,1)S(1)}, bf16[8,256,512]{2,1,0:T(8,128)(2,1)S(1)}, bf16[8,256,512]{2,1,0:T(8,128)(2,1)S(1)}, f32[8,256,1]{2,1,0:T(8,128)S(1)}, f32[256,512]{1,0:T(8,128)S(1)}) custom-call(s32[4]{0:T(128)S(1)} %slice.180.refs_0_, ...), custom_call_target="tpu_custom_call", output_to_operand_aliasing={{0}: (14, {}), {1}: (15, {}), {2}: (16, {}), {3}: (17, {})} | custom-call | flops 2147483648 | bytes 8388608 | tf_op jit(solution)/shard_map/forward_2/pallas_call | solution.py:678
  31.3 5.7 %forward_6.1 = (bf16[8,256,512]{2,1,0:T(8,128)(2,1)S(1)}, bf16[8,256,512]{2,1,0:T(8,128)(2,1)S(1)}, bf16[8,256,512]{2,1,0:T(8,128)(2,1)S(1)}, f32[8,256,1]{2,1,0...) custom-call(s32[2]{0:T(128)S(1)} %get-tuple-element.236.refs_0_, ...), custom_call_target="tpu_custom_call", output_to_operand_aliasing={{0}: (12, {}), {1}: (13, {}), {2}: (14, {}), {3}: (15, {})} | custom-call | flops 2147483648 | bytes 8388608 | tf_op jit(solution)/shard_map/forward_6/pallas_call | solution.py:678
  40.1 16.0 %backward.1 = (bf16[8,256,512]{2,1,0:T(8,128)(2,1)}, bf16[2,4,256,512]{3,2,1,0:T(8,128)(2,1)S(1)}, f32[256,512]{1,0:T(8,128)S(1)}, bf16[2048,512]{1,0:T(8,128)(2,1)S(1)}, f32[2,512]{1,0:T(2,128)S(1)}) custom-call(s32[8]{0:T(128)S(1)} %iota_xor_fusion.refs_0_, s32[8]{0:T(128)S(1)} %bitcast.72, s32[32]{0:T(128)S(1)} %fusion.17.refs_2_.refs_0_, ...), custom_call_target="tpu_custom_call" | custom-call | flops 7516192768 | bytes 20971520 | tf_op jit(solution)/shard_map/backward/pallas_call | solution.py:706
  57.3 3.2 %collective-permute-done.10 = f32[4,512]{1,0:T(4,128)S(1)} collective-permute-done((f32[4,512]{1,0:T(4,128)S(1)}, f32[4,512]{1,0:T(4,128)S(1)}, u32[]{:S(2)}, u32[]{:S(2)}) %collective-permute-start.10) | collective-permute-done | bytes 8224 | tf_op jit(solution)/shard_map/ppermute | solution.py:358
  65.9 4.4 %collective-permute-done.15 = f32[4,512]{1,0:T(4,128)S(1)} collective-permute-done((f32[4,512]{1,0:T(4,128)S(1)}, f32[4,512]{1,0:T(4,128)S(1)}, u32[]{:S(2)}, u32[]{:S(2)}) %collective-permute-start.15) | collective-permute-done | bytes 8224 | tf_op jit(solution)/shard_map/ppermute | solution.py:358
  78.0 3.1 %collective-permute-done.19 = f32[4,512]{1,0:T(4,128)S(1)} collective-permute-done((f32[4,512]{1,0:T(4,128)S(1)}, f32[4,512]{1,0:T(4,128)S(1)}, u32[]{:S(2)}, u32[]{:S(2)}) %collective-permute-start.19) | collective-permute-done | bytes 8224 | tf_op jit(solution)/shard_map/ppermute | solution.py:358
  81.1 3.0 %collective-permute-done.21 = bf16[128,512]{1,0:T(8,128)(2,1)S(1)} collective-permute-done((bf16[128,512]{1,0:T(8,128)(2,1)S(1)}, bf16[128,512]{1,0:T(8,128)(2,1)S(1)}, u32[]{:S(2)}, u32[]{:S(2)}) %collective-permute-start.21) | collective-permute-done | bytes 131104 | tf_op jit(solution)/shard_map/ppermute | solution.py:358
  87.1 2.2 %collective-permute-start.24 = (bf16[112,512]{1,0:T(8,128)(2,1)S(1)}, bf16[112,512]{1,0:T(8,128)(2,1)S(1)}, u32[]{:S(2)}, u32[]{:S(2)}) collective-permute-start(bf16[112,512]{1,0:T(8,128)(2,1)S(1)} %pad_maximum_fusion.8), channel_id=1, source_target_pairs={{0,6},{1,7},{2,4},{3,5},{4,2},{5,3},{6,0},{7,1},{8,14},{9,15},{10,... | collective-permute-start | bytes 344072 | tf_op jit(solution)/shard_map/ppermute | solution.py:358
  91.0 4.0 %collective-permute-done.23 = bf16[112,512]{1,0:T(8,128)(2,1)S(1)} collective-permute-done((bf16[112,512]{1,0:T(8,128)(2,1)S(1)}, bf16[112,512]{1,0:T(8,128)(2,1)S(1)}, u32[]{:S(2)}, u32[]{:S(2)}) %collective-permute-start.23) | collective-permute-done | bytes 114720 | tf_op jit(solution)/shard_map/ppermute | solution.py:358
  95.1 2.4 %collective-permute-start.29 = (f32[4,512]{1,0:T(4,128)S(1)}, f32[4,512]{1,0:T(4,128)S(1)}, u32[]{:S(2)}, u32[]{:S(2)}) collective-permute-start(f32[4,512]{1,0:T(4,128)S(1)} %add.112), channel_id=1, source_target_pairs={{0,4},{1,5},{2,6},{3,7},{4,0},{5,1},{6,2},{7,3},{8,12},{9,13},{10,... | collective-permute-start | bytes 24584 | tf_op jit(solution)/shard_map/ppermute | solution.py:358
  98.7 2.8 %collective-permute-start.27 = (bf16[112,512]{1,0:T(8,128)(2,1)S(1)}, bf16[112,512]{1,0:T(8,128)(2,1)S(1)}, u32[]{:S(2)}, u32[]{:S(2)}) collective-permute-start(bf16[112,512]{1,0:T(8,128)(2,1)S(1)} %add_convert_fusion.13), channel_id=1, source_target_pairs={{0,4},{1,5},{2,6},{3,7},{4,0},{5,1},{6,2},{7,3},{8,12},{9,13},{10,... | collective-permute-start | bytes 344072 | tf_op jit(solution)/shard_map/ppermute | solution.py:358
  102.3 7.0 %collective-permute-done.27 = bf16[112,512]{1,0:T(8,128)(2,1)S(1)} collective-permute-done((bf16[112,512]{1,0:T(8,128)(2,1)S(1)}, bf16[112,512]{1,0:T(8,128)(2,1)S(1)}, u32[]{:S(2)}, u32[]{:S(2)}) %collective-permute-start.27) | collective-permute-done | bytes 114720 | tf_op jit(solution)/shard_map/ppermute | solution.py:358
  109.3 2.8 %collective-permute-start.32 = (bf16[128,512]{1,0:T(8,128)(2,1)S(1)}, bf16[128,512]{1,0:T(8,128)(2,1)S(1)}, u32[]{:S(2)}, u32[]{:S(2)}) collective-permute-start(bf16[128,512]{1,0:T(8,128)(2,1)S(1)} %get-tuple-element.182), channel_id=1, source_target_pairs={{0,4},{1,5},{2,6},{3,7},{4,0},{5,1},{6,2},{7,3},{8,12},{9,13},{10,... | collective-permute-start | bytes 393224 | tf_op jit(solution)/shard_map/ppermute | solution.py:358
  115.2 4.0 %collective-permute-done.30 = bf16[224,512]{1,0:T(8,128)(2,1)S(1)} collective-permute-done((bf16[224,512]{1,0:T(8,128)(2,1)S(1)}, bf16[224,512]{1,0:T(8,128)(2,1)S(1)}, u32[]{:S(2)}, u32[]{:S(2)}) %collective-permute-start.30) | collective-permute-done | bytes 229408 | tf_op jit(solution)/shard_map/ppermute | solution.py:358
  119.5 2.2 %collective-permute-start.33 = (bf16[448,512]{1,0:T(8,128)(2,1)S(1)}, bf16[448,512]{1,0:T(8,128)(2,1)S(1)}, u32[]{:S(2)}, u32[]{:S(2)}) collective-permute-start(bf16[448,512]{1,0:T(8,128)(2,1)S(1)} %pad_maximum_fusion.refs_1_), channel_id=1, source_target_pairs={{0,8},{8,0},{16,24},{24,16},{1,9},{9,1},{17,25},{25,17},{2,10},{10... | collective-permute-start | bytes 1376264 | tf_op jit(solution)/shard_map/ppermute | solution.py:358
  123.8 2.0 %unpack_0.1 = (f32[1536,512]{1,0:T(8,128)}, f32[512,512]{1,0:T(8,128)}, f32[1024,512]{1,0:T(8,128)}, f32[512,512]{1,0:T(8,128)}) custom-call(s32[32]{0:T(128)S(1)} %fusion.17.refs_2_.refs_0_, bf16[448,512]{1,0:T(8,128)(2,1)S(1)} %pad_maximum_fusion.refs_1_, bf16[448,512]{1,0:T(8,128)(2,1)S(1)} %constant_dynamic-update-slice_fusion.refs_2_), custom_call_target="tpu_custom_call" | custom-call | bytes 2752512 | tf_op jit(solution)/shard_map/unpack_0/pallas_call | solution.py:814
  125.9 2.3 %collective-permute-done.33.refs_1_ = bf16[448,512]{1,0:T(8,128)(2,1)S(1)} collective-permute-done((bf16[448,512]{1,0:T(8,128)(2,1)S(1)}, bf16[448,512]{1,0:T(8,128)(2,1)S(1)}, u32[]{:S(2)}, u32[]{:S(2)}) %collective-permute-start.33) | collective-permute-done | bytes 458784 | tf_op jit(solution)/shard_map/ppermute | solution.py:358
  128.2 2.0 %collective-permute-done.34.refs_2_ = bf16[448,512]{1,0:T(8,128)(2,1)S(1)} collective-permute-done((bf16[448,512]{1,0:T(8,128)(2,1)S(1)}, bf16[448,512]{1,0:T(8,128)(2,1)S(1)}, u32[]{:S(2)}, u32[]{:S(2)}) %collective-permute-start.34) | collective-permute-done | bytes 458784 | tf_op jit(solution)/shard_map/ppermute | solution.py:358
  132.7 3.8 %unpack_4.1 = (f32[1536,512]{1,0:T(8,128)}, f32[512,512]{1,0:T(8,128)}, f32[1024,512]{1,0:T(8,128)}, f32[512,512]{1,0:T(8,128)}) custom-call(s32[32]{0:T(128)S(1)} %fusion.17.refs_2_.refs_0_, bf16[448,512]{1,0:T(8,128)(2,1)S(1)} %collective-permute-done.33.refs_1_, ...), custom_call_target="tpu_custom_call", output_to_operand_aliasing={{0}: (7, {}), {1}: (8, {}), {2}: (9, {}), {3}: (10, {})} | custom-call | bytes 8257536 | tf_op jit(solution)/shard_map/unpack_4/pallas_call | solution.py:814
  (157 shorter events, 41.7 us)
Async XLA Ops:
  2.3 18.1 %collective-permute-start.2 = (bf16[272,512]{1,0:T(8,128)(2,1)S(1)}, bf16[272,512]{1,0:T(8,128)(2,1)S(1)}, u32[]{:S(2)}, u32[]{:S(2)}) collective-permute-start(bf16[272,512]{1,0:T(8,128)(2,1)S(1)} %pack.1), channel_id=1, source_target_pairs={{0,2},{1,3},{2,0},{3,1},{4,6},{5,7},{6,4},{7,5},{8,10},{9,11},{10,... | collective-permute-start | bytes 835592 | tf_op jit(solution)/shard_map/ppermute | solution.py:358
  5.4 15.0 %collective-permute-start.1 = (bf16[272,512]{1,0:T(8,128)(2,1)S(1)}, bf16[272,512]{1,0:T(8,128)(2,1)S(1)}, u32[]{:S(2)}, u32[]{:S(2)}) collective-permute-start(bf16[272,512]{1,0:T(8,128)(2,1)S(1)} %pack.1), channel_id=1, source_target_pairs={{0,4},{1,5},{2,6},{3,7},{4,0},{5,1},{6,2},{7,3},{8,12},{9,13},{10,... | collective-permute-start | bytes 835592 | tf_op jit(solution)/shard_map/ppermute | solution.py:358
  8.0 12.4 %collective-permute-start = (bf16[272,512]{1,0:T(8,128)(2,1)S(1)}, bf16[272,512]{1,0:T(8,128)(2,1)S(1)}, u32[]{:S(2)}, u32[]{:S(2)}) collective-permute-start(bf16[272,512]{1,0:T(8,128)(2,1)S(1)} %pack.1), channel_id=1, source_target_pairs={{0,1},{1,0},{2,3},{3,2},{4,5},{5,4},{6,7},{7,6},{8,9},{9,8},{10,11... | collective-permute-start | bytes 835592 | tf_op jit(solution)/shard_map/ppermute | solution.py:358
  21.0 8.7 %collective-permute-start.5 = (bf16[272,512]{1,0:T(8,128)(2,1)S(1)}, bf16[272,512]{1,0:T(8,128)(2,1)S(1)}, u32[]{:S(2)}, u32[]{:S(2)}) collective-permute-start(bf16[272,512]{1,0:T(8,128)(2,1)S(1)} %collective-permute-done.1), channel_id=1, source_target_pairs={{0,2},{1,3},{2,0},{3,1},{4,6},{5,7},{6,4},{7,5},{8,10},{9,11},{10,... | collective-permute-start | bytes 835592 | tf_op jit(solution)/shard_map/ppermute | solution.py:358
  37.0 19.2 %collective-permute-start.8 = (bf16[384,512]{1,0:T(8,128)(2,1)S(1)}, bf16[384,512]{1,0:T(8,128)(2,1)S(1)}, u32[]{:S(2)}, u32[]{:S(2)}) collective-permute-start(bf16[384,512]{1,0:T(8,128)(2,1)S(1)} %get-tuple-element.210), channel_id=1, source_target_pairs={{0,16},{8,24},{16,0},{24,8},{1,17},{9,25},{17,1},{25,9},{2,18},{10... | collective-permute-start | bytes 1179656 | tf_op jit(solution)/shard_map/ppermute | solution.py:358
  38.6 17.6 %collective-permute-start.7 = (bf16[384,512]{1,0:T(8,128)(2,1)S(1)}, bf16[384,512]{1,0:T(8,128)(2,1)S(1)}, u32[]{:S(2)}, u32[]{:S(2)}) collective-permute-start(bf16[384,512]{1,0:T(8,128)(2,1)S(1)} %get-tuple-element.211), channel_id=1, source_target_pairs={{0,8},{8,0},{16,24},{24,16},{1,9},{9,1},{17,25},{25,17},{2,10},{10... | collective-permute-start | bytes 1179656 | tf_op jit(solution)/shard_map/ppermute | solution.py:358
  61.4 9.3 %collective-permute-start.14 = (bf16[384,512]{1,0:T(8,128)(2,1)S(1)}, bf16[384,512]{1,0:T(8,128)(2,1)S(1)}, u32[]{:S(2)}, u32[]{:S(2)}) collective-permute-start(bf16[384,512]{1,0:T(8,128)(2,1)S(1)} %pad_maximum_fusion.1), channel_id=1, source_target_pairs={{0,1},{1,0},{2,3},{3,2},{4,5},{5,4},{6,7},{7,6},{8,9},{9,8},{10,11... | collective-permute-start | bytes 1179656 | tf_op jit(solution)/shard_map/ppermute | solution.py:358
  61.6 8.8 %collective-permute-start.12 = (bf16[256,512]{1,0:T(8,128)(2,1)S(1)}, bf16[256,512]{1,0:T(8,128)(2,1)S(1)}, u32[]{:S(2)}, u32[]{:S(2)}) collective-permute-start(bf16[256,512]{1,0:T(8,128)(2,1)S(1)} %get-tuple-element.145), channel_id=1, source_target_pairs={{0,8},{8,0},{16,24},{24,16},{1,9},{9,1},{17,25},{25,17},{2,10},{10... | collective-permute-start | bytes 786440 | tf_op jit(solution)/shard_map/ppermute | solution.py:358
  62.1 8.3 %collective-permute-start.13 = (bf16[256,512]{1,0:T(8,128)(2,1)S(1)}, bf16[256,512]{1,0:T(8,128)(2,1)S(1)}, u32[]{:S(2)}, u32[]{:S(2)}) collective-permute-start(bf16[256,512]{1,0:T(8,128)(2,1)S(1)} %get-tuple-element.146), channel_id=1, source_target_pairs={{0,16},{8,24},{16,0},{24,8},{1,17},{9,25},{17,1},{25,9},{2,18},{10... | collective-permute-start | bytes 786440 | tf_op jit(solution)/shard_map/ppermute | solution.py:358
  62.6 8.1 %collective-permute-start.16 = (bf16[2,128,512]{2,1,0:T(8,128)(2,1)S(1)}, bf16[2,128,512]{2,1,0:T(8,128)(2,1)S(1)}, u32[]{:S(2)}, u32[]{:S(2)}) collective-permute-start(bf16[2,128,512]{2,1,0:T(8,128)(2,1)S(1)} %slice.197), channel_id=1, source_target_pairs={{0,2},{1,3},{2,0},{3,1},{4,6},{5,7},{6,4},{7,5},{8,10},{9,11},{10,... | collective-permute-start | bytes 786440 | tf_op jit(solution)/shard_map/ppermute | solution.py:358
  71.2 12.9 %collective-permute-start.20 = (bf16[2,128,512]{2,1,0:T(8,128)(2,1)S(1)}, bf16[2,128,512]{2,1,0:T(8,128)(2,1)S(1)}, u32[]{:S(2)}, u32[]{:S(2)}) collective-permute-start(bf16[2,128,512]{2,1,0:T(8,128)(2,1)S(1)} %slice.211), channel_id=1, source_target_pairs={{0,2},{1,3},{2,0},{3,1},{4,6},{5,7},{6,4},{7,5},{8,10},{9,11},{10,... | collective-permute-start | bytes 786440 | tf_op jit(solution)/shard_map/ppermute | solution.py:358
  73.0 11.1 %collective-permute-start.17 = (bf16[224,512]{1,0:T(8,128)(2,1)S(1)}, bf16[224,512]{1,0:T(8,128)(2,1)S(1)}, u32[]{:S(2)}, u32[]{:S(2)}) collective-permute-start(bf16[224,512]{1,0:T(8,128)(2,1)S(1)} %pad_maximum_fusion.2), channel_id=1, source_target_pairs={{0,16},{8,24},{16,0},{24,8},{1,17},{9,25},{17,1},{25,9},{2,18},{10... | collective-permute-start | bytes 688136 | tf_op jit(solution)/shard_map/ppermute | solution.py:358
  74.5 9.6 %collective-permute-start.18 = (bf16[224,512]{1,0:T(8,128)(2,1)S(1)}, bf16[224,512]{1,0:T(8,128)(2,1)S(1)}, u32[]{:S(2)}, u32[]{:S(2)}) collective-permute-start(bf16[224,512]{1,0:T(8,128)(2,1)S(1)} %pad_maximum_fusion.3), channel_id=1, source_target_pairs={{0,8},{8,0},{16,24},{24,16},{1,9},{9,1},{17,25},{25,17},{2,10},{10... | collective-permute-start | bytes 688136 | tf_op jit(solution)/shard_map/ppermute | solution.py:358
  76.0 8.1 %collective-permute-start.21 = (bf16[128,512]{1,0:T(8,128)(2,1)S(1)}, bf16[128,512]{1,0:T(8,128)(2,1)S(1)}, u32[]{:S(2)}, u32[]{:S(2)}) collective-permute-start(bf16[128,512]{1,0:T(8,128)(2,1)S(1)} %get-tuple-element.159), channel_id=1, source_target_pairs={{0,4},{1,5},{2,6},{3,7},{4,0},{5,1},{6,2},{7,3},{8,12},{9,13},{10,... | collective-permute-start | bytes 393224 | tf_op jit(solution)/shard_map/ppermute | solution.py:358
  86.5 8.5 %collective-permute-start.23 = (bf16[112,512]{1,0:T(8,128)(2,1)S(1)}, bf16[112,512]{1,0:T(8,128)(2,1)S(1)}, u32[]{:S(2)}, u32[]{:S(2)}) collective-permute-start(bf16[112,512]{1,0:T(8,128)(2,1)S(1)} %pad_maximum_fusion.7), channel_id=1, source_target_pairs={{0,4},{1,5},{2,6},{3,7},{4,0},{5,1},{6,2},{7,3},{8,12},{9,13},{10,... | collective-permute-start | bytes 344072 | tf_op jit(solution)/shard_map/ppermute | solution.py:358
  87.1 7.9 %collective-permute-start.24 = (bf16[112,512]{1,0:T(8,128)(2,1)S(1)}, bf16[112,512]{1,0:T(8,128)(2,1)S(1)}, u32[]{:S(2)}, u32[]{:S(2)}) collective-permute-start(bf16[112,512]{1,0:T(8,128)(2,1)S(1)} %pad_maximum_fusion.8), channel_id=1, source_target_pairs={{0,6},{1,7},{2,4},{3,5},{4,2},{5,3},{6,0},{7,1},{8,14},{9,15},{10,... | collective-permute-start | bytes 344072 | tf_op jit(solution)/shard_map/ppermute | solution.py:358
  98.7 10.6 %collective-permute-start.27 = (bf16[112,512]{1,0:T(8,128)(2,1)S(1)}, bf16[112,512]{1,0:T(8,128)(2,1)S(1)}, u32[]{:S(2)}, u32[]{:S(2)}) collective-permute-start(bf16[112,512]{1,0:T(8,128)(2,1)S(1)} %add_convert_fusion.13), channel_id=1, source_target_pairs={{0,4},{1,5},{2,6},{3,7},{4,0},{5,1},{6,2},{7,3},{8,12},{9,13},{10,... | collective-permute-start | bytes 344072 | tf_op jit(solution)/shard_map/ppermute | solution.py:358
  101.5 7.7 %collective-permute-start.28 = (bf16[112,512]{1,0:T(8,128)(2,1)S(1)}, bf16[112,512]{1,0:T(8,128)(2,1)S(1)}, u32[]{:S(2)}, u32[]{:S(2)}) collective-permute-start(bf16[112,512]{1,0:T(8,128)(2,1)S(1)} %add_convert_fusion.13), channel_id=1, source_target_pairs={{0,6},{1,7},{2,4},{3,5},{4,2},{5,3},{6,0},{7,1},{8,14},{9,15},{10,... | collective-permute-start | bytes 344072 | tf_op jit(solution)/shard_map/ppermute | solution.py:358
  112.1 7.1 %collective-permute-start.30 = (bf16[224,512]{1,0:T(8,128)(2,1)S(1)}, bf16[224,512]{1,0:T(8,128)(2,1)S(1)}, u32[]{:S(2)}, u32[]{:S(2)}) collective-permute-start(bf16[224,512]{1,0:T(8,128)(2,1)S(1)} %pad_maximum_fusion.4), channel_id=1, source_target_pairs={{0,16},{8,24},{16,0},{24,8},{1,17},{9,25},{17,1},{25,9},{2,18},{10... | collective-permute-start | bytes 688136 | tf_op jit(solution)/shard_map/ppermute | solution.py:358
  112.1 7.3 %collective-permute-start.31 = (bf16[224,512]{1,0:T(8,128)(2,1)S(1)}, bf16[224,512]{1,0:T(8,128)(2,1)S(1)}, u32[]{:S(2)}, u32[]{:S(2)}) collective-permute-start(bf16[224,512]{1,0:T(8,128)(2,1)S(1)} %pad_maximum_fusion.5), channel_id=1, source_target_pairs={{0,8},{8,0},{16,24},{24,16},{1,9},{9,1},{17,25},{25,17},{2,10},{10... | collective-permute-start | bytes 688136 | tf_op jit(solution)/shard_map/ppermute | solution.py:358
  119.5 8.7 %collective-permute-start.33 = (bf16[448,512]{1,0:T(8,128)(2,1)S(1)}, bf16[448,512]{1,0:T(8,128)(2,1)S(1)}, u32[]{:S(2)}, u32[]{:S(2)}) collective-permute-start(bf16[448,512]{1,0:T(8,128)(2,1)S(1)} %pad_maximum_fusion.refs_1_), channel_id=1, source_target_pairs={{0,8},{8,0},{16,24},{24,16},{1,9},{9,1},{17,25},{25,17},{2,10},{10... | collective-permute-start | bytes 1376264 | tf_op jit(solution)/shard_map/ppermute | solution.py:358
  121.7 8.5 %collective-permute-start.34 = (bf16[448,512]{1,0:T(8,128)(2,1)S(1)}, bf16[448,512]{1,0:T(8,128)(2,1)S(1)}, u32[]{:S(2)}, u32[]{:S(2)}) collective-permute-start(bf16[448,512]{1,0:T(8,128)(2,1)S(1)} %constant_dynamic-update-slice_fusion.refs_2_), channel_id=1, source_target_pairs={{0,16},{8,24},{16,0},{24,8},{1,17},{9,25},{17,1},{25,9},{2,18},{10... | collective-permute-start | bytes 1376264 | tf_op jit(solution)/shard_map/ppermute | solution.py:358
  122.7 7.5 %collective-permute-start.35 = (bf16[448,512]{1,0:T(8,128)(2,1)S(1)}, bf16[448,512]{1,0:T(8,128)(2,1)S(1)}, u32[]{:S(2)}, u32[]{:S(2)}) collective-permute-start(bf16[448,512]{1,0:T(8,128)(2,1)S(1)} %pad_maximum_fusion.refs_1_), channel_id=1, source_target_pairs={{0,1},{1,0},{2,3},{3,2},{4,5},{5,4},{6,7},{7,6},{8,9},{9,8},{10,11... | collective-permute-start | bytes 1376264 | tf_op jit(solution)/shard_map/ppermute | solution.py:358
  122.7 7.5 %collective-permute-start.36 = (bf16[448,512]{1,0:T(8,128)(2,1)S(1)}, bf16[448,512]{1,0:T(8,128)(2,1)S(1)}, u32[]{:S(2)}, u32[]{:S(2)}) collective-permute-start(bf16[448,512]{1,0:T(8,128)(2,1)S(1)} %constant_dynamic-update-slice_fusion.refs_2_), channel_id=1, source_target_pairs={{0,1},{1,0},{2,3},{3,2},{4,5},{5,4},{6,7},{7,6},{8,9},{9,8},{10,11... | collective-permute-start | bytes 1376264 | tf_op jit(solution)/shard_map/ppermute | solution.py:358
  (35 other events, 169.9 us)

commit v6 on v4

--- a/solution.py
+++ b/solution.py
@@ -446,13 +446,11 @@
         join(parts[0][0], parts[1][0]).astype(F32),
     ).astype(BF16)
     got_1, got_2, got_small = exchange((kept, "dev", 2), (kept, "dev", 4), (small, "dev", 4))
-    (got_3,) = exchange((got_2, "dev", 2))
+    got_3, got_late = exchange((got_2, "dev", 2), (owned_late[1], "dev", 4))
     small = small + got_small
 
     side_a, side_b = join(kept, got_1), join(got_2, got_3)
-    got_a, got_b, got_late = exchange(
-        (side_a, "grp", 2), (side_b, "grp", 1), (owned_late[1], "dev", 4)
-    )
+    got_a, got_b = exchange((side_a, "grp", 2), (side_b, "grp", 1))
     from_senders = join(owned_early[0], owned_late[0]).astype(F32) + join(
         got_early, got_late
     ).astype(F32)

time: 135 us -> 138 us (1.022)
  starting transfers between devices: 41.9 us -> 43.5 us
    ppermute x39, starting transfers between devices: 41.9 us -> 43.5 us  [swap(): return lax.ppermute(values, axis, [(i, i ^ bit) for i in range(size)])]
    unnamed x40 -> x42, local copies, waits for them, and re-layouts: 7.04 us -> 7.06 us
  transfers between devices with their start and end apart: 39 -> 39, of which waited for: 19 -> 18; matrix products, arithmetic and copies ran while one was open for 2% -> 2% of each run, Pallas kernels for 23% -> 22%
where the time goes in v6:
time: 138 us
  starting transfers between devices  43.5 us (32%)
  waiting for transfers between devices  41.6 us (30%)
  Pallas kernels  40 us (29%)
  local copies, waits for them, and re-layouts  7.7 us (6%)
  other arithmetic  3.12 us (2%)
  between operations  1.39 us (1%)
    ppermute x39, starting transfers between devices, swap(): return lax.ppermute(values, axis, [(i, i ^ bit) for i in range(size)])  43.5 us
    ppermute x39, waiting for transfers between devices, swap(): return lax.ppermute(values, axis, [(i, i ^ bit) for i in range(size)])  41.6 us
    pallas_call x1, Pallas kernels, per_device(): pl.pallas_call(functools.partial(backward_kernel, len(pieces)), grid_spec...  16 us
    pallas_call x3, Pallas kernels, per_device(): pl.pallas_call(functools.partial(forward_kernel, len(chosen), first, last...  13.3 us
    unnamed x42, local copies, waits for them, and re-layouts  7.06 us
    pallas_call x2, Pallas kernels, per_device(): pl.pallas_call(functools.partial(unpack_kernel, (edge_scale, node_scale),...  5.79 us
    pallas_call x1, Pallas kernels, per_device(): pl.pallas_call(lift_kernel, grid=(peers,), in_specs=[owned, whole(peers,...  4.84 us
  transfers between devices with their start and end apart: 39, of which 18 were waited for; matrix products, arithmetic and copies ran while one was open for 2% of the time, Pallas kernels for 22%

profile of v6, /device:TPU:0, one launch (start us, length us, event | category | flops | bytes accessed | tf_op | source)
XLA Modules:
  0.0 137.6 jit_solution(17579501888171033969)
XLA Ops:
  2.3 3.1 %collective-permute-start.2 = (bf16[272,512]{1,0:T(8,128)(2,1)S(1)}, bf16[272,512]{1,0:T(8,128)(2,1)S(1)}, u32[]{:S(2)}, u32[]{:S(2)}) collective-permute-start(bf16[272,512]{1,0:T(8,128)(2,1)S(1)} %pack.1), channel_id=1, source_target_pairs={{0,2},{1,3},{2,0},{3,1},{4,6},{5,7},{6,4},{7,5},{8,10},{9,11},{10,... | collective-permute-start | bytes 835592 | tf_op jit(solution)/shard_map/ppermute | solution.py:358
  5.4 2.6 %collective-permute-start.1 = (bf16[272,512]{1,0:T(8,128)(2,1)S(1)}, bf16[272,512]{1,0:T(8,128)(2,1)S(1)}, u32[]{:S(2)}, u32[]{:S(2)}) collective-permute-start(bf16[272,512]{1,0:T(8,128)(2,1)S(1)} %pack.1), channel_id=1, source_target_pairs={{0,4},{1,5},{2,6},{3,7},{4,0},{5,1},{6,2},{7,3},{8,12},{9,13},{10,... | collective-permute-start | bytes 835592 | tf_op jit(solution)/shard_map/ppermute | solution.py:358
  13.5 4.8 %lift.1.refs_6_.refs_8_ = f32[8,256,512]{2,1,0:T(8,128)S(1)} custom-call(bf16[8,256,512]{2,1,0:T(8,128)(2,1)S(1)} %bitcast.75, s32[8,256]{1,0:T(8,128)S(1)} %bitcast.60, bf16[256,512]{1,0:T(8,128)(2,1)S(1)} %bitcast.40, bf16[1536,512]{1,0:T(8,128)(2,1)S(1)} %copy-done, f32[1,512]{1,0:T(1,128)S(1)} %bitcast.80), custom_call_target="tpu_custom_call" | custom-call | flops 2684354560 | bytes 6291456 | tf_op jit(solution)/shard_map/lift/pallas_call | solution.py:577
  18.4 2.1 %collective-permute-done.1 = bf16[272,512]{1,0:T(8,128)(2,1)S(1)} collective-permute-done((bf16[272,512]{1,0:T(8,128)(2,1)S(1)}, bf16[272,512]{1,0:T(8,128)(2,1)S(1)}, u32[]{:S(2)}, u32[]{:S(2)}) %collective-permute-start.1) | collective-permute-done | bytes 278560 | tf_op jit(solution)/shard_map/ppermute | solution.py:358
  21.5 2.9 %forward_0.1 = (bf16[8,256,512]{2,1,0:T(8,128)(2,1)S(1)}, bf16[8,256,512]{2,1,0:T(8,128)(2,1)S(1)}, bf16[8,256,512]{2,1,0:T(8,128)(2,1)S(1)}, f32[8,256,1]{2,1,0:T(8,128)S(1)}, f32[256,512]{1,0:T(8,128)S(1)}) custom-call(s32[2]{0:T(128)S(1)} %get-tuple-element.237.refs_0_, s32[8]{0:T(128)S(1)} %bitcast.69, s32[32]{0:T(128)S(1)} %fusion.18.refs_2_, ...), custom_call_target="tpu_custom_call" | custom-call | flops 2147483648 | bytes 8388608 | tf_op jit(solution)/shard_map/forward_0/pallas_call | solution.py:675
  24.5 4.9 %forward_2.1 = (bf16[8,256,512]{2,1,0:T(8,128)(2,1)S(1)}, bf16[8,256,512]{2,1,0:T(8,128)(2,1)S(1)}, bf16[8,256,512]{2,1,0:T(8,128)(2,1)S(1)}, f32[8,256,1]{2,1,0:T(8,128)S(1)}, f32[256,512]{1,0:T(8,128)S(1)}) custom-call(s32[4]{0:T(128)S(1)} %slice.180.refs_0_, ...), custom_call_target="tpu_custom_call", output_to_operand_aliasing={{0}: (14, {}), {1}: (15, {}), {2}: (16, {}), {3}: (17, {})} | custom-call | flops 2147483648 | bytes 8388608 | tf_op jit(solution)/shard_map/forward_2/pallas_call | solution.py:675
  31.3 5.5 %forward_6.1 = (bf16[8,256,512]{2,1,0:T(8,128)(2,1)S(1)}, bf16[8,256,512]{2,1,0:T(8,128)(2,1)S(1)}, bf16[8,256,512]{2,1,0:T(8,128)(2,1)S(1)}, f32[8,256,1]{2,1,0...) custom-call(s32[2]{0:T(128)S(1)} %get-tuple-element.236.refs_0_, ...), custom_call_target="tpu_custom_call", output_to_operand_aliasing={{0}: (12, {}), {1}: (13, {}), {2}: (14, {}), {3}: (15, {})} | custom-call | flops 2147483648 | bytes 8388608 | tf_op jit(solution)/shard_map/forward_6/pallas_call | solution.py:675
  39.9 16.0 %backward.1 = (bf16[8,256,512]{2,1,0:T(8,128)(2,1)}, bf16[2,4,256,512]{3,2,1,0:T(8,128)(2,1)S(1)}, f32[256,512]{1,0:T(8,128)S(1)}, bf16[2048,512]{1,0:T(8,128)(2,1)S(1)}, f32[2,512]{1,0:T(2,128)S(1)}) custom-call(s32[8]{0:T(128)S(1)} %iota_xor_fusion.refs_0_, s32[8]{0:T(128)S(1)} %bitcast.72, s32[32]{0:T(128)S(1)} %fusion.17.refs_2_.refs_0_, ...), custom_call_target="tpu_custom_call" | custom-call | flops 7516192768 | bytes 20971520 | tf_op jit(solution)/shard_map/backward/pallas_call | solution.py:703
  57.1 3.2 %collective-permute-done.10 = f32[4,512]{1,0:T(4,128)S(1)} collective-permute-done((f32[4,512]{1,0:T(4,128)S(1)}, f32[4,512]{1,0:T(4,128)S(1)}, u32[]{:S(2)}, u32[]{:S(2)}) %collective-permute-start.10) | collective-permute-done | bytes 8224 | tf_op jit(solution)/shard_map/ppermute | solution.py:358
  65.8 4.3 %collective-permute-done.15 = f32[4,512]{1,0:T(4,128)S(1)} collective-permute-done((f32[4,512]{1,0:T(4,128)S(1)}, f32[4,512]{1,0:T(4,128)S(1)}, u32[]{:S(2)}, u32[]{:S(2)}) %collective-permute-start.15) | collective-permute-done | bytes 8224 | tf_op jit(solution)/shard_map/ppermute | solution.py:358
  78.0 3.1 %collective-permute-done.19 = f32[4,512]{1,0:T(4,128)S(1)} collective-permute-done((f32[4,512]{1,0:T(4,128)S(1)}, f32[4,512]{1,0:T(4,128)S(1)}, u32[]{:S(2)}, u32[]{:S(2)}) %collective-permute-start.19) | collective-permute-done | bytes 8224 | tf_op jit(solution)/shard_map/ppermute | solution.py:358
  81.1 3.0 %collective-permute-done.21 = bf16[128,512]{1,0:T(8,128)(2,1)S(1)} collective-permute-done((bf16[128,512]{1,0:T(8,128)(2,1)S(1)}, bf16[128,512]{1,0:T(8,128)(2,1)S(1)}, u32[]{:S(2)}, u32[]{:S(2)}) %collective-permute-start.21) | collective-permute-done | bytes 131104 | tf_op jit(solution)/shard_map/ppermute | solution.py:358
  87.0 2.3 %collective-permute-start.24 = (bf16[112,512]{1,0:T(8,128)(2,1)S(1)}, bf16[112,512]{1,0:T(8,128)(2,1)S(1)}, u32[]{:S(2)}, u32[]{:S(2)}) collective-permute-start(bf16[112,512]{1,0:T(8,128)(2,1)S(1)} %pad_maximum_fusion.8), channel_id=1, source_target_pairs={{0,6},{1,7},{2,4},{3,5},{4,2},{5,3},{6,0},{7,1},{8,14},{9,15},{10,... | collective-permute-start | bytes 344072 | tf_op jit(solution)/shard_map/ppermute | solution.py:358
  91.0 3.9 %collective-permute-done.23 = bf16[112,512]{1,0:T(8,128)(2,1)S(1)} collective-permute-done((bf16[112,512]{1,0:T(8,128)(2,1)S(1)}, bf16[112,512]{1,0:T(8,128)(2,1)S(1)}, u32[]{:S(2)}, u32[]{:S(2)}) %collective-permute-start.23) | collective-permute-done | bytes 114720 | tf_op jit(solution)/shard_map/ppermute | solution.py:358
  95.0 2.2 %collective-permute-start.28 = (f32[4,512]{1,0:T(4,128)S(1)}, f32[4,512]{1,0:T(4,128)S(1)}, u32[]{:S(2)}, u32[]{:S(2)}) collective-permute-start(f32[4,512]{1,0:T(4,128)S(1)} %add.112), channel_id=1, source_target_pairs={{0,4},{1,5},{2,6},{3,7},{4,0},{5,1},{6,2},{7,3},{8,12},{9,13},{10,... | collective-permute-start | bytes 24584 | tf_op jit(solution)/shard_map/ppermute | solution.py:358
  97.3 2.4 %collective-permute-start.27 = (bf16[112,512]{1,0:T(8,128)(2,1)S(1)}, bf16[112,512]{1,0:T(8,128)(2,1)S(1)}, u32[]{:S(2)}, u32[]{:S(2)}) collective-permute-start(bf16[112,512]{1,0:T(8,128)(2,1)S(1)} %add_convert_fusion.13), channel_id=1, source_target_pairs={{0,4},{1,5},{2,6},{3,7},{4,0},{5,1},{6,2},{7,3},{8,12},{9,13},{10,... | collective-permute-start | bytes 344072 | tf_op jit(solution)/shard_map/ppermute | solution.py:358
  100.1 3.1 %collective-permute-done.26 = bf16[112,512]{1,0:T(8,128)(2,1)S(1)} collective-permute-done((bf16[112,512]{1,0:T(8,128)(2,1)S(1)}, bf16[112,512]{1,0:T(8,128)(2,1)S(1)}, u32[]{:S(2)}, u32[]{:S(2)}) %collective-permute-start.26) | collective-permute-done | bytes 114720 | tf_op jit(solution)/shard_map/ppermute | solution.py:358
  103.2 3.1 %collective-permute-start.30 = (bf16[128,512]{1,0:T(8,128)(2,1)S(1)}, bf16[128,512]{1,0:T(8,128)(2,1)S(1)}, u32[]{:S(2)}, u32[]{:S(2)}) collective-permute-start(bf16[128,512]{1,0:T(8,128)(2,1)S(1)} %get-tuple-element.178), channel_id=1, source_target_pairs={{0,4},{1,5},{2,6},{3,7},{4,0},{5,1},{6,2},{7,3},{8,12},{9,13},{10,... | collective-permute-start | bytes 393224 | tf_op jit(solution)/shard_map/ppermute | solution.py:358
  106.3 2.2 %collective-permute-start.29 = (bf16[112,512]{1,0:T(8,128)(2,1)S(1)}, bf16[112,512]{1,0:T(8,128)(2,1)S(1)}, u32[]{:S(2)}, u32[]{:S(2)}) collective-permute-start(bf16[112,512]{1,0:T(8,128)(2,1)S(1)} %collective-permute-done.27), channel_id=1, source_target_pairs={{0,2},{1,3},{2,0},{3,1},{4,6},{5,7},{6,4},{7,5},{8,10},{9,11},{10,... | collective-permute-start | bytes 344072 | tf_op jit(solution)/shard_map/ppermute | solution.py:358
  108.5 2.7 %collective-permute-done.29 = bf16[112,512]{1,0:T(8,128)(2,1)S(1)} collective-permute-done((bf16[112,512]{1,0:T(8,128)(2,1)S(1)}, bf16[112,512]{1,0:T(8,128)(2,1)S(1)}, u32[]{:S(2)}, u32[]{:S(2)}) %collective-permute-start.29) | collective-permute-done | bytes 114720 | tf_op jit(solution)/shard_map/ppermute | solution.py:358
  114.1 3.3 %collective-permute-done.31 = bf16[224,512]{1,0:T(8,128)(2,1)S(1)} collective-permute-done((bf16[224,512]{1,0:T(8,128)(2,1)S(1)}, bf16[224,512]{1,0:T(8,128)(2,1)S(1)}, u32[]{:S(2)}, u32[]{:S(2)}) %collective-permute-start.31) | collective-permute-done | bytes 229408 | tf_op jit(solution)/shard_map/ppermute | solution.py:358
  118.9 2.5 %collective-permute-start.33 = (bf16[448,512]{1,0:T(8,128)(2,1)S(1)}, bf16[448,512]{1,0:T(8,128)(2,1)S(1)}, u32[]{:S(2)}, u32[]{:S(2)}) collective-permute-start(bf16[448,512]{1,0:T(8,128)(2,1)S(1)} %pad_maximum_fusion.refs_1_), channel_id=1, source_target_pairs={{0,8},{8,0},{16,24},{24,16},{1,9},{9,1},{17,25},{25,17},{2,10},{10... | collective-permute-start | bytes 1376264 | tf_op jit(solution)/shard_map/ppermute | solution.py:358
  122.5 5.7 %collective-permute-done.33.refs_1_ = bf16[448,512]{1,0:T(8,128)(2,1)S(1)} collective-permute-done((bf16[448,512]{1,0:T(8,128)(2,1)S(1)}, bf16[448,512]{1,0:T(8,128)(2,1)S(1)}, u32[]{:S(2)}, u32[]{:S(2)}) %collective-permute-start.33) | collective-permute-done | bytes 458784 | tf_op jit(solution)/shard_map/ppermute | solution.py:358
  133.7 3.8 %unpack_4.1 = (f32[1536,512]{1,0:T(8,128)}, f32[512,512]{1,0:T(8,128)}, f32[1024,512]{1,0:T(8,128)}, f32[512,512]{1,0:T(8,128)}) custom-call(s32[32]{0:T(128)S(1)} %fusion.17.refs_2_.refs_0_, bf16[448,512]{1,0:T(8,128)(2,1)S(1)} %collective-permute-done.33.refs_1_, ...), custom_call_target="tpu_custom_call", output_to_operand_aliasing={{0}: (7, {}), {1}: (8, {}), {2}: (9, {}), {3}: (10, {})} | custom-call | bytes 8257536 | tf_op jit(solution)/shard_map/unpack_4/pallas_call | solution.py:811
  (157 shorter events, 43.6 us)
Async XLA Ops:
  2.3 18.1 %collective-permute-start.2 = (bf16[272,512]{1,0:T(8,128)(2,1)S(1)}, bf16[272,512]{1,0:T(8,128)(2,1)S(1)}, u32[]{:S(2)}, u32[]{:S(2)}) collective-permute-start(bf16[272,512]{1,0:T(8,128)(2,1)S(1)} %pack.1), channel_id=1, source_target_pairs={{0,2},{1,3},{2,0},{3,1},{4,6},{5,7},{6,4},{7,5},{8,10},{9,11},{10,... | collective-permute-start | bytes 835592 | tf_op jit(solution)/shard_map/ppermute | solution.py:358
  5.4 15.0 %collective-permute-start.1 = (bf16[272,512]{1,0:T(8,128)(2,1)S(1)}, bf16[272,512]{1,0:T(8,128)(2,1)S(1)}, u32[]{:S(2)}, u32[]{:S(2)}) collective-permute-start(bf16[272,512]{1,0:T(8,128)(2,1)S(1)} %pack.1), channel_id=1, source_target_pairs={{0,4},{1,5},{2,6},{3,7},{4,0},{5,1},{6,2},{7,3},{8,12},{9,13},{10,... | collective-permute-start | bytes 835592 | tf_op jit(solution)/shard_map/ppermute | solution.py:358
  8.0 12.4 %collective-permute-start = (bf16[272,512]{1,0:T(8,128)(2,1)S(1)}, bf16[272,512]{1,0:T(8,128)(2,1)S(1)}, u32[]{:S(2)}, u32[]{:S(2)}) collective-permute-start(bf16[272,512]{1,0:T(8,128)(2,1)S(1)} %pack.1), channel_id=1, source_target_pairs={{0,1},{1,0},{2,3},{3,2},{4,5},{5,4},{6,7},{7,6},{8,9},{9,8},{10,11... | collective-permute-start | bytes 835592 | tf_op jit(solution)/shard_map/ppermute | solution.py:358
  21.0 8.7 %collective-permute-start.5 = (bf16[272,512]{1,0:T(8,128)(2,1)S(1)}, bf16[272,512]{1,0:T(8,128)(2,1)S(1)}, u32[]{:S(2)}, u32[]{:S(2)}) collective-permute-start(bf16[272,512]{1,0:T(8,128)(2,1)S(1)} %collective-permute-done.1), channel_id=1, source_target_pairs={{0,2},{1,3},{2,0},{3,1},{4,6},{5,7},{6,4},{7,5},{8,10},{9,11},{10,... | collective-permute-start | bytes 835592 | tf_op jit(solution)/shard_map/ppermute | solution.py:358
  36.8 19.2 %collective-permute-start.8 = (bf16[384,512]{1,0:T(8,128)(2,1)S(1)}, bf16[384,512]{1,0:T(8,128)(2,1)S(1)}, u32[]{:S(2)}, u32[]{:S(2)}) collective-permute-start(bf16[384,512]{1,0:T(8,128)(2,1)S(1)} %get-tuple-element.210), channel_id=1, source_target_pairs={{0,16},{8,24},{16,0},{24,8},{1,17},{9,25},{17,1},{25,9},{2,18},{10... | collective-permute-start | bytes 1179656 | tf_op jit(solution)/shard_map/ppermute | solution.py:358
  38.4 17.6 %collective-permute-start.7 = (bf16[384,512]{1,0:T(8,128)(2,1)S(1)}, bf16[384,512]{1,0:T(8,128)(2,1)S(1)}, u32[]{:S(2)}, u32[]{:S(2)}) collective-permute-start(bf16[384,512]{1,0:T(8,128)(2,1)S(1)} %get-tuple-element.211), channel_id=1, source_target_pairs={{0,8},{8,0},{16,24},{24,16},{1,9},{9,1},{17,25},{25,17},{2,10},{10... | collective-permute-start | bytes 1179656 | tf_op jit(solution)/shard_map/ppermute | solution.py:358
  61.2 9.4 %collective-permute-start.14 = (bf16[384,512]{1,0:T(8,128)(2,1)S(1)}, bf16[384,512]{1,0:T(8,128)(2,1)S(1)}, u32[]{:S(2)}, u32[]{:S(2)}) collective-permute-start(bf16[384,512]{1,0:T(8,128)(2,1)S(1)} %pad_maximum_fusion.1), channel_id=1, source_target_pairs={{0,1},{1,0},{2,3},{3,2},{4,5},{5,4},{6,7},{7,6},{8,9},{9,8},{10,11... | collective-permute-start | bytes 1179656 | tf_op jit(solution)/shard_map/ppermute | solution.py:358
  61.4 8.8 %collective-permute-start.12 = (bf16[256,512]{1,0:T(8,128)(2,1)S(1)}, bf16[256,512]{1,0:T(8,128)(2,1)S(1)}, u32[]{:S(2)}, u32[]{:S(2)}) collective-permute-start(bf16[256,512]{1,0:T(8,128)(2,1)S(1)} %get-tuple-element.145), channel_id=1, source_target_pairs={{0,8},{8,0},{16,24},{24,16},{1,9},{9,1},{17,25},{25,17},{2,10},{10... | collective-permute-start | bytes 786440 | tf_op jit(solution)/shard_map/ppermute | solution.py:358
  61.9 8.3 %collective-permute-start.13 = (bf16[256,512]{1,0:T(8,128)(2,1)S(1)}, bf16[256,512]{1,0:T(8,128)(2,1)S(1)}, u32[]{:S(2)}, u32[]{:S(2)}) collective-permute-start(bf16[256,512]{1,0:T(8,128)(2,1)S(1)} %get-tuple-element.146), channel_id=1, source_target_pairs={{0,16},{8,24},{16,0},{24,8},{1,17},{9,25},{17,1},{25,9},{2,18},{10... | collective-permute-start | bytes 786440 | tf_op jit(solution)/shard_map/ppermute | solution.py:358
  62.4 8.2 %collective-permute-start.16 = (bf16[2,128,512]{2,1,0:T(8,128)(2,1)S(1)}, bf16[2,128,512]{2,1,0:T(8,128)(2,1)S(1)}, u32[]{:S(2)}, u32[]{:S(2)}) collective-permute-start(bf16[2,128,512]{2,1,0:T(8,128)(2,1)S(1)} %slice.197), channel_id=1, source_target_pairs={{0,2},{1,3},{2,0},{3,1},{4,6},{5,7},{6,4},{7,5},{8,10},{9,11},{10,... | collective-permute-start | bytes 786440 | tf_op jit(solution)/shard_map/ppermute | solution.py:358
  71.1 13.0 %collective-permute-start.20 = (bf16[2,128,512]{2,1,0:T(8,128)(2,1)S(1)}, bf16[2,128,512]{2,1,0:T(8,128)(2,1)S(1)}, u32[]{:S(2)}, u32[]{:S(2)}) collective-permute-start(bf16[2,128,512]{2,1,0:T(8,128)(2,1)S(1)} %slice.211), channel_id=1, source_target_pairs={{0,2},{1,3},{2,0},{3,1},{4,6},{5,7},{6,4},{7,5},{8,10},{9,11},{10,... | collective-permute-start | bytes 786440 | tf_op jit(solution)/shard_map/ppermute | solution.py:358
  72.9 11.2 %collective-permute-start.17 = (bf16[224,512]{1,0:T(8,128)(2,1)S(1)}, bf16[224,512]{1,0:T(8,128)(2,1)S(1)}, u32[]{:S(2)}, u32[]{:S(2)}) collective-permute-start(bf16[224,512]{1,0:T(8,128)(2,1)S(1)} %pad_maximum_fusion.2), channel_id=1, source_target_pairs={{0,16},{8,24},{16,0},{24,8},{1,17},{9,25},{17,1},{25,9},{2,18},{10... | collective-permute-start | bytes 688136 | tf_op jit(solution)/shard_map/ppermute | solution.py:358
  74.4 9.7 %collective-permute-start.18 = (bf16[224,512]{1,0:T(8,128)(2,1)S(1)}, bf16[224,512]{1,0:T(8,128)(2,1)S(1)}, u32[]{:S(2)}, u32[]{:S(2)}) collective-permute-start(bf16[224,512]{1,0:T(8,128)(2,1)S(1)} %pad_maximum_fusion.3), channel_id=1, source_target_pairs={{0,8},{8,0},{16,24},{24,16},{1,9},{9,1},{17,25},{25,17},{2,10},{10... | collective-permute-start | bytes 688136 | tf_op jit(solution)/shard_map/ppermute | solution.py:358
  75.9 8.1 %collective-permute-start.21 = (bf16[128,512]{1,0:T(8,128)(2,1)S(1)}, bf16[128,512]{1,0:T(8,128)(2,1)S(1)}, u32[]{:S(2)}, u32[]{:S(2)}) collective-permute-start(bf16[128,512]{1,0:T(8,128)(2,1)S(1)} %get-tuple-element.159), channel_id=1, source_target_pairs={{0,4},{1,5},{2,6},{3,7},{4,0},{5,1},{6,2},{7,3},{8,12},{9,13},{10,... | collective-permute-start | bytes 393224 | tf_op jit(solution)/shard_map/ppermute | solution.py:358
  84.9 6.1 %collective-permute-start.22 = (bf16[112,512]{1,0:T(8,128)(2,1)S(1)}, bf16[112,512]{1,0:T(8,128)(2,1)S(1)}, u32[]{:S(2)}, u32[]{:S(2)}) collective-permute-start(bf16[112,512]{1,0:T(8,128)(2,1)S(1)} %pad_maximum_fusion.6), channel_id=1, source_target_pairs={{0,2},{1,3},{2,0},{3,1},{4,6},{5,7},{6,4},{7,5},{8,10},{9,11},{10,... | collective-permute-start | bytes 344072 | tf_op jit(solution)/shard_map/ppermute | solution.py:358
  86.4 8.5 %collective-permute-start.23 = (bf16[112,512]{1,0:T(8,128)(2,1)S(1)}, bf16[112,512]{1,0:T(8,128)(2,1)S(1)}, u32[]{:S(2)}, u32[]{:S(2)}) collective-permute-start(bf16[112,512]{1,0:T(8,128)(2,1)S(1)} %pad_maximum_fusion.7), channel_id=1, source_target_pairs={{0,4},{1,5},{2,6},{3,7},{4,0},{5,1},{6,2},{7,3},{8,12},{9,13},{10,... | collective-permute-start | bytes 344072 | tf_op jit(solution)/shard_map/ppermute | solution.py:358
  87.0 7.9 %collective-permute-start.24 = (bf16[112,512]{1,0:T(8,128)(2,1)S(1)}, bf16[112,512]{1,0:T(8,128)(2,1)S(1)}, u32[]{:S(2)}, u32[]{:S(2)}) collective-permute-start(bf16[112,512]{1,0:T(8,128)(2,1)S(1)} %pad_maximum_fusion.8), channel_id=1, source_target_pairs={{0,6},{1,7},{2,4},{3,5},{4,2},{5,3},{6,0},{7,1},{8,14},{9,15},{10,... | collective-permute-start | bytes 344072 | tf_op jit(solution)/shard_map/ppermute | solution.py:358
  103.2 8.0 %collective-permute-start.30 = (bf16[128,512]{1,0:T(8,128)(2,1)S(1)}, bf16[128,512]{1,0:T(8,128)(2,1)S(1)}, u32[]{:S(2)}, u32[]{:S(2)}) collective-permute-start(bf16[128,512]{1,0:T(8,128)(2,1)S(1)} %get-tuple-element.178), channel_id=1, source_target_pairs={{0,4},{1,5},{2,6},{3,7},{4,0},{5,1},{6,2},{7,3},{8,12},{9,13},{10,... | collective-permute-start | bytes 393224 | tf_op jit(solution)/shard_map/ppermute | solution.py:358
  111.3 6.1 %collective-permute-start.31 = (bf16[224,512]{1,0:T(8,128)(2,1)S(1)}, bf16[224,512]{1,0:T(8,128)(2,1)S(1)}, u32[]{:S(2)}, u32[]{:S(2)}) collective-permute-start(bf16[224,512]{1,0:T(8,128)(2,1)S(1)} %pad_maximum_fusion.4), channel_id=1, source_target_pairs={{0,16},{8,24},{16,0},{24,8},{1,17},{9,25},{17,1},{25,9},{2,18},{10... | collective-permute-start | bytes 688136 | tf_op jit(solution)/shard_map/ppermute | solution.py:358
  112.0 6.8 %collective-permute-start.32 = (bf16[224,512]{1,0:T(8,128)(2,1)S(1)}, bf16[224,512]{1,0:T(8,128)(2,1)S(1)}, u32[]{:S(2)}, u32[]{:S(2)}) collective-permute-start(bf16[224,512]{1,0:T(8,128)(2,1)S(1)} %pad_maximum_fusion.5), channel_id=1, source_target_pairs={{0,8},{8,0},{16,24},{24,16},{1,9},{9,1},{17,25},{25,17},{2,10},{10... | collective-permute-start | bytes 688136 | tf_op jit(solution)/shard_map/ppermute | solution.py:358
  118.9 9.3 %collective-permute-start.33 = (bf16[448,512]{1,0:T(8,128)(2,1)S(1)}, bf16[448,512]{1,0:T(8,128)(2,1)S(1)}, u32[]{:S(2)}, u32[]{:S(2)}) collective-permute-start(bf16[448,512]{1,0:T(8,128)(2,1)S(1)} %pad_maximum_fusion.refs_1_), channel_id=1, source_target_pairs={{0,8},{8,0},{16,24},{24,16},{1,9},{9,1},{17,25},{25,17},{2,10},{10... | collective-permute-start | bytes 1376264 | tf_op jit(solution)/shard_map/ppermute | solution.py:358
  121.4 8.5 %collective-permute-start.34 = (bf16[448,512]{1,0:T(8,128)(2,1)S(1)}, bf16[448,512]{1,0:T(8,128)(2,1)S(1)}, u32[]{:S(2)}, u32[]{:S(2)}) collective-permute-start(bf16[448,512]{1,0:T(8,128)(2,1)S(1)} %constant_dynamic-update-slice_fusion.refs_2_), channel_id=1, source_target_pairs={{0,16},{8,24},{16,0},{24,8},{1,17},{9,25},{17,1},{25,9},{2,18},{10... | collective-permute-start | bytes 1376264 | tf_op jit(solution)/shard_map/ppermute | solution.py:358
  121.4 8.5 %collective-permute-start.35 = (bf16[448,512]{1,0:T(8,128)(2,1)S(1)}, bf16[448,512]{1,0:T(8,128)(2,1)S(1)}, u32[]{:S(2)}, u32[]{:S(2)}) collective-permute-start(bf16[448,512]{1,0:T(8,128)(2,1)S(1)} %pad_maximum_fusion.refs_1_), channel_id=1, source_target_pairs={{0,1},{1,0},{2,3},{3,2},{4,5},{5,4},{6,7},{7,6},{8,9},{9,8},{10,11... | collective-permute-start | bytes 1376264 | tf_op jit(solution)/shard_map/ppermute | solution.py:358
  121.4 8.5 %collective-permute-start.36 = (bf16[448,512]{1,0:T(8,128)(2,1)S(1)}, bf16[448,512]{1,0:T(8,128)(2,1)S(1)}, u32[]{:S(2)}, u32[]{:S(2)}) collective-permute-start(bf16[448,512]{1,0:T(8,128)(2,1)S(1)} %constant_dynamic-update-slice_fusion.refs_2_), channel_id=1, source_target_pairs={{0,1},{1,0},{2,3},{3,2},{4,5},{5,4},{6,7},{7,6},{8,9},{9,8},{10,11... | collective-permute-start | bytes 1376264 | tf_op jit(solution)/shard_map/ppermute | solution.py:358
  (35 other events, 171.4 us)
